TPU v7x, 128 devices: a whole 4x4x4 slice. The times are simulated.
128 devices in a mesh: expert: 16 (over x, z), context: 4 (over y), dp: 2 (over core).
Axes of the slice: x: 4, y: 4, z: 4, core: 2. Of those that a mesh axis runs over, the one named last changes fastest.
Arguments:
- layer_input: bfloat16 [2, 4, 2048, 1024], P('dp', 'context', 'expert'), may hold values from -6 to 6
- grad_output: bfloat16 [2, 4, 2048, 1024], P('dp', 'context', 'expert'), may hold values from -6 to 6
- norm1_gain: float32 [1024], replicated, may hold values from 0.5 to 1.5
- norm2_gain: float32 [1024], replicated, may hold values from 0.5 to 1.5
- w_query: bfloat16 [1024, 1024], replicated, may hold values from -0.75 to 0.75
- w_key: bfloat16 [1024, 512], replicated, may hold values from -0.75 to 0.75
- w_value: bfloat16 [1024, 512], replicated, may hold values from -0.75 to 0.75
- w_out: bfloat16 [1024, 1024], replicated, may hold values from -1.5 to 1.5
- w_router: bfloat16 [1024, 32], replicated, may hold values from -0.09375 to 0.09375
- w_gate_up: bfloat16 [32, 1024, 1024], P('expert', ('context', 'dp')), may hold values from -0.375 to 0.375
- w_down: bfloat16 [32, 512, 1024], P('expert', ('context', 'dp')), may hold values from -4 to 4
- routes: int32 [2, 4, 2048, 8], P('dp', 'context', 'expert'), may hold values from 0 to 31, all different within a row; in each aligned block of 128 rows (0 to 127, 128 to 255, ..., all dimensions but the last counted through in order) at most 48 rows name the same one
Outputs:
- block_out: float32 [2, 4, 2048, 1024], P('dp', 'context', 'expert')
- grad_input: float32 [2, 4, 2048, 1024], P('dp', 'context', 'expert')
- grad_norm1: float32 [1024], replicated
- grad_norm2: float32 [1024], replicated
- grad_w_query: float32 [1024, 1024], replicated
- grad_w_key: float32 [1024, 512], replicated
- grad_w_value: float32 [1024, 512], replicated
- grad_w_out: float32 [1024, 1024], replicated
- grad_w_router: float32 [1024, 32], replicated
- grad_w_gate_up: float32 [32, 1024, 1024], P('expert', ('context', 'dp'))
- grad_w_down: float32 [32, 512, 1024], P('expert', ('context', 'dp'))
Inputs may be any that keep to these rules, and one draw needn't show every extreme that they name: `routes`: each row names 8 different experts. Taken in the order (sequence, block, position), in each aligned block of 128 rows (the tokens of one device) no expert is named by more than 48 rows, a bound that some block reaches.
All inputs are finite; a program needn't handle non-finite values.
Results may differ from a plain program's by a relative error of at most 0.024.
Values may be sent and summed in bfloat16 or wider, within the bound.
No kernel may reach another device: no remote copies, remote signals or barrier semaphores. Data moves between devices by JAX's collectives and lax.ppermute only.
A program may use at most 192 MiB of HBM per device.

v0:
```python
import jax
import jax.numpy as jnp
import numpy as np
from jax import lax
from jax.sharding import PartitionSpec as P

D = 1024
HEAD_DIM = 64
F = 512
EXPERTS = 32
TOPK = 8
CAP = 48


norm_eps = 1e-06
score_scale = 0.015625
branch_scale = 0.22
rope_base = 10000.0
huge_negative = -1e30
highest_precision = lax.Precision.HIGHEST


def rope_tables(positions, head_size):
    frequency = rope_base ** (-jnp.arange(0, head_size, 2, dtype=jnp.float32) / head_size)
    angles = positions.astype(jnp.float32)[:, None] * frequency[None, :]
    angles = jnp.concatenate([angles, angles], -1)
    return (jnp.cos(angles), jnp.sin(angles))


def rope_turn(values, cosine_table, sine_table):
    half_size = values.shape[-1] // 2
    turned = jnp.concatenate([-values[..., half_size:], values[..., :half_size]], -1)
    return values * cosine_table[:, None, :] + turned * sine_table[:, None, :]


def rope_back(gradients, cosine_table, sine_table):
    half_size = gradients.shape[-1] // 2
    scaled = gradients * sine_table[:, None, :]
    return gradients * cosine_table[:, None, :] + jnp.concatenate(
        [scaled[..., half_size:], -scaled[..., :half_size]], -1
    )


def norm_back(grad_act, normed, inverse, gain_values):
    gain_grad = jnp.sum(grad_act * normed, 0)
    scaled = grad_act * gain_values
    return (
        gain_grad,
        inverse * (scaled - normed * jnp.mean(scaled * normed, axis=-1, keepdims=True)),
    )


def key_piece(pairs, block_index, block_rows, pair_width):
    block_slice = pairs[block_index * block_rows : (block_index + 1) * block_rows]
    key_rows = block_slice[:, :pair_width].reshape(block_rows, -1, HEAD_DIM)
    value_rows = block_slice[:, pair_width:].reshape(block_rows, -1, HEAD_DIM)
    return (key_rows, value_rows)


def block_scores(queries, key_rows, block_index, block_rows, query_pos):
    scores = (
        jnp.einsum("qhgd,khd->hgqk", queries, key_rows, preferred_element_type=jnp.float32)
        * score_scale
    )
    key_pos = block_index * block_rows + jnp.arange(block_rows, dtype=jnp.int32)
    visible = key_pos[None, :] <= query_pos[:, None]
    return jnp.where(visible, scores, huge_negative)


def attend_forward(queries, pairs, query_pos, block_rows, pair_width, context_size, context_index):
    query_rows, kv_count, group_count, head_size = queries.shape

    def keep_state(state_tuple):
        return state_tuple

    running_max = jnp.full((kv_count, group_count, query_rows), huge_negative, jnp.float32)
    running_sum = jnp.zeros((kv_count, group_count, query_rows), jnp.float32)
    running_out = jnp.zeros(queries.shape, jnp.float32)
    for block_index in range(context_size):
        key_rows, value_rows = key_piece(pairs, block_index, block_rows, pair_width)

        def visit_block(
            state_tuple, key_rows=key_rows, value_rows=value_rows, block_index=block_index
        ):
            old_max, old_sum, old_out = state_tuple
            scores = block_scores(queries, key_rows, block_index, block_rows, query_pos)
            new_max = jnp.maximum(old_max, jnp.max(scores, -1))
            weights = jnp.exp(scores - new_max[..., None])
            shrink = jnp.exp(old_max - new_max)
            new_sum = old_sum * shrink + jnp.sum(weights, -1)
            added = jnp.einsum(
                "hgqk,khd->qhgd",
                weights.astype(jnp.bfloat16),
                value_rows,
                preferred_element_type=jnp.float32,
            )
            new_out = old_out * jnp.transpose(shrink, (2, 0, 1))[..., None] + added
            return (new_max, new_sum, new_out)

        running_max, running_sum, running_out = lax.cond(
            block_index <= context_index,
            visit_block,
            keep_state,
            (running_max, running_sum, running_out),
        )
    attended_full = running_out / jnp.transpose(running_sum, (2, 0, 1))[..., None]
    log_total = running_max + jnp.log(running_sum)
    return (attended_full, log_total)


def attend_backward(
    queries,
    grad_attended,
    attended_full,
    log_total,
    pairs,
    query_pos,
    block_rows,
    pair_width,
    context_size,
    context_index,
):
    row_dot = jnp.transpose(
        jnp.sum(grad_attended.astype(jnp.float32) * attended_full, -1), (1, 2, 0)
    )
    grad_query_rot = jnp.zeros(queries.shape, jnp.float32)
    pieces = []
    for block_index in range(context_size):
        key_rows, value_rows = key_piece(pairs, block_index, block_rows, pair_width)

        def revisit(
            grad_query_now, key_rows=key_rows, value_rows=value_rows, block_index=block_index
        ):
            scores = block_scores(queries, key_rows, block_index, block_rows, query_pos)
            weights = jnp.exp(scores - log_total[..., None])
            grad_weights = jnp.einsum(
                "qhgd,khd->hgqk", grad_attended, value_rows, preferred_element_type=jnp.float32
            )
            grad_scores = (weights * (grad_weights - row_dot[..., None])).astype(jnp.bfloat16)
            grad_query_now = grad_query_now + score_scale * jnp.einsum(
                "hgqk,khd->qhgd", grad_scores, key_rows, preferred_element_type=jnp.float32
            )
            grad_key_rows = score_scale * jnp.einsum(
                "hgqk,qhgd->khd", grad_scores, queries, preferred_element_type=jnp.float32
            )
            grad_value_rows = jnp.einsum(
                "hgqk,qhgd->khd",
                weights.astype(jnp.bfloat16),
                grad_attended,
                preferred_element_type=jnp.float32,
            )
            joined = jnp.concatenate(
                [
                    grad_key_rows.reshape(block_rows, pair_width),
                    grad_value_rows.reshape(block_rows, pair_width),
                ],
                -1,
            )
            return (grad_query_now, joined)

        def skip_block(grad_query_now):
            return (grad_query_now, jnp.zeros((block_rows, 2 * pair_width), jnp.float32))

        grad_query_rot, block_terms = lax.cond(
            block_index <= context_index, revisit, skip_block, grad_query_rot
        )
        pieces.append(block_terms)
    return (grad_query_rot, jnp.concatenate(pieces, 0))


def local(
    layer_input,
    grad_output,
    norm1_gain,
    norm2_gain,
    w_query,
    w_key,
    w_value,
    w_out,
    w_router,
    w_gate_up,
    w_down,
    routes,
):
    local_rows = layer_input.shape[2]
    expert_size = lax.axis_size("expert")
    context_size = lax.axis_size("context")
    block_rows = local_rows * expert_size
    context_index = lax.axis_index("context")
    expert_index = lax.axis_index("expert")
    head_count = w_query.shape[1] // HEAD_DIM
    key_heads = w_key.shape[1] // HEAD_DIM
    group_size = head_count // key_heads
    key_width = w_key.shape[1]
    local_experts = w_gate_up.shape[0]
    heads_each = head_count // expert_size
    pairs_each = max(1, heads_each // group_size)
    head_table = np.array(
        [[owner * heads_each // group_size] for owner in range(expert_size)], np.int32
    )
    head_onehot = np.zeros((expert_size, pairs_each, key_heads), np.float32)
    for owner in range(expert_size):
        head_onehot[owner, 0, head_table[owner, 0]] = 1.0
    inputs = layer_input[0, 0].astype(jnp.float32)
    inverse1 = lax.rsqrt(jnp.mean(inputs * inputs, axis=-1, keepdims=True) + norm_eps)
    normed1 = inputs * inverse1
    act1 = (normed1 * norm1_gain).astype(jnp.bfloat16)
    query_raw = jnp.dot(act1, w_query, preferred_element_type=jnp.float32).reshape(
        local_rows, head_count, HEAD_DIM
    )
    key_raw = jnp.dot(act1, w_key, preferred_element_type=jnp.float32).reshape(
        local_rows, key_heads, HEAD_DIM
    )
    value_raw = jnp.dot(act1, w_value, preferred_element_type=jnp.float32)
    positions = (
        context_index * block_rows
        + expert_index * local_rows
        + jnp.arange(local_rows, dtype=jnp.int32)
    )
    cosine_table, sine_table = rope_tables(positions, HEAD_DIM)
    query_flat = (
        rope_turn(query_raw, cosine_table, sine_table)
        .astype(jnp.bfloat16)
        .reshape(local_rows, head_count * HEAD_DIM)
    )
    key_rot = rope_turn(key_raw, cosine_table, sine_table).astype(jnp.bfloat16)
    value_low = value_raw.astype(jnp.bfloat16)
    key_value_rows = jnp.concatenate([key_rot.reshape(local_rows, key_width), value_low], -1)
    block_pairs = lax.all_gather(key_value_rows, "expert", axis=0, tiled=True)
    whole_pairs = lax.all_gather(block_pairs, "context", axis=0, tiled=True)
    query_rot = query_flat.reshape(local_rows, key_heads, group_size, HEAD_DIM)
    attended_full, log_total = attend_forward(
        query_rot, whole_pairs, positions, block_rows, key_width, context_size, context_index
    )
    attended = attended_full.reshape(local_rows, head_count * HEAD_DIM).astype(jnp.bfloat16)
    hidden_state = inputs + branch_scale * jnp.dot(
        attended, w_out, preferred_element_type=jnp.float32
    )
    inverse2 = lax.rsqrt(jnp.mean(hidden_state * hidden_state, axis=-1, keepdims=True) + norm_eps)
    normed2 = hidden_state * inverse2
    act2 = (normed2 * norm2_gain).astype(jnp.bfloat16)
    router_probs = jax.nn.softmax(
        jnp.dot(act2, w_router, preferred_element_type=jnp.float32), axis=-1
    )
    token_routes = routes[0, 0]
    choose = token_routes[:, :, None] == jnp.arange(EXPERTS, dtype=jnp.int32)
    choose_float = choose.astype(jnp.float32)
    gate_values = jnp.sum(choose_float * router_probs[:, None, :], -1)
    expert_hits = jnp.sum(choose.astype(jnp.int32), 1)
    slot_rows = jnp.cumsum(expert_hits, 0) - expert_hits
    slot_of = jnp.take_along_axis(slot_rows, token_routes, 1)
    slot_index = (token_routes * CAP + slot_of).reshape(-1)
    spread_rows = jnp.broadcast_to(act2[:, None, :], (local_rows, TOPK, D)).reshape(-1, D)
    send_rows = jnp.zeros((EXPERTS * CAP, D), jnp.bfloat16).at[slot_index].set(spread_rows)
    send_rows = send_rows.reshape(expert_size, local_experts, CAP, D)
    gate_up_all, down_all = (
        lax.all_gather(w_gate_up, ("context", "dp"), axis=1, tiled=True),
        lax.all_gather(w_down, ("context", "dp"), axis=1, tiled=True),
    )
    received = lax.all_to_all(send_rows, "expert", split_axis=0, concat_axis=0, tiled=True)
    gate_up_pre = jnp.einsum(
        "necd,edf->necf", received, gate_up_all, preferred_element_type=jnp.float32
    )
    hidden = (jax.nn.silu(gate_up_pre[..., :F]) * gate_up_pre[..., F:]).astype(jnp.bfloat16)
    result = jnp.einsum(
        "necf,efd->necd", hidden, down_all, preferred_element_type=jnp.float32
    ).astype(jnp.bfloat16)
    returned = lax.all_to_all(result, "expert", split_axis=0, concat_axis=0, tiled=True)
    returned, received, gate_up_pre, hidden = (returned, received, gate_up_pre, hidden)
    picked = (
        returned.reshape(EXPERTS * CAP, D)[slot_index]
        .reshape(local_rows, TOPK, D)
        .astype(jnp.float32)
    )
    mixture_sum = jnp.sum(gate_values[..., None] * picked, 1)
    block_out = hidden_state + branch_scale * mixture_sum
    grad_top = grad_output[0, 0].astype(jnp.float32)
    grad_moe = branch_scale * grad_top
    grad_gates = jnp.sum(picked * grad_moe[:, None, :], -1)
    grad_rows = (gate_values[..., None] * grad_moe[:, None, :]).astype(jnp.bfloat16).reshape(-1, D)
    grad_send = jnp.zeros((EXPERTS * CAP, D), jnp.bfloat16).at[slot_index].set(grad_rows)
    grad_recv = lax.all_to_all(
        grad_send.reshape(expert_size, local_experts, CAP, D),
        "expert",
        split_axis=0,
        concat_axis=0,
        tiled=True,
    )
    gate_part = gate_up_pre[..., :F]
    up_part = gate_up_pre[..., F:]
    grad_hidden = jnp.einsum(
        "necd,efd->necf", grad_recv, down_all, preferred_element_type=jnp.float32
    )
    sigmoid_gate = jax.nn.sigmoid(gate_part)
    grad_gate_part = grad_hidden * up_part * sigmoid_gate * (1.0 + gate_part * (1.0 - sigmoid_gate))
    grad_up_part = grad_hidden * gate_part * sigmoid_gate
    grad_mixed = jnp.concatenate([grad_gate_part, grad_up_part], -1).astype(jnp.bfloat16)
    down_grad = jnp.einsum("necf,necd->efd", hidden, grad_recv, preferred_element_type=jnp.float32)
    gate_up_grad = jnp.einsum(
        "necd,necf->edf", received, grad_mixed, preferred_element_type=jnp.float32
    )
    grad_in_rows = jnp.einsum(
        "necf,edf->necd", grad_mixed, gate_up_all, preferred_element_type=jnp.float32
    ).astype(jnp.bfloat16)
    grad_back = lax.all_to_all(
        grad_in_rows, "expert", split_axis=0, concat_axis=0, tiled=True
    ).reshape(EXPERTS * CAP, D)
    grad_act2 = jnp.sum(grad_back[slot_index].reshape(local_rows, TOPK, D).astype(jnp.float32), 1)
    grad_probs = jnp.sum(choose_float * grad_gates[:, :, None], 1)
    grad_logits = router_probs * (
        grad_probs - jnp.sum(router_probs * grad_probs, -1, keepdims=True)
    )
    grad_act2 = grad_act2 + jnp.dot(
        grad_logits, w_router.astype(jnp.float32).T, precision=highest_precision
    )
    router_grad = jnp.dot(act2.astype(jnp.float32).T, grad_logits, precision=highest_precision)
    norm2_grad, norm2_term = norm_back(grad_act2, normed2, inverse2, norm2_gain)
    grad_state = grad_top + norm2_term
    grad_attn = (branch_scale * grad_state).astype(jnp.bfloat16)
    out_grad = jnp.einsum("td,te->de", attended, grad_attn, preferred_element_type=jnp.float32)
    grad_attended = jnp.dot(grad_attn, w_out.T, preferred_element_type=jnp.float32).astype(
        jnp.bfloat16
    )
    grad_attended_heads = grad_attended.reshape(local_rows, key_heads, group_size, HEAD_DIM)
    grad_query_rot, key_terms = attend_backward(
        query_rot,
        grad_attended_heads,
        attended_full,
        log_total,
        whole_pairs,
        positions,
        block_rows,
        key_width,
        context_size,
        context_index,
    )
    grad_query_rot = grad_query_rot.reshape(local_rows, head_count * HEAD_DIM)
    own_terms = lax.psum_scatter(
        key_terms.astype(jnp.bfloat16), "context", scatter_dimension=0, tiled=True
    ).astype(jnp.float32)
    own_terms = lax.psum_scatter(
        own_terms.astype(jnp.bfloat16), "expert", scatter_dimension=0, tiled=True
    ).astype(jnp.float32)
    grad_key = rope_back(
        own_terms[:, :key_width].reshape(local_rows, key_heads, HEAD_DIM), cosine_table, sine_table
    )
    grad_key = grad_key.reshape(local_rows, key_width).astype(jnp.bfloat16)
    grad_value = own_terms[:, key_width:].astype(jnp.bfloat16)
    grad_query = rope_back(
        grad_query_rot.reshape(local_rows, head_count, HEAD_DIM), cosine_table, sine_table
    )
    grad_query = grad_query.reshape(local_rows, head_count * HEAD_DIM).astype(jnp.bfloat16)
    query_grad = jnp.einsum("td,te->de", act1, grad_query, preferred_element_type=jnp.float32)
    key_grad = jnp.einsum("td,te->de", act1, grad_key, preferred_element_type=jnp.float32)
    value_grad = jnp.einsum("td,te->de", act1, grad_value, preferred_element_type=jnp.float32)
    grad_act1 = jnp.dot(grad_query, w_query.T, preferred_element_type=jnp.float32)
    grad_act1 = grad_act1 + jnp.dot(grad_key, w_key.T, preferred_element_type=jnp.float32)
    grad_act1 = grad_act1 + jnp.dot(grad_value, w_value.T, preferred_element_type=jnp.float32)
    norm1_grad, norm1_term = norm_back(grad_act1, normed1, inverse1, norm1_gain)
    grad_input = grad_state + norm1_term
    gate_up_grad, down_grad = (
        lax.psum_scatter(
            gate_up_grad.astype(jnp.bfloat16), ("context", "dp"), scatter_dimension=1, tiled=True
        ).astype(jnp.float32),
        lax.psum_scatter(
            down_grad.astype(jnp.bfloat16), ("context", "dp"), scatter_dimension=1, tiled=True
        ).astype(jnp.float32),
    )
    dense_sums = lax.psum(
        (query_grad, key_grad, value_grad, out_grad, router_grad, norm1_grad, norm2_grad),
        ("expert", "context", "dp"),
    )
    return (
        block_out.reshape(1, 1, local_rows, D),
        grad_input.reshape(1, 1, local_rows, D),
        dense_sums[5],
        dense_sums[6],
        dense_sums[0],
        dense_sums[1],
        dense_sums[2],
        dense_sums[3],
        dense_sums[4],
        gate_up_grad,
        down_grad,
    )


def solution(mesh):
    placed = (
        P("dp", "context", "expert", None),
        P("dp", "context", "expert", None),
        P(),
        P(),
        P(),
        P(),
        P(),
        P(),
        P(),
        P("expert", ("context", "dp"), None),
        P("expert", ("context", "dp"), None),
        P("dp", "context", "expert", None),
    )
    return jax.shard_map(
        local,
        mesh=mesh,
        in_specs=placed,
        out_specs=(
            P("dp", "context", "expert", None),
            P("dp", "context", "expert", None),
            P(),
            P(),
            P(),
            P(),
            P(),
            P(),
            P(),
            P("expert", ("context", "dp"), None),
            P("expert", ("context", "dp"), None),
        ),
        check_vma=False,
    )
```

profile of v0, /device:TPU:1, one launch (start us, length us, event | category | flops | bytes accessed | tf_op | source)
XLA Modules:
  0.0 1268.7 jit_solution(12966889706246019045)
XLA Ops:
  14.4 55.0 %all-gather.5.cloned.1.call-done = bf16[2048,1024]{1,0:T(8,128)(2,1)} async-done(((bf16[128,1024]{1,0:T(8,128)(2,1)}), bf16[2048,1024]{1,0:T(8,128)(2,1)}) %all-gather.5.cloned.1.call-update) | async-done | bytes 4194320 | tf_op jit(solution)/shard_map/all_gather | solution.py:229
  84.9 139.9 %all-gather.7.cloned.1.call-done = bf16[8192,1024]{1,0:T(8,128)(2,1)} async-done(((bf16[2048,1024]{1,0:T(8,128)(2,1)}), bf16[8192,1024]{1,0:T(8,128)(2,1)}) %all-gather.7.cloned.1.call-update) | async-done | bytes 16777232 | tf_op jit(solution)/shard_map/all_gather | solution.py:230
  224.8 12.1 fusion.275
  268.6 24.6 %conditional.8 = (f32[8,2,128]{2,1,0:T(2,128)}, f32[8,2,128]{2,1,0:T(2,128)S(1)}, f32[128,8,2,64]{0,3,2,1:T(8,128)S(1)}) conditional(s32[]{:T(128)} %convert_element_type.198, () %tuple.76, (s32[128]{0:T(128)S(1)}, bf16[2048,8,64]{0,2,1:T(8,128)(2,1)}, bf16[128,8,2,64]{0,3,2,1:T(8,128)(2,1)S(1)}, bf16[2048,8,64]{0,2,1:T(8,128)(2,1)}) %tuple.208), branch_computations={%region_1.0_spmd, %region_2.5_spmd} | conditional | flops 1120280576 | bytes 131949136 | solution.py:100
  283.4 9.1 fusion.1
  293.5 13.7 %conditional.11 = (f32[8,2,128]{2,1,0:T(2,128)S(1)}, f32[128,8,2,64]{0,3,2,1:T(8,128)S(1)}, f32[8,2,128]{2,1,0:T(2,128)}) conditional(s32[]{:T(128)} %convert_element_type.195, (f32[8,2,128]{2,1,0:T(2,128)}, f32[8,2,128]{2,1,0:T(2,128)S(1)}, f32[128,8,2,64]{0,3,2,1:T(8,128)S(1)}) %get-tuple-element.457, (s32[128]{0:T(128)S(1)}, ...), branch_computations={%region_13.14_spmd.clone, %region_14.17_spmd.clone} | conditional | flops 1120411648 | bytes 132530768 | solution.py:100
  333.1 30.3 %all-to-all-done = bf16[16,2,48,1024]{3,2,1,0:T(8,128)(2,1)} async-done(((bf16[16,2,48,1024]{3,2,1,0:T(8,128)(2,1)}), bf16[16,2,48,1024]{3,2,1,0:T(8,128)(2,1)}, u32[]{:S(2)}, u32[]{:S(2)}) %all-to-all-start) | async-done | bytes 3145760 | tf_op jit(solution)/shard_map/all_to_all | solution.py:260
  372.5 9.2 fusion.200
  381.8 29.9 %all-gather.11.cloned.1.call-done = bf16[2,512,1024]{2,1,0:T(8,128)(2,1)} async-done(((bf16[2,64,1024]{2,1,0:T(8,128)(2,1)}), bf16[2,512,1024]{2,1,0:T(8,128)(2,1)}) %all-gather.11.cloned.1.call-update) | async-done | bytes 2097168 | tf_op jit(solution)/shard_map/all_gather | solution.py:258
  438.9 30.7 %all-to-all-done.3 = bf16[16,2,48,1024]{3,2,1,0:T(8,128)(2,1)} async-done(((bf16[16,2,48,1024]{3,2,1,0:T(8,128)(2,1)}), bf16[16,2,48,1024]{3,2,1,0:T(8,128)(2,1)}, u32[]{:S(2)}, u32[]{:S(2)}) %all-to-all-start.3) | async-done | bytes 3145760 | tf_op jit(solution)/shard_map/all_to_all | solution.py:305
  489.0 23.5 %all-to-all-done.1 = bf16[16,2,48,1024]{3,2,1,0:T(8,128)(2,1)} async-done(((bf16[16,2,48,1024]{3,2,1,0:T(8,128)(2,1)}), bf16[16,2,48,1024]{3,2,1,0:T(8,128)(2,1)}, u32[]{:S(2)}, u32[]{:S(2)}) %all-to-all-start.1) | async-done | bytes 3145760 | tf_op jit(solution)/shard_map/all_to_all | solution.py:268
  532.8 38.6 %conditional.12 = (f32[128,8,2,64]{0,3,2,1:T(8,128)S(1)}, bf16[2048,1024]{0,1:T(8,128)(2,1)}) conditional(s32[]{:T(128)} %convert_element_type.198, () %tuple.81, (s32[128]{0:T(128)S(1)}, bf16[2048,8,64]{0,2,1:T(8,128)(2,1)}, bf16[128,8,2,64]{0,3,2,1:T(8,128)(2,1)S(1)}, f32[8,2,128]{2,1,0:T(2,128)S(1)}, bf16[2048,8,64]{0,2,1:T(8,128)(2,1)}, ...), branch_computations={%region_32.33_spmd, %region_33.34_spmd} | conditional | flops 2737176576 | bytes 113533512 | solution.py:164
  533.0 9.7 fusion.78
  542.7 11.0 fusion.72
  553.7 10.7 fusion.68
  579.1 10.1 conditional.14
  589.3 13.2 %conditional.15 = (f32[128,8,2,64]{0,3,2,1:T(8,128)S(1)}, bf16[2048,1024]{0,1:T(8,128)(2,1)}) conditional(s32[]{:T(128)} %convert_element_type.195, f32[128,8,2,64]{0,3,2,1:T(8,128)S(1)} %get-tuple-element.248, (s32[128]{0:T(128)S(1)}, bf16[2048,8,64]{0,2,1:T(8,128)(2,1)S(1)}, bf16[128,8,2,64]{0,3,2,1:T(8,128)(2,1)S(1)}, ...), branch_computations={%region_38.39_spmd, %region_39.40_spmd} | conditional | flops 2737309696 | bytes 105685544 | solution.py:164
  602.5 13.6 %pad_maximum_fusion = bf16[8192,1024]{0,1:T(8,128)(2,1)} fusion(bf16[2048,1024]{0,1:T(8,128)(2,1)} %get-tuple-element.262, bf16[2048,1024]{0,1:T(8,128)(2,1)} %get-tuple-element.261, bf16[2048,1024]{0,1:T(8,128)(2,1)} %get-tuple-element.260, bf16[2048,1024]{0,1:T(8,128)(2,1)} %get-tuple-element.259), kind=kLoop, calls=%fused_computation.171 | loop fusion | flops 67108864 | bytes 33554432 | tf_op jit(solution)/shard_map/concatenate | solution.py:168
  616.1 299.1 %reduce-scatter.7.cloned.1.call-done = bf16[2048,1024]{0,1:T(8,128)(2,1)} async-done(((bf16[8192,1024]{0,1:T(8,128)(2,1)}), bf16[2048,1024]{0,1:T(8,128)(2,1)}) %reduce-scatter.7.cloned.1.call-update) | async-done | bytes 4194320 | tf_op jit(solution)/shard_map/reduce_scatter | solution.py:338
  944.2 53.4 %reduce-scatter.13.cloned.1.call-done = bf16[128,1024]{1,0:T(8,128)(2,1)} async-done(((bf16[2048,1024]{1,0:T(8,128)(2,1)}), bf16[128,1024]{1,0:T(8,128)(2,1)}) %reduce-scatter.13.cloned.1.call-update) | async-done | bytes 262160
  1006.0 25.5 %reduce-scatter.11.cloned.1.call-done = bf16[2,64,1024]{2,1,0:T(8,128)(2,1)} async-done(((bf16[2,512,1024]{2,1,0:T(8,128)(2,1)}), bf16[2,64,1024]{2,1,0:T(8,128)(2,1)}) %reduce-scatter.11.cloned.1.call-update) | async-done | bytes 262160 | tf_op jit(solution)/shard_map/reduce_scatter | solution.py:365
  1033.4 37.3 %reduce-scatter.9.cloned.1.call-done = bf16[2,128,1024]{2,1,0:T(8,128)(2,1)} async-done(((bf16[2,1024,1024]{2,1,0:T(8,128)(2,1)}), bf16[2,128,1024]{2,1,0:T(8,128)(2,1)}) %reduce-scatter.9.cloned.1.call-update) | async-done | bytes 524304 | tf_op jit(solution)/shard_map/reduce_scatter | solution.py:362
  1074.9 68.8 %all-reduce = (f32[1024]{0:T(1024)}, f32[1024]{0:T(1024)}) all-reduce(f32[1024]{0:T(1024)S(1)} %get-tuple-element.342, f32[1024]{0:T(1024)S(1)} %copy-done.50), channel_id=1, replica_groups=mesh['expert'=16,'context'=4,'dp'=2] {'expert','context','dp'}, use_global_device_ids=true, to_apply=%region_44.45 | all-reduce | flops 2048 | bytes 16384 | tf_op jit(solution)/shard_map/psum | solution.py:369
  1144.8 105.8 %all-reduce.4.cloned.1.call-done = (f32[1024,1024]{1,0:T(8,128)}, f32[1024,512]{1,0:T(8,128)}, f32[1024,512]{1,0:T(8,128)}, f32[1024,1024]{1,0:T(8,128)}, f32[1024,32]{0,1:T(8,128)}) async-done(((f32[1024,1024]{1,0:T(8,128)}, f32[1024,512]{1,0:T(8,128)}, f32[1024,512]{1,0:T(8,128)}, f32[1024,1024]{1,0:T(8,128)}, f32[1024,32]{0,1:T(8,128)}), (f32[1024,1024]{1,0:T(8,128)}, f32[1024,512]{1,0:T(8,128)}, ...) | async-done | bytes 12714000 | tf_op jit(solution)/shard_map/psum | solution.py:369
  (232 shorter events, 249.4 us)
Async XLA Ops:
  7.2 300.8 %copy-start = (bf16[1024,1024]{1,0:T(8,128)(2,1)S(1)}, bf16[1024,1024]{1,0:T(8,128)(2,1)}, u32[]{:S(2)}) copy-start(bf16[1024,1024]{1,0:T(8,128)(2,1)} %param.35) | copy-start | bytes 6291460
  7.2 62.2 %all-gather.5.cloned.1.call-start = ((), (), s32[]{:S(2)}) async-start(), calls=%async_computation.8 | async-start | bytes 4456448 | tf_op jit(solution)/shard_map/all_gather | solution.py:229
  8.5 73.4 %copy-start.48 = (f32[128]{0:T(128)}, f32[128]{0:T(128)S(1)}, u32[]{:S(2)}) copy-start(f32[128]{0:T(128)S(1)} %add_rsqrt_fusion.1) | copy-start | bytes 1540
  8.7 76.1 %copy-start.31 = (f32[128,64]{0,1:T(8,128)}, f32[128,64]{0,1:T(8,128)S(1)}, u32[]{:S(2)}) copy-start(f32[128,64]{0,1:T(8,128)S(1)} %get-tuple-element.390) | copy-start | bytes 98308
  8.7 76.1 %copy-start.34 = (f32[128,64]{0,1:T(8,128)}, f32[128,64]{0,1:T(8,128)S(1)}, u32[]{:S(2)}) copy-start(f32[128,64]{0,1:T(8,128)S(1)} %get-tuple-element.391) | copy-start | bytes 98308
  11.9 58.3 %copy-start.46 = (s32[1,1,128,8]{2,3,1,0:T(8,128)S(1)}, s32[1,1,128,8]{2,3,1,0:T(8,128)}, u32[]{:S(2)}) copy-start(s32[1,1,128,8]{2,3,1,0:T(8,128)} %param.39) | copy-start | bytes 12292
  14.4 210.4 %all-gather.7.cloned.1.call-start = ((), (), s32[]{:S(2)}) async-start(), calls=%async_computation.9 | async-start | bytes 20971520 | tf_op jit(solution)/shard_map/all_gather | solution.py:230
  69.4 303.1 %all-gather.9.cloned.1.call-start = ((), (), s32[]{:S(2)}) async-start(), calls=%async_computation.10 | async-start | bytes 4718592 | tf_op jit(solution)/shard_map/all_gather | solution.py:257
  308.8 15.7 %copy-start.18 = (bf16[128,1024]{1,0:T(8,128)(2,1)}, bf16[128,1024]{1,0:T(8,128)(2,1)S(1)}, u32[]{:S(2)}) copy-start(bf16[128,1024]{1,0:T(8,128)(2,1)S(1)} %multiply_convert_fusion.2) | copy-start | bytes 786436
  316.2 47.2 %all-to-all-start = ((bf16[16,2,48,1024]{3,2,1,0:T(8,128)(2,1)}), bf16[16,2,48,1024]{3,2,1,0:T(8,128)(2,1)}, u32[]{:S(2)}, u32[]{:S(2)}) async-start(bf16[16,2,48,1024]{3,2,1,0:T(8,128)(2,1)} %bitcast.599), calls=%async_computation | async-start | bytes 6291456 | tf_op jit(solution)/shard_map/all_to_all | solution.py:260
  323.1 88.6 %all-gather.11.cloned.1.call-start = ((), (), s32[]{:S(2)}) async-start(), calls=%async_computation.11 | async-start | bytes 2359296 | tf_op jit(solution)/shard_map/all_gather | solution.py:258
  324.8 200.7 %copy-start.38 = (f32[128,32]{0,1:T(8,128)}, f32[128,32]{0,1:T(8,128)S(1)}, u32[]{:S(2)}) copy-start(f32[128,32]{0,1:T(8,128)S(1)} %fusion.258) | copy-start | bytes 49156
  363.4 48.2 %all-to-all-start.2 = ((bf16[16,2,48,1024]{3,2,1,0:T(8,128)(2,1)}), bf16[16,2,48,1024]{3,2,1,0:T(8,128)(2,1)}, u32[]{:S(2)}, u32[]{:S(2)}) async-start(bf16[16,2,48,1024]{3,2,1,0:T(8,128)(2,1)} %bitcast.600), calls=%async_computation.2 | async-start | bytes 6291456 | tf_op jit(solution)/shard_map/all_to_all | solution.py:282
  426.1 43.4 %all-to-all-start.3 = ((bf16[16,2,48,1024]{3,2,1,0:T(8,128)(2,1)}), bf16[16,2,48,1024]{3,2,1,0:T(8,128)(2,1)}, u32[]{:S(2)}, u32[]{:S(2)}) async-start(bf16[16,2,48,1024]{3,2,1,0:T(8,128)(2,1)} %copy.215), calls=%async_computation.3 | async-start | bytes 6291456 | tf_op jit(solution)/shard_map/all_to_all | solution.py:305
  469.6 43.0 %all-to-all-start.1 = ((bf16[16,2,48,1024]{3,2,1,0:T(8,128)(2,1)}), bf16[16,2,48,1024]{3,2,1,0:T(8,128)(2,1)}, u32[]{:S(2)}, u32[]{:S(2)}) async-start(bf16[16,2,48,1024]{3,2,1,0:T(8,128)(2,1)} %copy.212), calls=%async_computation.1 | async-start | bytes 6291456 | tf_op jit(solution)/shard_map/all_to_all | solution.py:268
  476.2 439.1 %reduce-scatter.7.cloned.1.call-start = ((), (), s32[]{:S(2)}) async-start(), calls=%async_computation.12 | async-start | bytes 20971520 | tf_op jit(solution)/shard_map/reduce_scatter | solution.py:338
  616.1 381.5 %reduce-scatter.13.cloned.1.call-start = ((), (), s32[]{:S(2)}) async-start(), calls=%async_computation.15 | async-start | bytes 4456448
  921.7 109.9 %reduce-scatter.11.cloned.1.call-start = ((), (), s32[]{:S(2)}) async-start(), calls=%async_computation.14 | async-start | bytes 2359296 | tf_op jit(solution)/shard_map/reduce_scatter | solution.py:365
  928.2 142.5 %reduce-scatter.9.cloned.1.call-start = ((), (), s32[]{:S(2)}) async-start(), calls=%async_computation.13 | async-start | bytes 4718592 | tf_op jit(solution)/shard_map/reduce_scatter | solution.py:362
  936.6 314.0 %all-reduce.4.cloned.1.call-start = ((), (), s32[]{:S(2)}) async-start(), calls=%async_computation.16 | async-start | bytes 25427968 | tf_op jit(solution)/shard_map/psum | solution.py:369
  1002.6 70.2 %copy-start.16 = (bf16[1024,512]{1,0:T(8,128)(2,1)S(1)}, bf16[1024,512]{1,0:T(8,128)(2,1)}, u32[]{:S(2)}) copy-start(bf16[1024,512]{1,0:T(8,128)(2,1)} %param.33) | copy-start | bytes 3145732
  1002.6 71.7 %copy-start.17 = (bf16[1024,512]{1,0:T(8,128)(2,1)S(1)}, bf16[1024,512]{1,0:T(8,128)(2,1)}, u32[]{:S(2)}) copy-start(bf16[1024,512]{1,0:T(8,128)(2,1)} %param.34) | copy-start | bytes 3145732
  1002.7 71.7 %copy-start.37 = (bf16[128,1024]{1,0:T(8,128)(2,1)S(1)}, bf16[128,1024]{1,0:T(8,128)(2,1)}, u32[]{:S(2)}) copy-start(bf16[128,1024]{1,0:T(8,128)(2,1)} %reduce-scatter.13.cloned.1.call-done) | copy-start | bytes 786436
  1006.0 68.9 %copy-start.50 = (f32[1024]{0:T(1024)S(1)}, f32[1024]{0:T(1024)}, u32[]{:S(2)}) copy-start(f32[1024]{0:T(1024)} %get-tuple-element.340) | copy-start | bytes 12292
  (36 other events, 168.7 us)
Sparse Core Ops, SparseCore 0:
  14.5 54.8 all-gather.4
  71.0 153.6 all-gather.6
  226.5 33.4 all-gather.8
  325.3 86.3 all-gather.10
  616.2 299.0 reduce-scatter.6
  921.8 75.7 reduce-scatter.12
  1000.0 31.5 reduce-scatter.10
  1034.0 36.6 reduce-scatter.8
  1077.8 172.7 all-reduce.3
where the time goes:
time: 1280 us; the launch traced here: 1270 us
  waiting for transfers between devices  832 us (65%)
  local copies, waits for them, and re-layouts  121 us (9%)
  matrix products  109 us (9%)
  blocking collectives  68.8 us (5%)
  other arithmetic  56.2 us (4%)
  loops' own time  37.6 us (3%)
  starting transfers between devices  29.5 us (2%)
  between operations  14.9 us (1%)
    reduce_scatter x1, waiting for transfers between devices, local(): lax.psum_scatter(key_terms.astype(jnp.bfloat16), 'context', scatter_dimen...  299 us
    all_gather x1, waiting for transfers between devices, local(): whole_pairs = lax.all_gather(block_pairs, 'context', axis=0, tiled=True)  140 us
    psum x1, waiting for transfers between devices, local(): lax.psum((query_grad, key_grad, value_grad, out_grad, router_grad, norm1_...  106 us
    psum x1, blocking collectives, local(): lax.psum((query_grad, key_grad, value_grad, out_grad, router_grad, norm1_...  68.8 us
    all_gather x1, waiting for transfers between devices, local(): block_pairs = lax.all_gather(key_value_rows, 'expert', axis=0, tiled=True)  55 us
    unnamed x10, waiting for transfers between devices  54.7 us
    reduce_scatter x1, waiting for transfers between devices, local(): lax.psum_scatter(gate_up_grad.astype(jnp.bfloat16), ('context', 'dp'), sc...  37.3 us
    all_to_all x1, waiting for transfers between devices, local(): lax.all_to_all(grad_in_rows, 'expert', split_axis=0, concat_axis=0, tiled...  30.7 us
  transfers between devices with their start and end apart: 13, of which 11 were waited for; matrix products, arithmetic and copies ran while one was open for 13% of the time, Pallas kernels for 0%

commit v1 on v0

v1 whole, which is shorter than its diff:
```python
import functools

import jax
import jax.numpy as jnp
import numpy as np
from jax import lax
from jax.experimental import pallas as pl
from jax.experimental.pallas import tpu as pltpu
from jax.sharding import PartitionSpec as P

D = 1024
HEAD_DIM = 64
F = 512
EXPERTS = 32
CAP = 48
TOK = 128
BLOCK = 2048
LANES = 128
SLOTS = EXPERTS * CAP
PAIRS = 8
CHUNK = 512

norm_eps = 1e-06
score_scale = 0.015625
branch_scale = 0.22
rope_base = 10000.0
huge_negative = -1e30
bf16 = jnp.bfloat16
f32 = jnp.float32
VMEM_LIMIT = 56 * 1024 * 1024


def call(kernel, out_shape, flops, moved, **kw):
    return pl.pallas_call(
        kernel,
        out_shape=out_shape,
        compiler_params=pltpu.CompilerParams(vmem_limit_bytes=VMEM_LIMIT),
        cost_estimate=pl.CostEstimate(flops=int(flops), bytes_accessed=int(moved), transcendentals=0),
        **kw,
    )


def struct(shape, dtype):
    return jax.ShapeDtypeStruct(shape, dtype)


def dot(a, b):
    return jnp.dot(a, b, preferred_element_type=f32)


def dot_rows(a, b):
    return lax.dot_general(a, b, (((1,), (1,)), ((), ())), preferred_element_type=f32)


def dot_down(a, b):
    return lax.dot_general(a, b, (((0,), (0,)), ((), ())), preferred_element_type=f32)


def split2(x):
    hi = x.astype(bf16)
    return hi, (x - hi.astype(f32)).astype(bf16)


def lane_index(shape):
    return lax.broadcasted_iota(jnp.int32, shape, len(shape) - 1)


def project_kernel(x_ref, gain_ref, wq_ref, wk_ref, wv_ref, cos_ref, sin_ref, act_ref, q_ref, kv_ref):
    x = x_ref[...].astype(f32)
    inverse = lax.rsqrt(jnp.mean(x * x, axis=-1, keepdims=True) + norm_eps)
    act = (x * inverse * gain_ref[...]).astype(bf16)
    act_ref[...] = act
    cos = cos_ref[...]
    sin = sin_ref[...]
    lane = lane_index((TOK, LANES))
    first = lane % HEAD_DIM < HEAD_DIM // 2
    left = lane < HEAD_DIM

    def turn(v):
        moved = jnp.where(first, pltpu.roll(v, LANES - 32, 1), pltpu.roll(v, 32, 1))
        return v * cos + moved * sin

    q = dot(act, wq_ref[...])
    for j in range(PAIRS):
        rows = turn(q[:, j * LANES : (j + 1) * LANES]).astype(bf16)
        q_ref[2 * j] = rows[: TOK // 2]
        q_ref[2 * j + 1] = rows[TOK // 2 :]
    k = dot(act, wk_ref[...])
    v = dot(act, wv_ref[...])
    for b in range(PAIRS // 2):
        kb = turn(k[:, b * LANES : (b + 1) * LANES])
        vb = v[:, b * LANES : (b + 1) * LANES]
        even = jnp.where(left, kb, pltpu.roll(vb, HEAD_DIM, 1)).astype(bf16)
        odd = jnp.where(left, pltpu.roll(kb, HEAD_DIM, 1), vb).astype(bf16)
        kv_ref[4 * b] = even
        kv_ref[4 * b + 1] = even
        kv_ref[4 * b + 2] = odd
        kv_ref[4 * b + 3] = odd


def project(x, gain, wq, wk, wv, cos, sin):
    return call(
        project_kernel,
        (struct((TOK, D), bf16), struct((16, TOK // 2, LANES), bf16), struct((16, TOK, LANES), bf16)),
        2 * TOK * D * 2048,
        6e6,
        name="project",
    )(x, gain.reshape(1, D), wq, wk, wv, cos, sin)


def query_of_head(q, head, left):
    q = q.astype(f32) * score_scale
    if head:
        q = pltpu.roll(q, HEAD_DIM, 1)
    return jnp.where(left, q, 0.0).astype(bf16)


def forward_kernel(place_ref, q_ref, kv_ref, o_ref, low_ref, lse_ref, qm_ref, top_ref, acc_ref):
    tile = 1024
    context = place_ref[0]
    half = place_ref[1]
    left = lane_index((CHUNK, LANES)) < HEAD_DIM
    left_keys = lane_index((tile, LANES)) < HEAD_DIM
    for chunk in range(2):
        whole = 2 * (context if chunk == 0 else 3 - context) + chunk
        for head in range(2):
            qm_ref[head] = query_of_head(q_ref[chunk], head, left)
            top_ref[head] = jnp.full((CHUNK, LANES), huge_negative, f32)
            acc_ref[head] = jnp.zeros((CHUNK, LANES), f32)

        def step(index, masked):
            keys = kv_ref[pl.ds(pl.multiple_of(index * tile, tile), tile), :]
            values = jnp.where(left_keys, jnp.ones_like(keys), keys)
            for head in range(2):
                for part in range(2):
                    rows = slice(part * 256, part * 256 + 256)
                    s = dot_rows(qm_ref[head, rows], keys)
                    if masked:
                        r = lax.broadcasted_iota(jnp.int32, s.shape, 0) + part * 256
                        place = r + (r // 64) * 64 + half * 64
                        s = jnp.where(lane_index(s.shape) <= place, s, huge_negative)
                    old = top_ref[head, rows]
                    new = jnp.maximum(old, jnp.max(s, axis=1, keepdims=True))
                    p = jnp.exp(s - new[:, :1]).astype(bf16)
                    acc_ref[head, rows] = acc_ref[head, rows] * jnp.exp(old - new) + dot(p, values)
                    top_ref[head, rows] = new

        def visit(index, carry):
            step(index, False)
            return carry

        lax.fori_loop(0, whole, visit, 0)
        step(whole, True)
        outs = []
        for head in range(2):
            acc = acc_ref[head]
            outs.append(pltpu.roll(acc, HEAD_DIM, 1) / acc)
            total = top_ref[head] + jnp.log(jnp.where(left, acc, 1.0))
            lse_ref[2 * chunk + head] = jnp.transpose(total)[0:8]
        o = jnp.where(left, outs[0], pltpu.roll(outs[1], HEAD_DIM, 1))
        o_ref[chunk] = o
        low_ref[chunk] = o.astype(bf16)


def attend_forward(place, q, kv):
    smem = pl.BlockSpec(memory_space=pltpu.SMEM)
    vmem = pl.BlockSpec(memory_space=pltpu.VMEM)
    return call(
        forward_kernel,
        (
            struct((2, CHUNK, LANES), f32),
            struct((2, CHUNK, LANES), bf16),
            struct((4, 8, CHUNK), f32),
        ),
        2e10,
        4e6,
        in_specs=[smem, vmem, vmem],
        out_specs=(vmem, vmem, vmem),
        scratch_shapes=[
            pltpu.VMEM((2, CHUNK, LANES), bf16),
            pltpu.VMEM((2, CHUNK, LANES), f32),
            pltpu.VMEM((2, CHUNK, LANES), f32),
        ],
        name="attend",
    )(place, q, kv)


def backward_kernel(
    place_ref, q_ref, do_ref, o_ref, lse_ref, kv_ref, dq_ref, dkv_ref, qm_ref, dom_ref, row_ref, dqt_ref, acc_ref
):
    tile = 512
    context = place_ref[0]
    half = place_ref[1]
    left = lane_index((CHUNK, LANES)) < HEAD_DIM
    acc_ref[...] = jnp.zeros_like(acc_ref)
    for chunk in range(2):
        whole = 2 * (2 * (context if chunk == 0 else 3 - context) + chunk)
        do = do_ref[chunk].astype(f32)
        product = jnp.transpose(do * o_ref[chunk])
        for head in range(2):
            qm_ref[head] = query_of_head(q_ref[chunk], head, left)
            moved = do if head else pltpu.roll(do, HEAD_DIM, 1)
            dom_ref[head] = jnp.where(left, 0.0, moved).astype(bf16)
            dqt_ref[head] = jnp.zeros((LANES, CHUNK), f32)
            rows = product[head * HEAD_DIM : (head + 1) * HEAD_DIM]
            row_ref[head] = jnp.broadcast_to(jnp.sum(rows, axis=0, keepdims=True), (8, CHUNK))

        def step(index, offset):
            span = pl.ds(pl.multiple_of(index * tile, tile), tile)
            keys = kv_ref[span, :]
            for head in range(2):
                qm = qm_ref[head]
                dom = dom_ref[head]
                s = dot_rows(keys, qm)
                dp = dot_rows(keys, dom)
                p = jnp.exp(s - lse_ref[2 * chunk + head, 0:1])
                if offset is not None:
                    r = lane_index(s.shape)
                    place = r + (r // 64) * 64 + half * 64
                    key = lax.broadcasted_iota(jnp.int32, s.shape, 0) + offset
                    p = jnp.where(key <= place, p, 0.0)
                ds = (p * (dp - row_ref[head, 0:1])).astype(bf16)
                acc_ref[span, :] += dot(ds, qm) + dot(p.astype(bf16), dom)
                dqt_ref[head] += dot_down(keys, ds)

        def visit(index, carry):
            step(index, None)
            return carry

        lax.fori_loop(0, whole, visit, 0)
        step(whole, 0)
        step(whole + 1, tile)
        parts = [jnp.transpose(dqt_ref[head]) * score_scale for head in range(2)]
        dq_ref[chunk] = jnp.where(left, parts[0], pltpu.roll(parts[1], HEAD_DIM, 1)).astype(bf16)
    dkv_ref[...] = acc_ref[...].astype(bf16)


def attend_backward(place, q, do, o, lse, kv):
    smem = pl.BlockSpec(memory_space=pltpu.SMEM)
    vmem = pl.BlockSpec(memory_space=pltpu.VMEM)
    rows = kv.shape[0]
    return call(
        backward_kernel,
        (struct((2, CHUNK, LANES), bf16), struct((rows, LANES), bf16)),
        5e10,
        8e6,
        in_specs=[smem] + [vmem] * 5,
        out_specs=(vmem, vmem),
        scratch_shapes=[
            pltpu.VMEM((2, CHUNK, LANES), bf16),
            pltpu.VMEM((2, CHUNK, LANES), bf16),
            pltpu.VMEM((2, 8, CHUNK), f32),
            pltpu.VMEM((2, LANES, CHUNK), f32),
            pltpu.VMEM((rows, LANES), f32),
        ],
        name="attend_back",
    )(place, q, do, o, lse, kv)


def middle_kernel(
    att_ref, x_ref, wo_ref, gain_ref, wr_ref, pick_ref, attended_ref, hidden_ref, act_ref, probs_ref, send_ref
):
    for j in range(PAIRS):
        for h in range(2):
            attended_ref[h * 64 : h * 64 + 64, j * LANES : (j + 1) * LANES] = att_ref[2 * j + h]
    hidden = x_ref[...].astype(f32) + branch_scale * dot(attended_ref[...], wo_ref[...])
    hidden_ref[...] = hidden
    inverse = lax.rsqrt(jnp.mean(hidden * hidden, axis=-1, keepdims=True) + norm_eps)
    act = (hidden * inverse * gain_ref[...]).astype(bf16)
    act_ref[...] = act
    send_ref[...] = dot(pick_ref[...], act).astype(bf16)
    logits = dot(act, wr_ref[...])
    raised = jnp.exp(logits - jnp.max(logits, axis=-1, keepdims=True))
    probs_ref[...] = raised / jnp.sum(raised, axis=-1, keepdims=True)


def middle(att, x, wo, gain, wr, pick):
    return call(
        middle_kernel,
        (
            struct((TOK, D), bf16),
            struct((TOK, D), f32),
            struct((TOK, D), bf16),
            struct((TOK, EXPERTS), f32),
            struct((SLOTS, D), bf16),
        ),
        2 * TOK * D * (D + SLOTS),
        8e6,
        name="middle",
    )(att, x, wo, gain.reshape(1, D), wr, pick)


def expert_kernel(x_ref, top_ref, gu_ref, down_ref, back_ref, hidden_ref, mixed_ref, gg_ref):
    ones = jnp.ones((8, F), bf16)
    for part in range(2):
        take = slice(8 * part, 8 * part + 8)
        rows = slice(384 * part, 384 * part + 384)
        pre = dot(x_ref[take].reshape(384, D), gu_ref[...])
        raw = branch_scale * dot_rows(top_ref[take].reshape(384, D), down_ref[...])
        gate = pre[:, :F]
        up = pre[:, F:]
        sig = 1.0 / (1.0 + jnp.exp(-gate))
        act = gate * sig
        hidden = (act * up).astype(bf16)
        hidden_ref[rows] = hidden
        hi, lo = split2(hidden.astype(f32) * raw)
        gg_ref[:, rows] = dot_rows(ones, hi) + dot_rows(ones, lo)
        mixed_gate = (raw * up * sig * (1.0 + gate * (1.0 - sig))).astype(bf16)
        mixed_up = (raw * act).astype(bf16)
        mixed_ref[rows, :F] = mixed_gate
        mixed_ref[rows, F:] = mixed_up
        back = dot_rows(mixed_gate, gu_ref[:, :F]) + dot_rows(mixed_up, gu_ref[:, F:])
        back_ref[take] = back.astype(bf16).reshape(8, CAP, D)


def experts(x, top, gate_up, down):
    per = pl.BlockSpec((16, None, CAP, D), lambda n: (0, n, 0, 0))
    return call(
        expert_kernel,
        (
            struct((16, 2, CAP, D), bf16),
            struct((2, 768, F), bf16),
            struct((2, 768, D), bf16),
            struct((2, 8, 768), f32),
        ),
        2 * SLOTS * D * 2560,
        2e7,
        grid=(2,),
        in_specs=[
            per,
            per,
            pl.BlockSpec((None, D, D), lambda n: (n, 0, 0)),
            pl.BlockSpec((None, F, D), lambda n: (n, 0, 0)),
        ],
        out_specs=(
            per,
            pl.BlockSpec((None, 768, F), lambda n: (n, 0, 0)),
            pl.BlockSpec((None, 768, D), lambda n: (n, 0, 0)),
            pl.BlockSpec((None, 8, 768), lambda n: (n, 0, 0)),
        ),
        name="experts",
    )(x, top, gate_up, down)


def expert_grads_kernel(x_ref, top_ref, gate_ref, hidden_ref, mixed_ref, down_ref, out_ref, dgu_ref, ddown_ref):
    hidden = hidden_ref[...]
    gate = gate_ref[...]
    out_ref[...] = dot(hidden, down_ref[...]).astype(bf16).reshape(16, CAP, D)
    top = (branch_scale * gate * top_ref[...].reshape(768, D).astype(f32)).astype(bf16)
    ddown_ref[...] = dot_down(hidden, top).astype(bf16)
    mixed = (gate * mixed_ref[...].astype(f32)).astype(bf16)
    dgu_ref[...] = dot_down(x_ref[...].reshape(768, D), mixed).astype(bf16)


def expert_grads(x, top, gate, hidden, mixed, down):
    per = pl.BlockSpec((16, None, CAP, D), lambda n: (0, n, 0, 0))
    return call(
        expert_grads_kernel,
        (struct((16, 2, CAP, D), bf16), struct((2, D, D), bf16), struct((2, F, D), bf16)),
        2 * SLOTS * D * 2048,
        2.4e7,
        grid=(2,),
        in_specs=[
            per,
            per,
            pl.BlockSpec((None, 768, 1), lambda n: (n, 0, 0)),
            pl.BlockSpec((None, 768, F), lambda n: (n, 0, 0)),
            pl.BlockSpec((None, 768, D), lambda n: (n, 0, 0)),
            pl.BlockSpec((None, F, D), lambda n: (n, 0, 0)),
        ],
        out_specs=(
            per,
            pl.BlockSpec((None, D, D), lambda n: (n, 0, 0)),
            pl.BlockSpec((None, F, D), lambda n: (n, 0, 0)),
        ),
        name="expert_grads",
    )(x, top, gate, hidden, mixed, down)


def turn_back_kernel(
    back_ref, mix_ref, spot_ref, gg_ref, owner_ref, probs_ref, wr_ref, act_ref, hidden_ref, gain_ref, top_ref, wo_ref,
    state_ref, attn_ref, send_ref, router_ref, norm_ref,
):
    both = dot(mix_ref[...], back_ref[...])
    grad = both[:TOK] + both[TOK:]
    hi, lo = split2(spot_ref[...].astype(f32) * gg_ref[...])
    grad_probs = dot(hi, owner_ref[...]) + dot(lo, owner_ref[...])
    probs = probs_ref[...]
    logits = probs * (grad_probs - jnp.sum(probs * grad_probs, axis=-1, keepdims=True))
    hi, lo = split2(logits)
    grad = grad + dot_rows(hi, wr_ref[...]) + dot_rows(lo, wr_ref[...])
    act = act_ref[...]
    router_ref[...] = dot_down(act, hi) + dot_down(act, lo)
    hidden = hidden_ref[...]
    inverse = lax.rsqrt(jnp.mean(hidden * hidden, axis=-1, keepdims=True) + norm_eps)
    normed = hidden * inverse
    norm_ref[...] = jnp.broadcast_to(jnp.sum(grad * normed, axis=0, keepdims=True), (8, D))
    scaled = grad * gain_ref[...]
    state = top_ref[...].astype(f32) + inverse * (scaled - normed * jnp.mean(scaled * normed, axis=-1, keepdims=True))
    state_ref[...] = state
    attn = (branch_scale * state).astype(bf16)
    attn_ref[...] = attn
    attended = dot_rows(attn, wo_ref[...]).astype(bf16)
    for j in range(PAIRS):
        for h in range(2):
            send_ref[2 * j + h] = attended[h * 64 : h * 64 + 64, j * LANES : (j + 1) * LANES]


def turn_back(back, mix, spot, gg, owner, probs, wr, act, hidden, gain, top, wo):
    return call(
        turn_back_kernel,
        (
            struct((TOK, D), f32),
            struct((TOK, D), bf16),
            struct((16, TOK // 2, LANES), bf16),
            struct((D, EXPERTS), f32),
            struct((8, D), f32),
        ),
        2 * 256 * D * (D + SLOTS),
        8e6,
        name="turn_back",
    )(back, mix, spot, gg, owner, probs, wr, act, hidden, gain.reshape(1, D), top, wo)


def finish_kernel(
    dq_ref, dkv_ref, cos_ref, sin_ref, x_ref, gain_ref, wq_ref, wk_ref, wv_ref, state_ref, act_ref,
    out_ref, norm_ref, dw_ref, flat_ref,
):
    cos = cos_ref[...]
    sin = sin_ref[...]
    lane = lane_index((TOK, LANES))
    first = lane % HEAD_DIM < HEAD_DIM // 2
    left = lane < HEAD_DIM

    def back(v):
        scaled = v * sin
        return v * cos + jnp.where(first, pltpu.roll(scaled, LANES - 32, 1), pltpu.roll(scaled, 32, 1))

    for j in range(PAIRS):
        rows = jnp.concatenate([dq_ref[2 * j], dq_ref[2 * j + 1]], axis=0).astype(f32)
        flat_ref[:, j * LANES : (j + 1) * LANES] = back(rows).astype(bf16)
    for b in range(PAIRS // 2):
        even = dkv_ref[4 * b].astype(f32) + dkv_ref[4 * b + 1].astype(f32)
        odd = dkv_ref[4 * b + 2].astype(f32) + dkv_ref[4 * b + 3].astype(f32)
        k = jnp.where(left, even, pltpu.roll(odd, HEAD_DIM, 1))
        v = jnp.where(left, pltpu.roll(even, HEAD_DIM, 1), odd)
        flat_ref[:, D + b * LANES : D + (b + 1) * LANES] = back(k).astype(bf16)
        flat_ref[:, D + 512 + b * LANES : D + 512 + (b + 1) * LANES] = v.astype(bf16)
    dw_ref[...] = dot_down(act_ref[...], flat_ref[...]).astype(bf16)
    grad = dot_rows(flat_ref[:, :D], wq_ref[...])
    grad = grad + dot_rows(flat_ref[:, D : D + 512], wk_ref[...])
    grad = grad + dot_rows(flat_ref[:, D + 512 :], wv_ref[...])
    x = x_ref[...].astype(f32)
    inverse = lax.rsqrt(jnp.mean(x * x, axis=-1, keepdims=True) + norm_eps)
    normed = x * inverse
    norm_ref[...] = jnp.broadcast_to(jnp.sum(grad * normed, axis=0, keepdims=True), (8, D))
    scaled = grad * gain_ref[...]
    out_ref[...] = state_ref[...] + inverse * (scaled - normed * jnp.mean(scaled * normed, axis=-1, keepdims=True))


def finish(dq, dkv, cos, sin, x, gain, wq, wk, wv, state, act):
    return call(
        finish_kernel,
        (struct((TOK, D), f32), struct((8, D), f32), struct((D, 2048), bf16)),
        2 * 2 * 256 * D * 2048,
        1.2e7,
        scratch_shapes=[pltpu.VMEM((TOK, 2048), bf16)],
        name="finish",
    )(dq, dkv, cos, sin, x, gain.reshape(1, D), wq, wk, wv, state, act)


def to_owners(x):
    return lax.all_to_all(x, "expert", split_axis=0, concat_axis=0, tiled=True)


def mirror(x):
    return lax.ppermute(x, "context", [(0, 3), (1, 2), (2, 1), (3, 0)])


def swap_cores(x):
    return lax.ppermute(x, "dp", [(0, 1), (1, 0)])


def sum_everywhere(x):
    rows, columns = x.shape
    core = lax.axis_index("dp")
    parts = x.reshape(2, rows // 2, columns)
    mine = lax.dynamic_index_in_dim(parts, core, 0, False)
    other = lax.dynamic_index_in_dim(parts, 1 - core, 0, False)
    half = (mine.astype(f32) + swap_cores(other).astype(f32)).astype(bf16)
    pieces = lax.all_to_all(
        half.reshape(64, rows // 128, columns), ("expert", "context"), split_axis=0, concat_axis=0, tiled=True
    )
    total = jnp.sum(pieces.astype(f32), 0).astype(bf16)
    half = lax.all_gather(total, ("expert", "context"), axis=0, tiled=True)
    other = swap_cores(half)
    low = jnp.where(core == 0, half, other)
    high = jnp.where(core == 0, other, half)
    return jnp.concatenate([low, high], 0)


def local(
    layer_input, grad_output, norm1_gain, norm2_gain, w_query, w_key, w_value, w_out, w_router, w_gate_up, w_down, routes
):
    context = lax.axis_index("context")
    expert = lax.axis_index("expert")
    x = layer_input[0, 0]
    top = grad_output[0, 0]

    positions = context * BLOCK + expert * TOK + jnp.arange(TOK, dtype=jnp.int32)
    frequency = rope_base ** (-jnp.arange(0, HEAD_DIM, 2, dtype=f32) / HEAD_DIM)
    angles = positions.astype(f32)[:, None] * frequency[None, :]
    cos, sin = jnp.cos(angles), jnp.sin(angles)
    cos = jnp.concatenate([cos] * 4, -1)
    sin = jnp.concatenate([-sin, sin] * 2, -1)

    hits = jnp.sum((routes[0, 0][:, :, None] == jnp.arange(EXPERTS, dtype=jnp.int32)).astype(f32), 1)
    lower = np.tril(np.ones((TOK, TOK), np.float32), -1)
    place = dot(jnp.asarray(lower, bf16), hits.astype(bf16))
    owner = np.repeat(np.eye(EXPERTS, dtype=np.float32), CAP, 0)
    owner16 = jnp.asarray(owner, bf16)
    slot_number = jnp.arange(SLOTS, dtype=jnp.int32) % CAP
    marked = jnp.where(hits > 0.5, place, 255.0).astype(bf16)
    spot = (dot_rows(marked, owner16) == slot_number[None, :].astype(f32)).astype(bf16)
    pick = (dot_rows(owner16, marked) == slot_number[:, None].astype(f32)).astype(bf16)

    act1, q_send, kv_send = project(x, norm1_gain, w_query, w_key, w_value, cos, sin)
    kv_block = to_owners(kv_send).reshape(BLOCK, LANES)
    kv = lax.all_gather(kv_block, "context", axis=0, tiled=True)
    q_own = to_owners(q_send).reshape(2, CHUNK, LANES)
    q = jnp.stack([q_own[0], mirror(q_own[1])], 0)

    gate_up = lax.all_gather(w_gate_up, ("context", "dp"), axis=1, tiled=True)
    down = lax.all_gather(w_down, ("context", "dp"), axis=1, tiled=True)
    top_rows = to_owners(dot(pick, top).astype(bf16).reshape(16, 2, CAP, D))

    seat = jnp.stack([context, expert % 2]).astype(jnp.int32)
    o, o_low, lse = attend_forward(seat, q, kv)
    o_own = jnp.stack([o_low[0], mirror(o_low[1])], 0)
    att = to_owners(o_own.reshape(16, TOK // 2, LANES))

    attended, hidden, act2, probs, send = middle(att, x, w_out, norm2_gain, w_router, pick)
    rows = to_owners(send.reshape(16, 2, CAP, D))

    hi, lo = split2(probs)
    mix = jnp.concatenate([dot(hi, owner16.T).astype(bf16) * spot, dot(lo, owner16.T).astype(bf16) * spot], 0)
    gate_slots = jnp.sum(mix[:TOK].astype(f32) + mix[TOK:].astype(f32), 0).reshape(16, 2, CAP)
    gates = to_owners(gate_slots).transpose(1, 0, 2).reshape(2, 768, 1)

    grad_rows, expert_hidden, mixed, gg = experts(rows, top_rows, gate_up, down)
    back = to_owners(grad_rows).reshape(SLOTS, D)
    gg_back = to_owners(gg[:, 0].reshape(2, 16, CAP).transpose(1, 0, 2)).reshape(1, SLOTS)
    out_rows, dgu, ddown = expert_grads(rows, top_rows, gates, expert_hidden, mixed, down)

    state, attn, do_send, router_grad, norm2_grad = turn_back(
        back, mix, spot, gg_back, owner16, probs, w_router, act2, hidden, norm2_gain, top, w_out
    )
    do_own = to_owners(do_send).reshape(2, CHUNK, LANES)
    do = jnp.stack([do_own[0], mirror(do_own[1])], 0)

    grad_gate_up = lax.psum_scatter(dgu, ("context", "dp"), scatter_dimension=1, tiled=True).astype(f32)
    grad_down = lax.psum_scatter(ddown, ("context", "dp"), scatter_dimension=1, tiled=True).astype(f32)

    out_grad = dot_down(attended, attn).astype(bf16)
    extra = jnp.concatenate(
        [router_grad.reshape(32, D), norm2_grad[:1], jnp.zeros((95, D), f32)], 0
    ).astype(bf16)
    early = sum_everywhere(jnp.concatenate([out_grad, extra], 0))

    dq, dkv = attend_backward(seat, q, do, o, lse, kv)
    dq_own = jnp.stack([dq[0], mirror(dq[1])], 0).reshape(16, TOK // 2, LANES)
    dq_back = to_owners(dq_own)
    dkv_own = lax.psum_scatter(dkv, "context", scatter_dimension=0, tiled=True)
    dkv_back = to_owners(dkv_own.reshape(16, TOK, LANES))

    grad_input, norm1_grad, dw = finish(
        dq_back, dkv_back, cos, sin, x, norm1_gain, w_query, w_key, w_value, state, act1
    )

    returned = to_owners(out_rows).reshape(SLOTS, D)
    mixture = dot(mix, returned)
    block_out = hidden + branch_scale * (mixture[:TOK] + mixture[TOK:])

    last = jnp.concatenate([norm1_grad[:1], jnp.zeros((127, D), f32)], 0).astype(bf16)
    last = jnp.concatenate([last, jnp.zeros((128, D), bf16)], 1)
    late = sum_everywhere(jnp.concatenate([dw, last], 0))
    dw_sum = late[:D].astype(f32)
    return (
        block_out.reshape(1, 1, TOK, D),
        grad_input.reshape(1, 1, TOK, D),
        late[D, :D].astype(f32),
        early[D + 32].astype(f32),
        dw_sum[:, :D],
        dw_sum[:, D : D + 512],
        dw_sum[:, D + 512 :],
        early[:D].astype(f32),
        early[D : D + 32].astype(f32).reshape(D, EXPERTS),
        grad_gate_up,
        grad_down,
    )


def solution(mesh):
    tokens = P("dp", "context", "expert", None)
    weights = P("expert", ("context", "dp"), None)
    return jax.shard_map(
        local,
        mesh=mesh,
        in_specs=(tokens, tokens, P(), P(), P(), P(), P(), P(), P(), weights, weights, tokens),
        out_specs=(tokens, tokens, P(), P(), P(), P(), P(), P(), P(), weights, weights),
        check_vma=False,
    )
```

time: 1280 us -> 751 us (0.59)
  waiting for transfers between devices: 832 us -> 308 us
  Pallas kernels: 0 us -> 109 us
  blocking collectives: 68.8 us -> 169 us
  matrix products: 109 us -> 11.7 us
  local copies, waits for them, and re-layouts: 121 us -> 40.9 us
  loops' own time: 37.6 us -> 0 us
  starting transfers between devices: 29.5 us -> 51.2 us
  other arithmetic: 56.2 us -> 35.2 us
    reduce_scatter x3, waiting for transfers between devices: 362 us -> 77.1 us  [the longest x1 38.2 us: local(): lax.psum_scatter(dgu, ('context', 'dp'), scatter_dimension=1, tiled=True)]
    all_to_all x0 -> x7, blocking collectives: none -> 169 us  [the longest x2 95.1 us: sum_everywhere(): lax.all_to_all(half.reshape(64, rows // 128, columns), ('expert', 'contex...]
    all_gather x4 -> x5, waiting for transfers between devices: 225 us -> 88.9 us  [the longest x2 76.5 us: sum_everywhere(): half = lax.all_gather(total, ('expert', 'context'), axis=0, tiled=True)]
    pallas_call x0 -> x8, Pallas kernels: none -> 109 us  [the longest x1 31.7 us: attend_backward(): call(backward_kernel, (struct((2, CHUNK, LANES), bf16), struct((rows, LAN...]
    psum x1 -> x0, waiting for transfers between devices: 106 us -> none  [local(): lax.psum((query_grad, key_grad, value_grad, out_grad, router_grad, norm1_...]
    dot_general x28 -> x6, matrix products: 109 us -> 11.7 us  [the longest x4 9.17 us: dot(): return jnp.dot(a, b, preferred_element_type=f32)]
    psum x1 -> x0, blocking collectives: 68.8 us -> none  [local(): lax.psum((query_grad, key_grad, value_grad, out_grad, router_grad, norm1_...]
    unnamed x10 -> x8, waiting for transfers between devices: 54.7 us -> 2.15 us
  transfers between devices with their start and end apart: 13 -> 23, of which waited for: 11 -> 17; matrix products, arithmetic and copies ran while one was open for 13% -> 8% of each run, Pallas kernels for 0% -> 6%
where the time goes in v1:
time: 751 us; the launch traced here: 740 us
  waiting for transfers between devices  308 us (41%)
  blocking collectives  169 us (23%)
  Pallas kernels  109 us (15%)
  starting transfers between devices  51.2 us (7%)
  local copies, waits for them, and re-layouts  40.9 us (5%)
  other arithmetic  35.2 us (5%)
  between operations  15 us (2%)
  matrix products  11.7 us (2%)
    all_to_all x7, waiting for transfers between devices, to_owners(): return lax.all_to_all(x, 'expert', split_axis=0, concat_axis=0, tiled=True)  115 us
    all_to_all x2, blocking collectives, sum_everywhere(): lax.all_to_all(half.reshape(64, rows // 128, columns), ('expert', 'contex...  95.1 us
    all_gather x2, waiting for transfers between devices, sum_everywhere(): half = lax.all_gather(total, ('expert', 'context'), axis=0, tiled=True)  76.5 us
    all_to_all x5, blocking collectives, to_owners(): return lax.all_to_all(x, 'expert', split_axis=0, concat_axis=0, tiled=True)  73.6 us
    reduce_scatter x1, waiting for transfers between devices, local(): lax.psum_scatter(dgu, ('context', 'dp'), scatter_dimension=1, tiled=True)  38.2 us
    all_to_all x7, starting transfers between devices, to_owners(): return lax.all_to_all(x, 'expert', split_axis=0, concat_axis=0, tiled=True)  36.9 us
    pallas_call x1, Pallas kernels, attend_backward(): call(backward_kernel, (struct((2, CHUNK, LANES), bf16), struct((rows, LAN...  31.7 us
    pallas_call x1, Pallas kernels, attend_forward(): call(forward_kernel, (struct((2, CHUNK, LANES), f32), struct((2, CHUNK, L...  26.1 us
  transfers between devices with their start and end apart: 23, of which 17 were waited for; matrix products, arithmetic and copies ran while one was open for 8% of the time, Pallas kernels for 6%

profile of v1, /device:TPU:1, one launch (start us, length us, event | category | flops | bytes accessed | tf_op | source)
XLA Modules:
  0.0 739.7 jit_solution(3802282169069337037)
XLA Ops:
  12.5 19.0 %all_to_all.70 = bf16[16,128,128]{2,1,0:T(8,128)(2,1)} all-to-all(bf16[16,128,128]{2,1,0:T(8,128)(2,1)} %get-tuple-element.40), channel_id=1, replica_groups=mesh['expert'=16,'context'=4,'dp'=2] {'expert'}, dimensions={0} | all-to-all | bytes 1048576 | tf_op jit(solution)/shard_map/all_to_all | solution.py:473
  52.4 12.4 %all-gather.8.cloned.1.call-done.kv_ref = bf16[8192,128]{1,0:T(8,128)(2,1)} async-done(((bf16[2048,128]{1,0:T(8,128)(2,1)}), bf16[8192,128]{1,0:T(8,128)(2,1)}) %all-gather.8.cloned.1.call-update) | async-done | bytes 2097168 | tf_op jit(solution)/shard_map/all_gather | solution.py:529
  64.7 26.1 %attend.1 = (f32[2,512,128]{2,1,0:T(8,128)}, bf16[2,512,128]{2,1,0:T(8,128)(2,1)}, f32[4,8,512]{2,1,0:T(8,128)}) custom-call(s32[2]{0:T(128)} %pad_add_fusion.place_ref, bf16[2,512,128]{2,1,0:T(8,128)(2,1)} %pad_maximum_fusion.3.q_ref, bf16[8192,128]{1,0:T(8,128)(2,1)} %all-gather.8.cloned.1.call-done.kv_ref), custom_call_target="tpu_custom_call" | custom-call | flops 20000000000 | bytes 4000000 | tf_op jit(solution)/shard_map/attend/pallas_call | solution.py:168
  124.9 27.7 %all-to-all-done.4.top_ref = bf16[16,2,48,1024]{3,2,1,0:T(8,128)(2,1)} async-done(((bf16[16,2,48,1024]{3,2,1,0:T(8,128)(2,1)}), bf16[16,2,48,1024]{3,2,1,0:T(8,128)(2,1)}, u32[]{:S(2)}, u32[]{:S(2)}) %all-to-all-start.4) | async-done | bytes 3145760 | tf_op jit(solution)/shard_map/all_to_all | solution.py:473
  152.7 7.7 %all-to-all-start.3 = ((bf16[16,2,48,1024]{3,2,1,0:T(8,128)(2,1)}), bf16[16,2,48,1024]{3,2,1,0:T(8,128)(2,1)S(1)}, u32[]{:S(2)}, u32[]{:S(2)}) async-start(bf16[16,2,48,1024]{3,2,1,0:T(8,128)(2,1)} %bitcast.67), calls=%async_computation.3 | async-start | bytes 6291456 | tf_op jit(solution)/shard_map/all_to_all | solution.py:473
  160.5 36.1 %all-to-all-done.3.x_ref = bf16[16,2,48,1024]{3,2,1,0:T(8,128)(2,1)S(1)} async-done(((bf16[16,2,48,1024]{3,2,1,0:T(8,128)(2,1)}), bf16[16,2,48,1024]{3,2,1,0:T(8,128)(2,1)S(1)}, u32[]{:S(2)}, u32[]{:S(2)}) %all-to-all-start.3) | async-done | bytes 3145760 | tf_op jit(solution)/shard_map/all_to_all | solution.py:473
  198.2 15.4 %experts.1 = (bf16[16,2,48,1024]{3,2,1,0:T(8,128)(2,1)}, bf16[2,768,512]{2,1,0:T(8,128)(2,1)}, bf16[2,768,1024]{2,1,0:T(8,128)(2,1)}, f32[2,8,768]{2,1,0:T(8,128)}) custom-call(bf16[16,2,48,1024]{3,2,1,0:T(8,128)(2,1)} %copy-done.7, bf16[16,2,48,1024]{3,2,1,0:T(8,128)(2,1)} %all-to-all-done.4.top_ref, ...), custom_call_target="tpu_custom_call" | custom-call | flops 8053063680 | bytes 20000000 | tf_op jit(solution)/shard_map/experts/pallas_call | solution.py:318
  214.6 16.0 %all_to_all.71 = f32[16,2,48]{2,1,0:T(2,128)S(1)} all-to-all(f32[16,2,48]{2,1,0:T(2,128)S(1)} %bitcast.85), channel_id=1, replica_groups=mesh['expert'=16,'context'=4,'dp'=2] {'expert'}, dimensions={0} | all-to-all | bytes 12288 | tf_op jit(solution)/shard_map/all_to_all | solution.py:473
  240.2 29.5 %all-to-all-done.7 = bf16[16,2,48,1024]{3,2,1,0:T(8,128)(2,1)S(1)} async-done(((bf16[16,2,48,1024]{3,2,1,0:T(8,128)(2,1)}), bf16[16,2,48,1024]{3,2,1,0:T(8,128)(2,1)S(1)}, u32[]{:S(2)}, u32[]{:S(2)}) %all-to-all-start.7) | async-done | bytes 3145760 | tf_op jit(solution)/shard_map/all_to_all | solution.py:473
  278.0 16.0 %all_to_all.72 = bf16[16,64,128]{2,1,0:T(8,128)(2,1)S(1)} all-to-all(bf16[16,64,128]{2,1,0:T(8,128)(2,1)} %get-tuple-element.51), channel_id=1, replica_groups=mesh['expert'=16,'context'=4,'dp'=2] {'expert'}, dimensions={0} | all-to-all | bytes 524288 | tf_op jit(solution)/shard_map/all_to_all | solution.py:473
  299.8 31.7 %attend_back.1 = (bf16[2,512,128]{2,1,0:T(8,128)(2,1)}, bf16[8192,128]{1,0:T(8,128)(2,1)}) custom-call(s32[2]{0:T(128)} %pad_add_fusion.place_ref, bf16[2,512,128]{2,1,0:T(8,128)(2,1)} %pad_maximum_fusion.3.q_ref, bf16[2,512,128]{2,1,0:T(8,128)(2,1)} %pad_maximum_fusion.5.do_ref, f32[2,512,128]{2,1,0:T(8,128)} %get-tuple-element.52.o_ref, ...), custom_call_target="tpu_custom_call" | custom-call | flops 49999998976 | bytes 8000000 | tf_op jit(solution)/shard_map/attend_back/pallas_call | solution.py:242
  337.6 10.6 %all_to_all.73.dq_ref = bf16[16,64,128]{2,1,0:T(8,128)(2,1)} all-to-all(bf16[16,64,128]{2,1,0:T(8,128)(2,1)S(1)} %bitcast.69), channel_id=1, replica_groups=mesh['expert'=16,'context'=4,'dp'=2] {'expert'}, dimensions={0} | all-to-all | bytes 524288 | tf_op jit(solution)/shard_map/all_to_all | solution.py:473
  348.3 15.0 %reduce-scatter.4.cloned.1.call-done = bf16[2048,128]{1,0:T(8,128)(2,1)} async-done(((bf16[8192,128]{1,0:T(8,128)(2,1)}), bf16[2048,128]{1,0:T(8,128)(2,1)}) %reduce-scatter.4.cloned.1.call-update) | async-done | bytes 524304 | tf_op jit(solution)/shard_map/reduce_scatter | solution.py:573
  363.2 6.7 all-to-all-start.11
  370.0 10.2 %all-to-all-done.11.dkv_ref = bf16[16,128,128]{2,1,0:T(8,128)(2,1)S(1)} async-done(((bf16[16,128,128]{2,1,0:T(8,128)(2,1)}), bf16[16,128,128]{2,1,0:T(8,128)(2,1)S(1)}, u32[]{:S(2)}, u32[]{:S(2)}) %all-to-all-start.11) | async-done | bytes 524320 | tf_op jit(solution)/shard_map/all_to_all | solution.py:473
  381.0 7.8 %finish.1 = (f32[128,1024]{1,0:T(8,128)}, f32[8,1024]{1,0:T(8,128)}, bf16[1024,2048]{1,0:T(8,128)(2,1)}) custom-call(bf16[16,64,128]{2,1,0:T(8,128)(2,1)} %all_to_all.73.dq_ref, bf16[16,128,128]{2,1,0:T(8,128)(2,1)} %copy-done.13, f32[128,128]{1,0:T(8,128)} %get-tuple-element.132.cos_ref, f32[128,128]{1,0:T(8,128)} %get-tuple-element.133.sin_ref, ...), custom_call_target="tpu_custom_call" | custom-call | flops 2147483648 | bytes 12000000 | tf_op jit(solution)/shard_map/finish/pallas_call | solution.py:462
  406.8 56.7 %all_to_all.74 = bf16[64,9,2048]{2,1,0:T(8,128)(2,1)} all-to-all(bf16[64,9,2048]{2,1,0:T(8,128)(2,1)} %reshape.158), channel_id=1, replica_groups=mesh['expert'=16,'context'=4,'dp'=2] {'expert','context'}, dimensions={0} | all-to-all | bytes 4718592 | tf_op jit(solution)/shard_map/all_to_all | solution.py:491
  470.4 7.9 %concatenate.36 = bf16[1152,1024]{1,0:T(8,128)(2,1)S(1)} concatenate(bf16[1024,1024]{1,0:T(8,128)(2,1)} %convolution_convert_fusion.3, bf16[32,1024]{1,0:T(8,128)(2,1)S(1)} %reshape.159, bf16[1,1024]{1,0:T(2,128)(2,1)S(1)} %slice.124, bf16[95,1024]{1,0:T(8,128)(2,1)S(1)} %broadcast_in_dim.6), dimensions={0} | concatenate | bytes 4718592 | tf_op jit(solution)/shard_map/concatenate | solution.py:568
  485.1 38.4 %all_to_all.75 = bf16[64,9,1024]{2,1,0:T(8,128)(2,1)S(1)} all-to-all(bf16[64,9,1024]{2,1,0:T(8,128)(2,1)} %reshape.161), channel_id=1, replica_groups=mesh['expert'=16,'context'=4,'dp'=2] {'expert','context'}, dimensions={0} | all-to-all | bytes 2359296 | tf_op jit(solution)/shard_map/all_to_all | solution.py:491
  524.6 12.0 %all_to_all.76 = f32[16,2,48]{2,1,0:T(2,128)S(1)} all-to-all(f32[16,2,48]{2,1,0:T(2,128)S(1)} %reshape.148), channel_id=1, replica_groups=mesh['expert'=16,'context'=4,'dp'=2] {'expert'}, dimensions={0} | all-to-all | bytes 12288 | tf_op jit(solution)/shard_map/all_to_all | solution.py:473
  538.0 12.2 %expert_grads.1 = (bf16[16,2,48,1024]{3,2,1,0:T(8,128)(2,1)}, bf16[2,1024,1024]{2,1,0:T(8,128)(2,1)}, bf16[2,512,1024]{2,1,0:T(8,128)(2,1)}) custom-call(bf16[16,2,48,1024]{3,2,1,0:T(8,128)(2,1)} %copy-done.7, bf16[16,2,48,1024]{3,2,1,0:T(8,128)(2,1)} %all-to-all-done.4.top_ref, f32[2,768,1]{2,1,0:T(8,128)} %reshape.174.gate_ref, ...), custom_call_target="tpu_custom_call" | custom-call | flops 6442450944 | bytes 24000000 | tf_op jit(solution)/shard_map/expert_grads/pallas_call | solution.py:357
  561.7 76.5 %all-gather.16.cloned.1.call-done = bf16[64,9,1024]{2,1,0:T(8,128)(2,1)} async-done(((bf16[1,9,1024]{2,1,0:T(8,128)(2,1)}), bf16[64,9,1024]{2,1,0:T(8,128)(2,1)}) %all-gather.16.cloned.1.call-update) | async-done | bytes 1179664 | tf_op jit(solution)/shard_map/all_gather | solution.py:495
  646.6 23.8 %reduce-scatter.8.cloned.1.call-done = bf16[2,64,1024]{2,1,0:T(8,128)(2,1)} async-done(((bf16[2,512,1024]{2,1,0:T(8,128)(2,1)}), bf16[2,64,1024]{2,1,0:T(8,128)(2,1)}) %reduce-scatter.8.cloned.1.call-update) | async-done | bytes 262160 | tf_op jit(solution)/shard_map/reduce_scatter | solution.py:562
  672.2 38.2 %reduce-scatter.6.cloned.1.call-done = bf16[2,128,1024]{2,1,0:T(8,128)(2,1)} async-done(((bf16[2,1024,1024]{2,1,0:T(8,128)(2,1)}), bf16[2,128,1024]{2,1,0:T(8,128)(2,1)}) %reduce-scatter.6.cloned.1.call-update) | async-done | bytes 524304 | tf_op jit(solution)/shard_map/reduce_scatter | solution.py:561
  (148 shorter events, 171.2 us)
Async XLA Ops:
  7.2 57.6 %all-gather.8.cloned.1.call-start = ((), (), s32[]{:S(2)}) async-start(), calls=%async_computation.17 | async-start | bytes 2621440 | tf_op jit(solution)/shard_map/all_gather | solution.py:529
  31.4 129.0 %all-gather.12.cloned.1.call-start = ((), (), s32[]{:S(2)}) async-start(), calls=%async_computation.19 | async-start | bytes 2359296 | tf_op jit(solution)/shard_map/all_gather | solution.py:534
  32.2 10.9 %all-to-all-start = ((bf16[16,64,128]{2,1,0:T(8,128)(2,1)}), bf16[16,64,128]{2,1,0:T(8,128)(2,1)S(1)}, u32[]{:S(2)}, u32[]{:S(2)}) async-start(bf16[16,64,128]{2,1,0:T(8,128)(2,1)} %get-tuple-element.39), calls=%async_computation | async-start | bytes 524288 | tf_op jit(solution)/shard_map/all_to_all | solution.py:473
  35.8 160.8 %all-gather.10.cloned.1.call-start = ((), (), s32[]{:S(2)}) async-start(), calls=%async_computation.18 | async-start | bytes 4718592 | tf_op jit(solution)/shard_map/all_gather | solution.py:533
  43.1 8.5 %collective-permute-start = (bf16[512,128]{1,0:T(8,128)(2,1)S(1)}, bf16[512,128]{1,0:T(8,128)(2,1)S(1)}, u32[]{:S(2)}, u32[]{:S(2)}) collective-permute-start(bf16[512,128]{1,0:T(8,128)(2,1)S(1)} %bitcast.79), channel_id=1, source_target_pairs={{0,6},{2,4},{4,2},{6,0},{1,7},{3,5},{5,3},{7,1},{8,14},{10,12},{12... | collective-permute-start | bytes 393224 | tf_op jit(solution)/shard_map/ppermute | solution.py:477
  52.4 39.6 %copy-start.19 = (bf16[128,128]{1,0:T(8,128)(2,1)S(1)}, bf16[128,128]{1,0:T(8,128)(2,1)}, u32[]{:S(2)}) copy-start(bf16[128,128]{1,0:T(8,128)(2,1)} %constant.85.clone) | copy-start | bytes 98308
  91.8 5.7 collective-permute-start.1
  98.2 13.6 %all-to-all-start.2 = ((bf16[16,64,128]{2,1,0:T(8,128)(2,1)}), bf16[16,64,128]{2,1,0:T(8,128)(2,1)S(1)}, u32[]{:S(2)}, u32[]{:S(2)}) async-start(bf16[16,64,128]{2,1,0:T(8,128)(2,1)} %bitcast.10), calls=%async_computation.2 | async-start | bytes 524288 | tf_op jit(solution)/shard_map/all_to_all | solution.py:473
  112.5 40.2 %all-to-all-start.4 = ((bf16[16,2,48,1024]{3,2,1,0:T(8,128)(2,1)}), bf16[16,2,48,1024]{3,2,1,0:T(8,128)(2,1)}, u32[]{:S(2)}, u32[]{:S(2)}) async-start(bf16[16,2,48,1024]{3,2,1,0:T(8,128)(2,1)} %bitcast.16), calls=%async_computation.4 | async-start | bytes 6291456 | tf_op jit(solution)/shard_map/all_to_all | solution.py:473
  152.7 43.9 %all-to-all-start.3 = ((bf16[16,2,48,1024]{3,2,1,0:T(8,128)(2,1)}), bf16[16,2,48,1024]{3,2,1,0:T(8,128)(2,1)S(1)}, u32[]{:S(2)}, u32[]{:S(2)}) async-start(bf16[16,2,48,1024]{3,2,1,0:T(8,128)(2,1)} %bitcast.67), calls=%async_computation.3 | async-start | bytes 6291456 | tf_op jit(solution)/shard_map/all_to_all | solution.py:473
  230.5 39.2 %all-to-all-start.7 = ((bf16[16,2,48,1024]{3,2,1,0:T(8,128)(2,1)}), bf16[16,2,48,1024]{3,2,1,0:T(8,128)(2,1)S(1)}, u32[]{:S(2)}, u32[]{:S(2)}) async-start(bf16[16,2,48,1024]{3,2,1,0:T(8,128)(2,1)} %get-tuple-element.48), calls=%async_computation.7 | async-start | bytes 6291456 | tf_op jit(solution)/shard_map/all_to_all | solution.py:473
  234.3 129.0 %reduce-scatter.4.cloned.1.call-start = ((), (), s32[]{:S(2)}) async-start(), calls=%async_computation.20 | async-start | bytes 2621440 | tf_op jit(solution)/shard_map/reduce_scatter | solution.py:573
  294.0 5.1 collective-permute-start.2
  332.5 5.1 collective-permute-start.3
  363.2 17.0 %all-to-all-start.11 = ((bf16[16,128,128]{2,1,0:T(8,128)(2,1)}), bf16[16,128,128]{2,1,0:T(8,128)(2,1)S(1)}, u32[]{:S(2)}, u32[]{:S(2)}) async-start(bf16[16,128,128]{2,1,0:T(8,128)(2,1)} %bitcast.74), calls=%async_computation.12 | async-start | bytes 1048576 | tf_op jit(solution)/shard_map/all_to_all | solution.py:473
  369.9 185.5 %all-gather.14.cloned.1.call-start = ((), (), s32[]{:S(2)}) async-start(), calls=%async_computation.23 | async-start | bytes 4259840 | tf_op jit(solution)/shard_map/all_gather | solution.py:495
  394.3 6.4 collective-permute-start.4
  467.2 171.0 %all-gather.16.cloned.1.call-start = ((), (), s32[]{:S(2)}) async-start(), calls=%async_computation.24 | async-start | bytes 2129920 | tf_op jit(solution)/shard_map/all_gather | solution.py:495
  478.4 4.6 collective-permute-start.6
  524.5 145.9 %reduce-scatter.8.cloned.1.call-start = ((), (), s32[]{:S(2)}) async-start(), calls=%async_computation.22 | async-start | bytes 2359296 | tf_op jit(solution)/shard_map/reduce_scatter | solution.py:562
  550.2 160.2 %reduce-scatter.6.cloned.1.call-start = ((), (), s32[]{:S(2)}) async-start(), calls=%async_computation.21 | async-start | bytes 4718592 | tf_op jit(solution)/shard_map/reduce_scatter | solution.py:561
  551.0 91.5 %all-to-all-start.6 = ((bf16[16,2,48,1024]{3,2,1,0:T(8,128)(2,1)}), bf16[16,2,48,1024]{3,2,1,0:T(8,128)(2,1)}, u32[]{:S(2)}, u32[]{:S(2)}) async-start(bf16[16,2,48,1024]{3,2,1,0:T(8,128)(2,1)} %get-tuple-element.47), calls=%async_computation.6 | async-start | bytes 6291456 | tf_op jit(solution)/shard_map/all_to_all | solution.py:473
  558.9 165.0 %collective-permute-start.5 = (bf16[576,2048]{1,0:T(8,128)(2,1)S(1)}, bf16[576,2048]{1,0:T(8,128)(2,1)}, u32[]{:S(2)}, u32[]{:S(2)}) collective-permute-start(bf16[576,2048]{1,0:T(8,128)(2,1)S(1)} %reshape.171), channel_id=1, source_target_pairs={{0,1},{1,0},{2,3},{3,2},{4,5},{5,4},{6,7},{7,6},{8,9},{9,8},{10,11... | collective-permute-start | bytes 7077896 | tf_op jit(solution)/shard_map/ppermute | solution.py:481
  640.8 71.9 %collective-permute-start.7 = (bf16[576,1024]{1,0:T(8,128)(2,1)S(1)}, bf16[576,1024]{1,0:T(8,128)(2,1)}, u32[]{:S(2)}, u32[]{:S(2)}) collective-permute-start(bf16[576,1024]{1,0:T(8,128)(2,1)S(1)} %reshape.173), channel_id=1, source_target_pairs={{0,1},{1,0},{2,3},{3,2},{4,5},{5,4},{6,7},{7,6},{8,9},{9,8},{10,11... | collective-permute-start | bytes 3538952 | tf_op jit(solution)/shard_map/ppermute | solution.py:481
  (19 other events, 191.0 us)
Sparse Core Ops, SparseCore 0:
  31.6 33.1 all-gather.7
  66.4 24.6 all-gather.11
  92.8 32.3 all-gather.9
  331.6 31.5 reduce-scatter.3
  467.3 84.8 all-gather.13
  556.0 82.1 all-gather.15
  641.3 29.0 reduce-scatter.7
  673.5 36.8 reduce-scatter.5

commit v2 on v1

--- a/solution.py
+++ b/solution.py
@@ -1,5 +1,3 @@
-import functools
-
 import jax
 import jax.numpy as jnp
 import numpy as np
@@ -257,9 +255,7 @@
     )(place, q, do, o, lse, kv)
 
 
-def middle_kernel(
-    att_ref, x_ref, wo_ref, gain_ref, wr_ref, pick_ref, attended_ref, hidden_ref, act_ref, probs_ref, send_ref
-):
+def middle_kernel(att_ref, x_ref, wo_ref, gain_ref, pick_ref, attended_ref, hidden_ref, send_ref):
     for j in range(PAIRS):
         for h in range(2):
             attended_ref[h * 64 : h * 64 + 64, j * LANES : (j + 1) * LANES] = att_ref[2 * j + h]
@@ -267,35 +263,35 @@
     hidden_ref[...] = hidden
     inverse = lax.rsqrt(jnp.mean(hidden * hidden, axis=-1, keepdims=True) + norm_eps)
     act = (hidden * inverse * gain_ref[...]).astype(bf16)
-    act_ref[...] = act
     send_ref[...] = dot(pick_ref[...], act).astype(bf16)
-    logits = dot(act, wr_ref[...])
-    raised = jnp.exp(logits - jnp.max(logits, axis=-1, keepdims=True))
-    probs_ref[...] = raised / jnp.sum(raised, axis=-1, keepdims=True)
-
-
-def middle(att, x, wo, gain, wr, pick):
+
+
+def middle(att, x, wo, gain, pick):
     return call(
         middle_kernel,
-        (
-            struct((TOK, D), bf16),
-            struct((TOK, D), f32),
-            struct((TOK, D), bf16),
-            struct((TOK, EXPERTS), f32),
-            struct((SLOTS, D), bf16),
-        ),
+        (struct((TOK, D), bf16), struct((TOK, D), f32), struct((SLOTS, D), bf16)),
         2 * TOK * D * (D + SLOTS),
         8e6,
         name="middle",
-    )(att, x, wo, gain.reshape(1, D), wr, pick)
-
-
-def expert_kernel(x_ref, top_ref, gu_ref, down_ref, back_ref, hidden_ref, mixed_ref, gg_ref):
-    ones = jnp.ones((8, F), bf16)
+    )(att, x, wo, gain.reshape(1, D), pick)
+
+
+def expert_kernel(
+    first_ref, x_ref, top_ref, gu_ref, down_ref, wr_ref, back_ref, hidden_ref, mixed_ref, gate_ref, logit_ref
+):
+    number = first_ref[0] + pl.program_id(0)
+    wr = wr_ref[...]
     for part in range(2):
         take = slice(8 * part, 8 * part + 8)
         rows = slice(384 * part, 384 * part + 384)
-        pre = dot(x_ref[take].reshape(384, D), gu_ref[...])
+        x = x_ref[take].reshape(384, D)
+        logits = dot(x, wr)
+        raised = jnp.exp(logits - jnp.max(logits, axis=-1, keepdims=True))
+        probs = raised / jnp.sum(raised, axis=-1, keepdims=True)
+        chosen = (lane_index(probs.shape) == number).astype(f32)
+        gate_value = jnp.sum(probs * chosen, axis=-1, keepdims=True)
+        gate_ref[rows] = gate_value
+        pre = dot(x, gu_ref[...])
         raw = branch_scale * dot_rows(top_ref[take].reshape(384, D), down_ref[...])
         gate = pre[:, :F]
         up = pre[:, F:]
@@ -303,17 +299,25 @@
         act = gate * sig
         hidden = (act * up).astype(bf16)
         hidden_ref[rows] = hidden
-        hi, lo = split2(hidden.astype(f32) * raw)
-        gg_ref[:, rows] = dot_rows(ones, hi) + dot_rows(ones, lo)
+        grad_gate = jnp.sum(hidden.astype(f32) * raw, axis=-1, keepdims=True)
+        grad_logits = (gate_value * grad_gate) * (chosen - probs)
+        logit_ref[rows] = grad_logits
+        raw = raw * gate_value
         mixed_gate = (raw * up * sig * (1.0 + gate * (1.0 - sig))).astype(bf16)
         mixed_up = (raw * act).astype(bf16)
         mixed_ref[rows, :F] = mixed_gate
         mixed_ref[rows, F:] = mixed_up
+        hi, lo = split2(grad_logits)
         back = dot_rows(mixed_gate, gu_ref[:, :F]) + dot_rows(mixed_up, gu_ref[:, F:])
+        back = back + dot_rows(hi, wr) + dot_rows(lo, wr)
         back_ref[take] = back.astype(bf16).reshape(8, CAP, D)
 
 
-def experts(x, top, gate_up, down):
+def owned(*shape):
+    return pl.BlockSpec((None, *shape), lambda n: (n, *([0] * len(shape))))
+
+
+def experts(first, x, top, gate_up, down, wr):
     per = pl.BlockSpec((16, None, CAP, D), lambda n: (0, n, 0, 0))
     return call(
         expert_kernel,
@@ -321,80 +325,71 @@
             struct((16, 2, CAP, D), bf16),
             struct((2, 768, F), bf16),
             struct((2, 768, D), bf16),
-            struct((2, 8, 768), f32),
+            struct((2, 768, 1), f32),
+            struct((2, 768, EXPERTS), f32),
         ),
         2 * SLOTS * D * 2560,
         2e7,
         grid=(2,),
         in_specs=[
+            pl.BlockSpec(memory_space=pltpu.SMEM),
             per,
             per,
-            pl.BlockSpec((None, D, D), lambda n: (n, 0, 0)),
-            pl.BlockSpec((None, F, D), lambda n: (n, 0, 0)),
+            owned(D, D),
+            owned(F, D),
+            pl.BlockSpec((D, EXPERTS), lambda n: (0, 0)),
         ],
-        out_specs=(
-            per,
-            pl.BlockSpec((None, 768, F), lambda n: (n, 0, 0)),
-            pl.BlockSpec((None, 768, D), lambda n: (n, 0, 0)),
-            pl.BlockSpec((None, 8, 768), lambda n: (n, 0, 0)),
-        ),
+        out_specs=(per, owned(768, F), owned(768, D), owned(768, 1), owned(768, EXPERTS)),
         name="experts",
-    )(x, top, gate_up, down)
-
-
-def expert_grads_kernel(x_ref, top_ref, gate_ref, hidden_ref, mixed_ref, down_ref, out_ref, dgu_ref, ddown_ref):
+    )(first, x, top, gate_up, down, wr)
+
+
+def expert_grads_kernel(
+    x_ref, top_ref, gate_ref, logit_ref, hidden_ref, mixed_ref, down_ref, out_ref, dgu_ref, ddown_ref, router_ref
+):
     hidden = hidden_ref[...]
     gate = gate_ref[...]
-    out_ref[...] = dot(hidden, down_ref[...]).astype(bf16).reshape(16, CAP, D)
+    x = x_ref[...].reshape(768, D)
+    out_ref[...] = (gate * dot(hidden, down_ref[...])).astype(bf16).reshape(16, CAP, D)
     top = (branch_scale * gate * top_ref[...].reshape(768, D).astype(f32)).astype(bf16)
     ddown_ref[...] = dot_down(hidden, top).astype(bf16)
-    mixed = (gate * mixed_ref[...].astype(f32)).astype(bf16)
-    dgu_ref[...] = dot_down(x_ref[...].reshape(768, D), mixed).astype(bf16)
-
-
-def expert_grads(x, top, gate, hidden, mixed, down):
+    dgu_ref[...] = dot_down(x, mixed_ref[...]).astype(bf16)
+    hi, lo = split2(logit_ref[...])
+    router_ref[...] = dot_down(x, hi) + dot_down(x, lo)
+
+
+def expert_grads(x, top, gate, logits, hidden, mixed, down):
     per = pl.BlockSpec((16, None, CAP, D), lambda n: (0, n, 0, 0))
     return call(
         expert_grads_kernel,
-        (struct((16, 2, CAP, D), bf16), struct((2, D, D), bf16), struct((2, F, D), bf16)),
+        (
+            struct((16, 2, CAP, D), bf16),
+            struct((2, D, D), bf16),
+            struct((2, F, D), bf16),
+            struct((2, D, EXPERTS), f32),
+        ),
         2 * SLOTS * D * 2048,
         2.4e7,
         grid=(2,),
-        in_specs=[
-            per,
-            per,
-            pl.BlockSpec((None, 768, 1), lambda n: (n, 0, 0)),
-            pl.BlockSpec((None, 768, F), lambda n: (n, 0, 0)),
-            pl.BlockSpec((None, 768, D), lambda n: (n, 0, 0)),
-            pl.BlockSpec((None, F, D), lambda n: (n, 0, 0)),
-        ],
-        out_specs=(
-            per,
-            pl.BlockSpec((None, D, D), lambda n: (n, 0, 0)),
-            pl.BlockSpec((None, F, D), lambda n: (n, 0, 0)),
-        ),
+        in_specs=[per, per, owned(768, 1), owned(768, EXPERTS), owned(768, F), owned(768, D), owned(F, D)],
+        out_specs=(per, owned(D, D), owned(F, D), owned(D, EXPERTS)),
         name="expert_grads",
-    )(x, top, gate, hidden, mixed, down)
+    )(x, top, gate, logits, hidden, mixed, down)
+
+
+def as_column(rows):
+    hi, lo = split2(rows)
+    ones = jnp.ones((TOK, LANES), bf16)
+    return dot_down(hi, ones) + dot_down(lo, ones)
 
 
 def turn_back_kernel(
-    back_ref, mix_ref, spot_ref, gg_ref, owner_ref, probs_ref, wr_ref, act_ref, hidden_ref, gain_ref, top_ref, wo_ref,
-    state_ref, attn_ref, send_ref, router_ref, norm_ref,
+    back_ref, spot_ref, hidden_ref, gain_ref, top_ref, wo_ref, state_ref, attn_ref, send_ref, norm_ref
 ):
-    both = dot(mix_ref[...], back_ref[...])
-    grad = both[:TOK] + both[TOK:]
-    hi, lo = split2(spot_ref[...].astype(f32) * gg_ref[...])
-    grad_probs = dot(hi, owner_ref[...]) + dot(lo, owner_ref[...])
-    probs = probs_ref[...]
-    logits = probs * (grad_probs - jnp.sum(probs * grad_probs, axis=-1, keepdims=True))
-    hi, lo = split2(logits)
-    grad = grad + dot_rows(hi, wr_ref[...]) + dot_rows(lo, wr_ref[...])
-    act = act_ref[...]
-    router_ref[...] = dot_down(act, hi) + dot_down(act, lo)
+    grad = dot(spot_ref[...], back_ref[...])
     hidden = hidden_ref[...]
     inverse = lax.rsqrt(jnp.mean(hidden * hidden, axis=-1, keepdims=True) + norm_eps)
     normed = hidden * inverse
-    norm_ref[...] = jnp.broadcast_to(jnp.sum(grad * normed, axis=0, keepdims=True), (8, D))
     scaled = grad * gain_ref[...]
     state = top_ref[...].astype(f32) + inverse * (scaled - normed * jnp.mean(scaled * normed, axis=-1, keepdims=True))
     state_ref[...] = state
@@ -404,27 +399,49 @@
     for j in range(PAIRS):
         for h in range(2):
             send_ref[2 * j + h] = attended[h * 64 : h * 64 + 64, j * LANES : (j + 1) * LANES]
-
-
-def turn_back(back, mix, spot, gg, owner, probs, wr, act, hidden, gain, top, wo):
+    norm_ref[...] = as_column(grad * normed)
+
+
+def turn_back(back, spot, hidden, gain, top, wo):
     return call(
         turn_back_kernel,
         (
             struct((TOK, D), f32),
             struct((TOK, D), bf16),
             struct((16, TOK // 2, LANES), bf16),
-            struct((D, EXPERTS), f32),
-            struct((8, D), f32),
+            struct((D, LANES), f32),
         ),
         2 * 256 * D * (D + SLOTS),
         8e6,
         name="turn_back",
-    )(back, mix, spot, gg, owner, probs, wr, act, hidden, gain.reshape(1, D), top, wo)
+    )(back, spot, hidden, gain.reshape(1, D), top, wo)
+
+
+def core_half(core):
+    return pl.ds(pl.multiple_of(core * 512, 512), 512)
+
+
+def early_kernel(core_ref, attended_ref, attn_ref, extra_ref, mine_ref, other_ref):
+    core = core_ref[0]
+    for which, out in ((core, mine_ref), (1 - core, other_ref)):
+        half = core_half(which)
+        out[:, :D] = dot_down(attended_ref[:, half], attn_ref[...]).astype(bf16)
+        out[:, D:] = extra_ref[half, :]
+
+
+def early_terms(core, attended, attn, extra):
+    smem = pl.BlockSpec(memory_space=pltpu.SMEM)
+    vmem = pl.BlockSpec(memory_space=pltpu.VMEM)
+    half = struct((512, D + LANES), bf16)
+    return call(
+        early_kernel, (half, half), 2 * TOK * D * D, 3e6, in_specs=[smem] + [vmem] * 3, out_specs=(vmem, vmem),
+        name="early",
+    )(core, attended, attn, extra)
 
 
 def finish_kernel(
-    dq_ref, dkv_ref, cos_ref, sin_ref, x_ref, gain_ref, wq_ref, wk_ref, wv_ref, state_ref, act_ref,
-    out_ref, norm_ref, dw_ref, flat_ref,
+    core_ref, dq_ref, dkv_ref, cos_ref, sin_ref, x_ref, gain_ref, wq_ref, wk_ref, wv_ref, state_ref, act_ref,
+    out_ref, mine_ref, other_ref, flat_ref, product_ref,
 ):
     cos = cos_ref[...]
     sin = sin_ref[...]
@@ -446,27 +463,75 @@
         v = jnp.where(left, pltpu.roll(even, HEAD_DIM, 1), odd)
         flat_ref[:, D + b * LANES : D + (b + 1) * LANES] = back(k).astype(bf16)
         flat_ref[:, D + 512 + b * LANES : D + 512 + (b + 1) * LANES] = v.astype(bf16)
-    dw_ref[...] = dot_down(act_ref[...], flat_ref[...]).astype(bf16)
     grad = dot_rows(flat_ref[:, :D], wq_ref[...])
     grad = grad + dot_rows(flat_ref[:, D : D + 512], wk_ref[...])
     grad = grad + dot_rows(flat_ref[:, D + 512 :], wv_ref[...])
     x = x_ref[...].astype(f32)
     inverse = lax.rsqrt(jnp.mean(x * x, axis=-1, keepdims=True) + norm_eps)
     normed = x * inverse
-    norm_ref[...] = jnp.broadcast_to(jnp.sum(grad * normed, axis=0, keepdims=True), (8, D))
+    product_ref[...] = grad * normed
     scaled = grad * gain_ref[...]
     out_ref[...] = state_ref[...] + inverse * (scaled - normed * jnp.mean(scaled * normed, axis=-1, keepdims=True))
-
-
-def finish(dq, dkv, cos, sin, x, gain, wq, wk, wv, state, act):
+    core = core_ref[0]
+    for which, out in ((1 - core, other_ref), (core, mine_ref)):
+        half = core_half(which)
+        out[:, :2048] = dot_down(act_ref[:, half], flat_ref[...]).astype(bf16)
+        out[:, 2048:] = as_column(product_ref[:, half]).astype(bf16)
+
+
+def finish(core, dq, dkv, cos, sin, x, gain, wq, wk, wv, state, act):
+    smem = pl.BlockSpec(memory_space=pltpu.SMEM)
+    vmem = pl.BlockSpec(memory_space=pltpu.VMEM)
+    half = struct((512, 2048 + LANES), bf16)
     return call(
         finish_kernel,
-        (struct((TOK, D), f32), struct((8, D), f32), struct((D, 2048), bf16)),
+        (struct((TOK, D), f32), half, half),
         2 * 2 * 256 * D * 2048,
         1.2e7,
-        scratch_shapes=[pltpu.VMEM((TOK, 2048), bf16)],
+        in_specs=[smem] + [vmem] * 11,
+        out_specs=(vmem, vmem, vmem),
+        scratch_shapes=[pltpu.VMEM((TOK, 2048), bf16), pltpu.VMEM((TOK, D), f32)],
         name="finish",
-    )(dq, dkv, cos, sin, x, gain.reshape(1, D), wq, wk, wv, state, act)
+    )(core, dq, dkv, cos, sin, x, gain.reshape(1, D), wq, wk, wv, state, act)
+
+
+def assemble_kernel(
+    core_ref, late_ref, late_other_ref, early_ref, early_other_ref, q_ref, k_ref, v_ref, o_ref, late_extra, early_extra
+):
+    core = core_ref[0]
+    for which, late, early in ((core, late_ref, early_ref), (1 - core, late_other_ref, early_other_ref)):
+        half = core_half(which)
+        q_ref[half, :] = late[:, :D].astype(f32)
+        k_ref[half, :] = late[:, D : D + 512].astype(f32)
+        v_ref[half, :] = late[:, D + 512 : 2048].astype(f32)
+        late_extra[half, :] = late[:, 2048:].astype(f32)
+        o_ref[half, :] = early[:, :D].astype(f32)
+        early_extra[half, :] = early[:, D:].astype(f32)
+
+
+def assemble(core, late, late_other, early, early_other):
+    smem = pl.BlockSpec(memory_space=pltpu.SMEM)
+    vmem = pl.BlockSpec(memory_space=pltpu.VMEM)
+    return call(
+        assemble_kernel,
+        (
+            struct((D, D), f32),
+            struct((D, 512), f32),
+            struct((D, 512), f32),
+            struct((D, D), f32),
+            struct((D, LANES), f32),
+            struct((D, LANES), f32),
+        ),
+        1e6,
+        1.9e7,
+        in_specs=[smem] + [vmem] * 4,
+        out_specs=(vmem,) * 6,
+        name="assemble",
+    )(core, late, late_other, early, early_other)
+
+
+def after(x, *earlier):
+    return lax.optimization_barrier((x, *earlier))[0]
 
 
 def to_owners(x):
@@ -481,22 +546,31 @@
     return lax.ppermute(x, "dp", [(0, 1), (1, 0)])
 
 
-def sum_everywhere(x):
-    rows, columns = x.shape
-    core = lax.axis_index("dp")
-    parts = x.reshape(2, rows // 2, columns)
-    mine = lax.dynamic_index_in_dim(parts, core, 0, False)
-    other = lax.dynamic_index_in_dim(parts, 1 - core, 0, False)
-    half = (mine.astype(f32) + swap_cores(other).astype(f32)).astype(bf16)
-    pieces = lax.all_to_all(
-        half.reshape(64, rows // 128, columns), ("expert", "context"), split_axis=0, concat_axis=0, tiled=True
-    )
-    total = jnp.sum(pieces.astype(f32), 0).astype(bf16)
-    half = lax.all_gather(total, ("expert", "context"), axis=0, tiled=True)
-    other = swap_cores(half)
-    low = jnp.where(core == 0, half, other)
-    high = jnp.where(core == 0, other, half)
-    return jnp.concatenate([low, high], 0)
+def shift(x, by):
+    return lax.ppermute(x, "context", [(i, (i + by) % 4) for i in range(4)])
+
+
+def sum_context(x, context):
+    parts = x.reshape(4, x.shape[0] // 4, x.shape[1])
+    pick = lambda by: lax.dynamic_index_in_dim(parts, (context + by) % 4, 0, False)
+    got = [shift(pick(by), by) for by in (1, 2, 3)]
+    total = pick(0).astype(f32)
+    for piece in got:
+        total = total + piece.astype(f32)
+    return total.astype(bf16)
+
+
+def gather_context(x, context):
+    got = [x] + [shift(x, by) for by in (1, 2, 3)]
+    rows = x.shape[0]
+    wide = jnp.concatenate([got[i] for i in (3, 2, 1, 0, 3, 2, 1)], 0)
+    return lax.dynamic_slice_in_dim(wide, (3 - context) * rows, 4 * rows, 0)
+
+
+def reduce_half(half, context):
+    rows, columns = half.shape
+    pieces = to_owners(half.reshape(16, rows // 16, columns))
+    return sum_context(jnp.sum(pieces.astype(f32), 0).astype(bf16), context)
 
 
 def local(
@@ -524,79 +598,80 @@
     spot = (dot_rows(marked, owner16) == slot_number[None, :].astype(f32)).astype(bf16)
     pick = (dot_rows(owner16, marked) == slot_number[:, None].astype(f32)).astype(bf16)
 
+    core = lax.axis_index("dp").astype(jnp.int32).reshape(1)
     act1, q_send, kv_send = project(x, norm1_gain, w_query, w_key, w_value, cos, sin)
-    kv_block = to_owners(kv_send).reshape(BLOCK, LANES)
-    kv = lax.all_gather(kv_block, "context", axis=0, tiled=True)
-    q_own = to_owners(q_send).reshape(2, CHUNK, LANES)
+    kv_block = to_owners(kv_send)
+    kv = lax.all_gather(kv_block.reshape(BLOCK, LANES), "context", axis=0, tiled=True)
+    q_own = to_owners(after(q_send, kv_block)).reshape(2, CHUNK, LANES)
     q = jnp.stack([q_own[0], mirror(q_own[1])], 0)
 
     gate_up = lax.all_gather(w_gate_up, ("context", "dp"), axis=1, tiled=True)
     down = lax.all_gather(w_down, ("context", "dp"), axis=1, tiled=True)
-    top_rows = to_owners(dot(pick, top).astype(bf16).reshape(16, 2, CAP, D))
+    top_send = dot(pick, top).astype(bf16).reshape(16, 2, CAP, D)
+    top_rows = to_owners(after(top_send, q_own))
 
     seat = jnp.stack([context, expert % 2]).astype(jnp.int32)
     o, o_low, lse = attend_forward(seat, q, kv)
+    o_low = after(o_low, top_rows)
     o_own = jnp.stack([o_low[0], mirror(o_low[1])], 0)
     att = to_owners(o_own.reshape(16, TOK // 2, LANES))
 
-    attended, hidden, act2, probs, send = middle(att, x, w_out, norm2_gain, w_router, pick)
+    attended, hidden, send = middle(att, x, w_out, norm2_gain, pick)
     rows = to_owners(send.reshape(16, 2, CAP, D))
-
-    hi, lo = split2(probs)
-    mix = jnp.concatenate([dot(hi, owner16.T).astype(bf16) * spot, dot(lo, owner16.T).astype(bf16) * spot], 0)
-    gate_slots = jnp.sum(mix[:TOK].astype(f32) + mix[TOK:].astype(f32), 0).reshape(16, 2, CAP)
-    gates = to_owners(gate_slots).transpose(1, 0, 2).reshape(2, 768, 1)
-
-    grad_rows, expert_hidden, mixed, gg = experts(rows, top_rows, gate_up, down)
-    back = to_owners(grad_rows).reshape(SLOTS, D)
-    gg_back = to_owners(gg[:, 0].reshape(2, 16, CAP).transpose(1, 0, 2)).reshape(1, SLOTS)
-    out_rows, dgu, ddown = expert_grads(rows, top_rows, gates, expert_hidden, mixed, down)
-
-    state, attn, do_send, router_grad, norm2_grad = turn_back(
-        back, mix, spot, gg_back, owner16, probs, w_router, act2, hidden, norm2_gain, top, w_out
+    first = (2 * expert).astype(jnp.int32).reshape(1)
+    grad_rows, expert_hidden, mixed, gates, logits = experts(first, rows, top_rows, gate_up, down, w_router)
+    back = to_owners(grad_rows)
+    out_rows, dgu, ddown, router_grad = expert_grads(rows, top_rows, gates, logits, expert_hidden, mixed, down)
+    back = after(back, dgu)
+    grad_gate_up = lax.psum_scatter(dgu, ("context", "dp"), scatter_dimension=1, tiled=True)
+    grad_down = lax.psum_scatter(ddown, ("context", "dp"), scatter_dimension=1, tiled=True)
+
+    state, attn, do_send, norm2_column = turn_back(
+        back.reshape(SLOTS, D), spot, hidden, norm2_gain, top, w_out
     )
     do_own = to_owners(do_send).reshape(2, CHUNK, LANES)
     do = jnp.stack([do_own[0], mirror(do_own[1])], 0)
 
-    grad_gate_up = lax.psum_scatter(dgu, ("context", "dp"), scatter_dimension=1, tiled=True).astype(f32)
-    grad_down = lax.psum_scatter(ddown, ("context", "dp"), scatter_dimension=1, tiled=True).astype(f32)
-
-    out_grad = dot_down(attended, attn).astype(bf16)
-    extra = jnp.concatenate(
-        [router_grad.reshape(32, D), norm2_grad[:1], jnp.zeros((95, D), f32)], 0
-    ).astype(bf16)
-    early = sum_everywhere(jnp.concatenate([out_grad, extra], 0))
+    returned = to_owners(after(out_rows, do))
+    router_wide = jnp.pad(router_grad[0] + router_grad[1], ((0, 0), (0, LANES - EXPERTS)))
+    extra = jnp.where(lane_index((D, LANES)) < EXPERTS, router_wide, norm2_column).astype(bf16)
+    early_mine, early_other = early_terms(core, attended, attn, extra)
+    early_half = (early_mine.astype(f32) + swap_cores(early_other).astype(f32)).astype(bf16)
 
     dq, dkv = attend_backward(seat, q, do, o, lse, kv)
+    dq, dkv, returned, grad_gate_up, grad_down = lax.optimization_barrier(
+        (dq, dkv, returned, grad_gate_up, grad_down)
+    )
     dq_own = jnp.stack([dq[0], mirror(dq[1])], 0).reshape(16, TOK // 2, LANES)
     dq_back = to_owners(dq_own)
     dkv_own = lax.psum_scatter(dkv, "context", scatter_dimension=0, tiled=True)
-    dkv_back = to_owners(dkv_own.reshape(16, TOK, LANES))
-
-    grad_input, norm1_grad, dw = finish(
-        dq_back, dkv_back, cos, sin, x, norm1_gain, w_query, w_key, w_value, state, act1
+    early_piece = reduce_half(after(early_half, dq_back), context)
+    dkv_back = to_owners(after(dkv_own, early_piece).reshape(16, TOK, LANES))
+    early_block = gather_context(early_piece, context)
+    early = lax.all_gather(early_block, "expert", axis=0, tiled=True)
+
+    grad_input, late_mine, late_other = finish(
+        core, dq_back, dkv_back, cos, sin, x, norm1_gain, w_query, w_key, w_value, state, act1
     )
-
-    returned = to_owners(out_rows).reshape(SLOTS, D)
-    mixture = dot(mix, returned)
-    block_out = hidden + branch_scale * (mixture[:TOK] + mixture[TOK:])
-
-    last = jnp.concatenate([norm1_grad[:1], jnp.zeros((127, D), f32)], 0).astype(bf16)
-    last = jnp.concatenate([last, jnp.zeros((128, D), bf16)], 1)
-    late = sum_everywhere(jnp.concatenate([dw, last], 0))
-    dw_sum = late[:D].astype(f32)
+    late_half = (late_mine.astype(f32) + swap_cores(late_other).astype(f32)).astype(bf16)
+    late_block = gather_context(reduce_half(late_half, context), context)
+    late = to_owners(jnp.broadcast_to(late_block[None], (16, *late_block.shape))).reshape(512, 2048 + LANES)
+
+    mixture = dot(spot, returned.reshape(SLOTS, D))
+    block_out = hidden + branch_scale * mixture
+    dwq, dwk, dwv, dwo, late_extra, early_extra = assemble(core, late, swap_cores(late), early, swap_cores(early))
     return (
         block_out.reshape(1, 1, TOK, D),
         grad_input.reshape(1, 1, TOK, D),
-        late[D, :D].astype(f32),
-        early[D + 32].astype(f32),
-        dw_sum[:, :D],
-        dw_sum[:, D : D + 512],
-        dw_sum[:, D + 512 :],
-        early[:D].astype(f32),
-        early[D : D + 32].astype(f32).reshape(D, EXPERTS),
-        grad_gate_up,
-        grad_down,
+        late_extra[:, 0],
+        early_extra[:, EXPERTS],
+        dwq,
+        dwk,
+        dwv,
+        dwo,
+        early_extra[:, :EXPERTS],
+        grad_gate_up.astype(f32),
+        grad_down.astype(f32),
     )
 
 

time: 751 us -> 565 us (0.75); the launches traced: 740 us -> 564 us
  blocking collectives: 169 us -> 48.7 us
  waiting for transfers between devices: 308 us -> 225 us
  starting transfers between devices: 51.2 us -> 88.8 us
  Pallas kernels: 109 us -> 136 us
  local copies, waits for them, and re-layouts: 40.9 us -> 21.4 us
  other arithmetic: 35.2 us -> 24.1 us
    all_to_all x2 -> x0, blocking collectives: 95.1 us -> none  [sum_everywhere(): lax.all_to_all(half.reshape(64, rows // 128, columns), ('expert', 'contex...]
    all_gather x3 -> x2, waiting for transfers between devices: 88.9 us -> 27 us  [the longest x1 23 us: local(): early = lax.all_gather(early_block, 'expert', axis=0, tiled=True)]
    all_to_all x7 -> x10, waiting for transfers between devices: 115 us -> 155 us  [to_owners(): return lax.all_to_all(x, 'expert', split_axis=0, concat_axis=0, tiled=True)]
    reduce_scatter x1, waiting for transfers between devices: 38.2 us -> 0.01 us  [local(): lax.psum_scatter(dgu, ('context', 'dp'), scatter_dimension=1, tiled=True)]
    all_to_all x5 -> x3, blocking collectives: 73.6 us -> 48.7 us  [to_owners(): return lax.all_to_all(x, 'expert', split_axis=0, concat_axis=0, tiled=True)]
    reduce_scatter x1, waiting for transfers between devices: 23.8 us -> 0.01 us  [local(): lax.psum_scatter(ddown, ('context', 'dp'), scatter_dimension=1, tiled=True)]
    reduce_scatter x1, waiting for transfers between devices: 15 us -> 0.01 us  [local(): dkv_own = lax.psum_scatter(dkv, 'context', scatter_dimension=0, tiled=True)]
    all_to_all x7 -> x10, starting transfers between devices: 36.9 us -> 51.8 us  [to_owners(): return lax.all_to_all(x, 'expert', split_axis=0, concat_axis=0, tiled=True)]
  transfers between devices with their start and end apart: 23 -> 37, of which waited for: 17 -> 24; matrix products, arithmetic and copies ran while one was open for 8% -> 6% of each run, Pallas kernels for 6% -> 15%
where the time goes in v2:
time: 565 us; the launch traced here: 564 us
  waiting for transfers between devices  225 us (40%)
  Pallas kernels  136 us (24%)
  starting transfers between devices  88.8 us (16%)
  blocking collectives  48.7 us (9%)
  other arithmetic  24.1 us (4%)
  local copies, waits for them, and re-layouts  21.4 us (4%)
  between operations  14.7 us (3%)
    all_to_all x10, waiting for transfers between devices, to_owners(): return lax.all_to_all(x, 'expert', split_axis=0, concat_axis=0, tiled=True)  155 us
    all_to_all x10, starting transfers between devices, to_owners(): return lax.all_to_all(x, 'expert', split_axis=0, concat_axis=0, tiled=True)  51.8 us
    all_to_all x3, blocking collectives, to_owners(): return lax.all_to_all(x, 'expert', split_axis=0, concat_axis=0, tiled=True)  48.7 us
    pallas_call x1, Pallas kernels, attend_forward(): call(forward_kernel, (struct((2, CHUNK, LANES), f32), struct((2, CHUNK, L...  37.4 us
    pallas_call x1, Pallas kernels, attend_backward(): call(backward_kernel, (struct((2, CHUNK, LANES), bf16), struct((rows, LAN...  31.5 us
    ppermute x4, waiting for transfers between devices, mirror(): return lax.ppermute(x, 'context', [(0, 3), (1, 2), (2, 1), (3, 0)])  26.1 us
    all_gather x1, waiting for transfers between devices, local(): early = lax.all_gather(early_block, 'expert', axis=0, tiled=True)  23 us
    ppermute x4, starting transfers between devices, swap_cores(): return lax.ppermute(x, 'dp', [(0, 1), (1, 0)])  20 us
  transfers between devices with their start and end apart: 37, of which 24 were waited for; matrix products, arithmetic and copies ran while one was open for 6% of the time, Pallas kernels for 15%

profile of v2, /device:TPU:1, one launch (start us, length us, event | category | flops | bytes accessed | tf_op | source)
XLA Modules:
  0.0 563.7 jit_solution(4360166433311278657)
XLA Ops:
  12.5 19.0 %all_to_all.65 = bf16[16,128,128]{2,1,0:T(8,128)(2,1)} all-to-all(bf16[16,128,128]{2,1,0:T(8,128)(2,1)} %get-tuple-element.58), channel_id=1, replica_groups=mesh['expert'=16,'context'=4,'dp'=2] {'expert'}, dimensions={0} | all-to-all | bytes 1048576 | tf_op jit(solution)/shard_map/all_to_all | solution.py:538
  64.8 37.4 %attend.1 = (f32[2,512,128]{2,1,0:T(8,128)}, bf16[2,512,128]{2,1,0:T(8,128)(2,1)}, f32[4,8,512]{2,1,0:T(8,128)}) custom-call(s32[2]{0:T(128)} %pad_add_fusion.place_ref, bf16[2,512,128]{2,1,0:T(8,128)(2,1)} %pad_maximum_fusion.q_ref, bf16[8192,128]{1,0:T(8,128)(2,1)} %all-gather.5.cloned.1.call-done.kv_ref), custom_call_target="tpu_custom_call" | custom-call | flops 20000000000 | bytes 4000000 | tf_op jit(solution)/shard_map/attend/pallas_call | solution.py:166
  103.5 8.8 %collective-permute-done.1 = bf16[512,128]{1,0:T(8,128)(2,1)S(1)} collective-permute-done((bf16[512,128]{1,0:T(8,128)(2,1)S(1)}, bf16[512,128]{1,0:T(8,128)(2,1)S(1)}, u32[]{:S(2)}, u32[]{:S(2)}) %collective-permute-start.1) | collective-permute-done | bytes 131104 | tf_op jit(solution)/shard_map/ppermute | solution.py:542
  113.0 6.7 %all-to-all-start.3 = ((bf16[16,64,128]{2,1,0:T(8,128)(2,1)}), bf16[16,64,128]{2,1,0:T(8,128)(2,1)}, u32[]{:S(2)}, u32[]{:S(2)}) async-start(bf16[16,64,128]{2,1,0:T(8,128)(2,1)} %bitcast.76), calls=%async_computation.3 | async-start | bytes 524288 | tf_op jit(solution)/shard_map/all_to_all | solution.py:538
  136.9 34.5 %all-to-all-done.4.x_ref = bf16[16,2,48,1024]{3,2,1,0:T(8,128)(2,1)S(1)} async-done(((bf16[16,2,48,1024]{3,2,1,0:T(8,128)(2,1)}), bf16[16,2,48,1024]{3,2,1,0:T(8,128)(2,1)S(1)}, u32[]{:S(2)}, u32[]{:S(2)}) %all-to-all-start.4) | async-done | bytes 3145760 | tf_op jit(solution)/shard_map/all_to_all | solution.py:538
  173.1 19.0 %experts.1 = (bf16[16,2,48,1024]{3,2,1,0:T(8,128)(2,1)}, bf16[2,768,512]{2,1,0:T(8,128)(2,1)}, bf16[2,768,1024]{2,1,0:T(8,128)(2,1)}, f32[2,768,1]{2,1,0:T(8,128)}, f32[2,768,32]{2,1,0:T(8,128)}) custom-call(s32[1]{0:T(128)} %bitcast.16.first_ref, bf16[16,2,48,1024]{3,2,1,0:T(8,128)(2,1)} %copy-done.2, bf16[16,2,48,1024]{3,2,1,0:T(8,128)(2,1)} %copy-done.1, ...), custom_call_target="tpu_custom_call" | custom-call | flops 8053063680 | bytes 20000000 | tf_op jit(solution)/shard_map/experts/pallas_call | solution.py:322
  192.1 14.3 %expert_grads.1 = (bf16[16,2,48,1024]{3,2,1,0:T(8,128)(2,1)}, bf16[2,1024,1024]{2,1,0:T(8,128)(2,1)}, bf16[2,512,1024]{2,1,0:T(8,128)(2,1)}, f32[2,1024,32]{2,1,0:T(8,128)}) custom-call(bf16[16,2,48,1024]{3,2,1,0:T(8,128)(2,1)} %copy-done.2, bf16[16,2,48,1024]{3,2,1,0:T(8,128)(2,1)} %copy-done.1, f32[2,768,1]{2,1,0:T(8,128)} %get-tuple-element.65.gate_ref, ...), custom_call_target="tpu_custom_call" | custom-call | flops 6442450944 | bytes 24000000 | tf_op jit(solution)/shard_map/expert_grads/pallas_call | solution.py:363
  206.4 8.6 %all-to-all-start.5 = ((bf16[16,2,48,1024]{3,2,1,0:T(8,128)(2,1)}), bf16[16,2,48,1024]{3,2,1,0:T(8,128)(2,1)S(1)}, u32[]{:S(2)}, u32[]{:S(2)}) async-start(bf16[16,2,48,1024]{3,2,1,0:T(8,128)(2,1)} %get-tuple-element.64), calls=%async_computation.5 | async-start | bytes 6291456 | tf_op jit(solution)/shard_map/all_to_all | solution.py:538
  215.6 35.2 %all-to-all-done.5 = bf16[16,2,48,1024]{3,2,1,0:T(8,128)(2,1)S(1)} async-done(((bf16[16,2,48,1024]{3,2,1,0:T(8,128)(2,1)}), bf16[16,2,48,1024]{3,2,1,0:T(8,128)(2,1)S(1)}, u32[]{:S(2)}, u32[]{:S(2)}) %all-to-all-start.5) | async-done | bytes 3145760 | tf_op jit(solution)/shard_map/all_to_all | solution.py:538
  252.5 5.6 turn_back.1
  258.1 16.6 %all_to_all.66 = bf16[16,64,128]{2,1,0:T(8,128)(2,1)S(1)} all-to-all(bf16[16,64,128]{2,1,0:T(8,128)(2,1)} %get-tuple-element.71), channel_id=1, replica_groups=mesh['expert'=16,'context'=4,'dp'=2] {'expert'}, dimensions={0} | all-to-all | bytes 524288 | tf_op jit(solution)/shard_map/all_to_all | solution.py:538
  286.4 31.5 %attend_back.1 = (bf16[2,512,128]{2,1,0:T(8,128)(2,1)}, bf16[8192,128]{1,0:T(8,128)(2,1)}) custom-call(s32[2]{0:T(128)} %pad_add_fusion.place_ref, bf16[2,512,128]{2,1,0:T(8,128)(2,1)} %pad_maximum_fusion.q_ref, bf16[2,512,128]{2,1,0:T(8,128)(2,1)} %pad_maximum_fusion.2.do_ref, f32[2,512,128]{2,1,0:T(8,128)} %get-tuple-element.72.o_ref, ...), custom_call_target="tpu_custom_call" | custom-call | flops 49999998976 | bytes 8000000 | tf_op jit(solution)/shard_map/attend_back/pallas_call | solution.py:240
  328.1 6.3 %collective-permute-start.4 = (bf16[512,1152]{1,0:T(8,128)(2,1)}, bf16[512,1152]{1,0:T(8,128)(2,1)}, u32[]{:S(2)}, u32[]{:S(2)}) collective-permute-start(bf16[512,1152]{1,0:T(8,128)(2,1)} %get-tuple-element.87), channel_id=1, source_target_pairs={{0,1},{1,0},{2,3},{3,2},{4,5},{5,4},{6,7},{7,6},{8,9},{9,8},{10,11... | collective-permute-start | bytes 3538952 | tf_op jit(solution)/shard_map/ppermute | solution.py:546
  335.9 7.1 %collective-permute-done.3 = bf16[512,128]{1,0:T(8,128)(2,1)S(1)} collective-permute-done((bf16[512,128]{1,0:T(8,128)(2,1)S(1)}, bf16[512,128]{1,0:T(8,128)(2,1)S(1)}, u32[]{:S(2)}, u32[]{:S(2)}) %collective-permute-start.3) | collective-permute-done | bytes 131104 | tf_op jit(solution)/shard_map/ppermute | solution.py:542
  360.7 16.3 %all-to-all-done.9 = bf16[16,32,1152]{2,1,0:T(8,128)(2,1)} async-done(((bf16[16,32,1152]{2,1,0:T(8,128)(2,1)}), bf16[16,32,1152]{2,1,0:T(8,128)(2,1)}, u32[]{:S(2)}, u32[]{:S(2)}) %all-to-all-start.9) | async-done | bytes 1179680 | tf_op jit(solution)/shard_map/all_to_all | solution.py:538
  387.2 13.2 %all_to_all.67.dkv_ref = bf16[16,128,128]{2,1,0:T(8,128)(2,1)} all-to-all(bf16[16,128,128]{2,1,0:T(8,128)(2,1)} %bitcast.82), channel_id=1, replica_groups=mesh['expert'=16,'context'=4,'dp'=2] {'expert'}, dimensions={0} | all-to-all | bytes 1048576 | tf_op jit(solution)/shard_map/all_to_all | solution.py:538
  400.4 7.8 %finish.1 = (f32[128,1024]{1,0:T(8,128)}, bf16[512,2176]{1,0:T(8,128)(2,1)}, bf16[512,2176]{1,0:T(8,128)(2,1)}) custom-call(s32[1]{0:T(128)} %bitcast.24.core_ref, bf16[16,64,128]{2,1,0:T(8,128)(2,1)} %all-to-all-done.8.dq_ref, bf16[16,128,128]{2,1,0:T(8,128)(2,1)} %all_to_all.67.dkv_ref, f32[128,128]{1,0:T(8,128)} %get-tuple-element.166.cos_ref, ...), custom_call_target="tpu_custom_call" | custom-call | flops 2147483648 | bytes 12000000 | tf_op jit(solution)/shard_map/finish/pallas_call | solution.py:486
  408.2 5.9 %collective-permute-start.8 = (bf16[512,2176]{1,0:T(8,128)(2,1)}, bf16[512,2176]{1,0:T(8,128)(2,1)S(1)}, u32[]{:S(2)}, u32[]{:S(2)}) collective-permute-start(bf16[512,2176]{1,0:T(8,128)(2,1)} %get-tuple-element.94), channel_id=1, source_target_pairs={{0,1},{1,0},{2,3},{3,2},{4,5},{5,4},{6,7},{7,6},{8,9},{9,8},{10,11... | collective-permute-start | bytes 6684680 | tf_op jit(solution)/shard_map/ppermute | solution.py:546
  429.8 27.1 %all-to-all-done.11 = bf16[16,32,2176]{2,1,0:T(8,128)(2,1)} async-done(((bf16[16,32,2176]{2,1,0:T(8,128)(2,1)}), bf16[16,32,2176]{2,1,0:T(8,128)(2,1)}, u32[]{:S(2)}, u32[]{:S(2)}) %all-to-all-start.11) | async-done | bytes 2228256 | tf_op jit(solution)/shard_map/all_to_all | solution.py:538
  472.9 6.1 %all-to-all-start.12 = ((bf16[16,32,2176]{2,1,0:T(8,128)(2,1)}), bf16[16,32,2176]{2,1,0:T(8,128)(2,1)}, u32[]{:S(2)}, u32[]{:S(2)}) async-start(bf16[16,32,2176]{2,1,0:T(8,128)(2,1)} %broadcast_in_dim.7), calls=%async_computation.15 | async-start | bytes 4456448 | tf_op jit(solution)/shard_map/all_to_all | solution.py:538
  480.5 24.8 %all-to-all-done.12 = bf16[16,32,2176]{2,1,0:T(8,128)(2,1)} async-done(((bf16[16,32,2176]{2,1,0:T(8,128)(2,1)}), bf16[16,32,2176]{2,1,0:T(8,128)(2,1)}, u32[]{:S(2)}, u32[]{:S(2)}) %all-to-all-start.12) | async-done | bytes 2228256 | tf_op jit(solution)/shard_map/all_to_all | solution.py:538
  505.3 6.2 %collective-permute-start.15 = (bf16[512,2176]{1,0:T(8,128)(2,1)}, bf16[512,2176]{1,0:T(8,128)(2,1)}, u32[]{:S(2)}, u32[]{:S(2)}) collective-permute-start(bf16[512,2176]{1,0:T(8,128)(2,1)} %bitcast.43.late_ref), channel_id=1, source_target_pairs={{0,1},{1,0},{2,3},{3,2},{4,5},{5,4},{6,7},{7,6},{8,9},{9,8},{10,11... | collective-permute-start | bytes 6684680 | tf_op jit(solution)/shard_map/ppermute | solution.py:546
  511.5 23.0 %all-gather.11.cloned.1.call-done.early_ref = bf16[512,1152]{1,0:T(8,128)(2,1)} async-done(((bf16[32,1152]{1,0:T(8,128)(2,1)}), bf16[512,1152]{1,0:T(8,128)(2,1)}) %all-gather.11.cloned.1.call-update) | async-done | bytes 1179664 | tf_op jit(solution)/shard_map/all_gather | solution.py:651
  542.3 8.7 %assemble.1 = (f32[1024,1024]{1,0:T(8,128)}, f32[1024,512]{1,0:T(8,128)}, f32[1024,512]{1,0:T(8,128)}, f32[1024,1024]{1,0:T(8,128)}, f32[1024,128]{1,0:T(8,128)}, /*index=5*/f32[1024,128]{1,0:T(8,128)}) custom-call(s32[1]{0:T(128)} %bitcast.24.core_ref, bf16[512,2176]{1,0:T(8,128)(2,1)} %bitcast.43.late_ref, ...), custom_call_target="tpu_custom_call" | custom-call | flops 1000000 | bytes 19000000 | tf_op jit(solution)/shard_map/assemble/pallas_call | solution.py:515
  (150 shorter events, 159.4 us)
Async XLA Ops:
  7.2 57.6 %all-gather.5.cloned.1.call-start = ((), (), s32[]{:S(2)}) async-start(), calls=%async_computation.16 | async-start | bytes 2621440 | tf_op jit(solution)/shard_map/all_gather | solution.py:604
  31.5 105.4 %all-gather.9.cloned.1.call-start = ((), (), s32[]{:S(2)}) async-start(), calls=%async_computation.18 | async-start | bytes 2359296 | tf_op jit(solution)/shard_map/all_gather | solution.py:609
  32.3 139.2 %all-gather.7.cloned.1.call-start = ((), (), s32[]{:S(2)}) async-start(), calls=%async_computation.17 | async-start | bytes 4718592 | tf_op jit(solution)/shard_map/all_gather | solution.py:608
  33.5 10.9 %all-to-all-start.1 = ((bf16[16,64,128]{2,1,0:T(8,128)(2,1)}), bf16[16,64,128]{2,1,0:T(8,128)(2,1)S(1)}, u32[]{:S(2)}, u32[]{:S(2)}) async-start(bf16[16,64,128]{2,1,0:T(8,128)(2,1)} %get-tuple-element.59), calls=%async_computation.1 | async-start | bytes 524288 | tf_op jit(solution)/shard_map/all_to_all | solution.py:538
  45.1 57.0 %all-to-all-start.2 = ((bf16[16,2,48,1024]{3,2,1,0:T(8,128)(2,1)}), bf16[16,2,48,1024]{3,2,1,0:T(8,128)(2,1)S(1)}, u32[]{:S(2)}, u32[]{:S(2)}) async-start(bf16[16,2,48,1024]{3,2,1,0:T(8,128)(2,1)} %bitcast.10), calls=%async_computation.2 | async-start | bytes 6291456 | tf_op jit(solution)/shard_map/all_to_all | solution.py:538
  50.5 8.7 %collective-permute-start = (bf16[512,128]{1,0:T(8,128)(2,1)}, bf16[512,128]{1,0:T(8,128)(2,1)}, u32[]{:S(2)}, u32[]{:S(2)}) collective-permute-start(bf16[512,128]{1,0:T(8,128)(2,1)} %bitcast.5), channel_id=1, source_target_pairs={{0,6},{2,4},{4,2},{6,0},{1,7},{3,5},{5,3},{7,1},{8,14},{10,12},{12... | collective-permute-start | bytes 393224 | tf_op jit(solution)/shard_map/ppermute | solution.py:542
  103.4 8.9 %collective-permute-start.1 = (bf16[512,128]{1,0:T(8,128)(2,1)S(1)}, bf16[512,128]{1,0:T(8,128)(2,1)S(1)}, u32[]{:S(2)}, u32[]{:S(2)}) collective-permute-start(bf16[512,128]{1,0:T(8,128)(2,1)S(1)} %get-tuple-element.152), channel_id=1, source_target_pairs={{0,6},{2,4},{4,2},{6,0},{1,7},{3,5},{5,3},{7,1},{8,14},{10,12},{12... | collective-permute-start | bytes 393224 | tf_op jit(solution)/shard_map/ppermute | solution.py:542
  113.0 14.1 %all-to-all-start.3 = ((bf16[16,64,128]{2,1,0:T(8,128)(2,1)}), bf16[16,64,128]{2,1,0:T(8,128)(2,1)}, u32[]{:S(2)}, u32[]{:S(2)}) async-start(bf16[16,64,128]{2,1,0:T(8,128)(2,1)} %bitcast.76), calls=%async_computation.3 | async-start | bytes 524288 | tf_op jit(solution)/shard_map/all_to_all | solution.py:538
  132.1 39.3 %all-to-all-start.4 = ((bf16[16,2,48,1024]{3,2,1,0:T(8,128)(2,1)}), bf16[16,2,48,1024]{3,2,1,0:T(8,128)(2,1)S(1)}, u32[]{:S(2)}, u32[]{:S(2)}) async-start(bf16[16,2,48,1024]{3,2,1,0:T(8,128)(2,1)} %bitcast.71), calls=%async_computation.4 | async-start | bytes 6291456 | tf_op jit(solution)/shard_map/all_to_all | solution.py:538
  136.0 181.8 %reduce-scatter.6.cloned.1.call-start = ((), (), s32[]{:S(2)}) async-start(), calls=%async_computation.20 | async-start | bytes 2359296 | tf_op jit(solution)/shard_map/reduce_scatter | solution.py:627
  206.4 44.5 %all-to-all-start.5 = ((bf16[16,2,48,1024]{3,2,1,0:T(8,128)(2,1)}), bf16[16,2,48,1024]{3,2,1,0:T(8,128)(2,1)S(1)}, u32[]{:S(2)}, u32[]{:S(2)}) async-start(bf16[16,2,48,1024]{3,2,1,0:T(8,128)(2,1)} %get-tuple-element.64), calls=%async_computation.5 | async-start | bytes 6291456 | tf_op jit(solution)/shard_map/all_to_all | solution.py:538
  215.0 106.7 %reduce-scatter.4.cloned.1.call-start = ((), (), s32[]{:S(2)}) async-start(), calls=%async_computation.19 | async-start | bytes 4718592 | tf_op jit(solution)/shard_map/reduce_scatter | solution.py:626
  280.6 41.1 %all-to-all-start.7 = ((bf16[16,2,48,1024]{3,2,1,0:T(8,128)(2,1)}), bf16[16,2,48,1024]{3,2,1,0:T(8,128)(2,1)S(1)}, u32[]{:S(2)}, u32[]{:S(2)}) async-start(bf16[16,2,48,1024]{3,2,1,0:T(8,128)(2,1)} %get-tuple-element.77), calls=%async_computation.7 | async-start | bytes 6291456 | tf_op jit(solution)/shard_map/all_to_all | solution.py:538
  285.9 101.3 %reduce-scatter.8.cloned.1.call-start = ((), (), s32[]{:S(2)}) async-start(), calls=%async_computation.21 | async-start | bytes 2621440 | tf_op jit(solution)/shard_map/reduce_scatter | solution.py:647
  328.1 20.7 %collective-permute-start.4 = (bf16[512,1152]{1,0:T(8,128)(2,1)}, bf16[512,1152]{1,0:T(8,128)(2,1)}, u32[]{:S(2)}, u32[]{:S(2)}) collective-permute-start(bf16[512,1152]{1,0:T(8,128)(2,1)} %get-tuple-element.87), channel_id=1, source_target_pairs={{0,1},{1,0},{2,3},{3,2},{4,5},{5,4},{6,7},{7,6},{8,9},{9,8},{10,11... | collective-permute-start | bytes 3538952 | tf_op jit(solution)/shard_map/ppermute | solution.py:546
  343.7 12.6 %all-to-all-start.8 = ((bf16[16,64,128]{2,1,0:T(8,128)(2,1)}), bf16[16,64,128]{2,1,0:T(8,128)(2,1)}, u32[]{:S(2)}, u32[]{:S(2)}) async-start(bf16[16,64,128]{2,1,0:T(8,128)(2,1)} %bitcast.75), calls=%async_computation.10 | async-start | bytes 524288 | tf_op jit(solution)/shard_map/all_to_all | solution.py:538
  356.3 20.8 %all-to-all-start.9 = ((bf16[16,32,1152]{2,1,0:T(8,128)(2,1)}), bf16[16,32,1152]{2,1,0:T(8,128)(2,1)}, u32[]{:S(2)}, u32[]{:S(2)}) async-start(bf16[16,32,1152]{2,1,0:T(8,128)(2,1)} %bitcast.70), calls=%async_computation.12 | async-start | bytes 2359296 | tf_op jit(solution)/shard_map/all_to_all | solution.py:538
  408.2 10.1 %collective-permute-start.8 = (bf16[512,2176]{1,0:T(8,128)(2,1)}, bf16[512,2176]{1,0:T(8,128)(2,1)S(1)}, u32[]{:S(2)}, u32[]{:S(2)}) collective-permute-start(bf16[512,2176]{1,0:T(8,128)(2,1)} %get-tuple-element.94), channel_id=1, source_target_pairs={{0,1},{1,0},{2,3},{3,2},{4,5},{5,4},{6,7},{7,6},{8,9},{9,8},{10,11... | collective-permute-start | bytes 6684680 | tf_op jit(solution)/shard_map/ppermute | solution.py:546
  421.9 35.0 %all-to-all-start.11 = ((bf16[16,32,2176]{2,1,0:T(8,128)(2,1)}), bf16[16,32,2176]{2,1,0:T(8,128)(2,1)}, u32[]{:S(2)}, u32[]{:S(2)}) async-start(bf16[16,32,2176]{2,1,0:T(8,128)(2,1)} %bitcast.69), calls=%async_computation.14 | async-start | bytes 4456448 | tf_op jit(solution)/shard_map/all_to_all | solution.py:538
  426.9 34.7 %collective-permute-start.17 = (bf16[8,1152]{1,0:T(8,128)(2,1)}, bf16[8,1152]{1,0:T(8,128)(2,1)S(1)}, u32[]{:S(2)}, u32[]{:S(2)}) collective-permute-start(bf16[8,1152]{1,0:T(8,128)(2,1)} %fusion.8), channel_id=1, source_target_pairs={{0,4},{2,6},{4,0},{6,2},{1,5},{3,7},{5,1},{7,3},{8,12},{10,14},{12... | collective-permute-start | bytes 55304 | tf_op jit(solution)/shard_map/ppermute | solution.py:550
  428.2 37.8 %collective-permute-start.18 = (bf16[8,1152]{1,0:T(8,128)(2,1)}, bf16[8,1152]{1,0:T(8,128)(2,1)S(1)}, u32[]{:S(2)}, u32[]{:S(2)}) collective-permute-start(bf16[8,1152]{1,0:T(8,128)(2,1)} %fusion.8), channel_id=1, source_target_pairs={{0,2},{2,4},{4,6},{6,0},{1,3},{3,5},{5,7},{7,1},{8,10},{10,12},{12... | collective-permute-start | bytes 55304 | tf_op jit(solution)/shard_map/ppermute | solution.py:550
  472.9 32.4 %all-to-all-start.12 = ((bf16[16,32,2176]{2,1,0:T(8,128)(2,1)}), bf16[16,32,2176]{2,1,0:T(8,128)(2,1)}, u32[]{:S(2)}, u32[]{:S(2)}) async-start(bf16[16,32,2176]{2,1,0:T(8,128)(2,1)} %broadcast_in_dim.7), calls=%async_computation.15 | async-start | bytes 4456448 | tf_op jit(solution)/shard_map/all_to_all | solution.py:538
  479.0 55.5 %all-gather.11.cloned.1.call-start = ((), (), s32[]{:S(2)}) async-start(), calls=%async_computation.22 | async-start | bytes 1253376 | tf_op jit(solution)/shard_map/all_gather | solution.py:651
  505.3 36.1 %collective-permute-start.15 = (bf16[512,2176]{1,0:T(8,128)(2,1)}, bf16[512,2176]{1,0:T(8,128)(2,1)}, u32[]{:S(2)}, u32[]{:S(2)}) collective-permute-start(bf16[512,2176]{1,0:T(8,128)(2,1)} %bitcast.43.late_ref), channel_id=1, source_target_pairs={{0,1},{1,0},{2,3},{3,2},{4,5},{5,4},{6,7},{7,6},{8,9},{9,8},{10,11... | collective-permute-start | bytes 6684680 | tf_op jit(solution)/shard_map/ppermute | solution.py:546
  (26 other events, 208.9 us)
Sparse Core Ops, SparseCore 0:
  31.6 33.1 all-gather.4
  66.5 24.9 all-gather.8
  93.1 34.9 all-gather.6
  206.5 35.1 reduce-scatter.5
  244.5 36.9 reduce-scatter.3
  321.9 37.2 reduce-scatter.7
  482.9 51.5 all-gather.10

commit v3 on v2

--- a/solution.py
+++ b/solution.py
@@ -113,10 +113,22 @@
     return jnp.where(left, q, 0.0).astype(bf16)
 
 
-def forward_kernel(place_ref, q_ref, kv_ref, o_ref, low_ref, lse_ref, qm_ref, top_ref, acc_ref):
+def forward_kernel(
+    place_ref, q_ref, own_ref, left_ref, far_a_ref, far_b_ref, right_ref,
+    o_ref, low_ref, lse_ref, kv_ref, qm_ref, top_ref, acc_ref,
+):
     tile = 1024
     context = place_ref[0]
     half = place_ref[1]
+
+    def block(back):
+        return pl.multiple_of(lax.rem(context + 4 - back, 4) * BLOCK, BLOCK)
+
+    kv_ref[pl.ds(block(0), BLOCK), :] = own_ref[...]
+    kv_ref[pl.ds(block(1), BLOCK), :] = left_ref[...]
+    kv_ref[pl.ds(block(2), BLOCK // 2), :] = far_a_ref[...]
+    kv_ref[pl.ds(pl.multiple_of(block(2) + BLOCK // 2, BLOCK // 2), BLOCK // 2), :] = far_b_ref[...]
+    kv_ref[pl.ds(block(3), BLOCK), :] = right_ref[...]
     left = lane_index((CHUNK, LANES)) < HEAD_DIM
     left_keys = lane_index((tile, LANES)) < HEAD_DIM
     for chunk in range(2):
@@ -160,7 +172,7 @@
         low_ref[chunk] = o.astype(bf16)
 
 
-def attend_forward(place, q, kv):
+def attend_forward(place, q, kv_parts):
     smem = pl.BlockSpec(memory_space=pltpu.SMEM)
     vmem = pl.BlockSpec(memory_space=pltpu.VMEM)
     return call(
@@ -169,22 +181,25 @@
             struct((2, CHUNK, LANES), f32),
             struct((2, CHUNK, LANES), bf16),
             struct((4, 8, CHUNK), f32),
+            struct((4 * BLOCK, LANES), bf16),
         ),
         2e10,
         4e6,
-        in_specs=[smem, vmem, vmem],
-        out_specs=(vmem, vmem, vmem),
+        in_specs=[smem] + [vmem] * 6,
+        out_specs=(vmem,) * 4,
         scratch_shapes=[
             pltpu.VMEM((2, CHUNK, LANES), bf16),
             pltpu.VMEM((2, CHUNK, LANES), f32),
             pltpu.VMEM((2, CHUNK, LANES), f32),
         ],
         name="attend",
-    )(place, q, kv)
+    )(place, q, *kv_parts)
 
 
 def backward_kernel(
-    place_ref, q_ref, do_ref, o_ref, lse_ref, kv_ref, dq_ref, dkv_ref, qm_ref, dom_ref, row_ref, dqt_ref, acc_ref
+    place_ref, q_ref, do_ref, o_ref, lse_ref, kv_ref,
+    dq_ref, d0_ref, d1a_ref, d1b_ref, d2a_ref, d2b_ref, d3a_ref, d3b_ref,
+    qm_ref, dom_ref, row_ref, dqt_ref, acc_ref,
 ):
     tile = 512
     context = place_ref[0]
@@ -230,7 +245,11 @@
         step(whole + 1, tile)
         parts = [jnp.transpose(dqt_ref[head]) * score_scale for head in range(2)]
         dq_ref[chunk] = jnp.where(left, parts[0], pltpu.roll(parts[1], HEAD_DIM, 1)).astype(bf16)
-    dkv_ref[...] = acc_ref[...].astype(bf16)
+    d0_ref[...] = acc_ref[pl.ds(pl.multiple_of(context * BLOCK, BLOCK), BLOCK), :]
+    for back, first, second in ((1, d1a_ref, d1b_ref), (2, d2a_ref, d2b_ref), (3, d3a_ref, d3b_ref)):
+        start = pl.multiple_of(lax.rem(context + 4 - back, 4) * BLOCK, BLOCK)
+        first[...] = acc_ref[pl.ds(start, BLOCK // 2), :].astype(bf16)
+        second[...] = acc_ref[pl.ds(pl.multiple_of(start + BLOCK // 2, BLOCK // 2), BLOCK // 2), :].astype(bf16)
 
 
 def attend_backward(place, q, do, o, lse, kv):
@@ -239,11 +258,12 @@
     rows = kv.shape[0]
     return call(
         backward_kernel,
-        (struct((2, CHUNK, LANES), bf16), struct((rows, LANES), bf16)),
+        (struct((2, CHUNK, LANES), bf16), struct((BLOCK, LANES), f32))
+        + (struct((BLOCK // 2, LANES), bf16),) * 6,
         5e10,
         8e6,
         in_specs=[smem] + [vmem] * 5,
-        out_specs=(vmem, vmem),
+        out_specs=(vmem,) * 8,
         scratch_shapes=[
             pltpu.VMEM((2, CHUNK, LANES), bf16),
             pltpu.VMEM((2, CHUNK, LANES), bf16),
@@ -255,7 +275,7 @@
     )(place, q, do, o, lse, kv)
 
 
-def middle_kernel(att_ref, x_ref, wo_ref, gain_ref, pick_ref, attended_ref, hidden_ref, send_ref):
+def middle_kernel(att_ref, x_ref, wo_ref, gain_ref, pick_ref, hidden_ref, send_ref, attended_ref):
     for j in range(PAIRS):
         for h in range(2):
             attended_ref[h * 64 : h * 64 + 64, j * LANES : (j + 1) * LANES] = att_ref[2 * j + h]
@@ -269,15 +289,28 @@
 def middle(att, x, wo, gain, pick):
     return call(
         middle_kernel,
-        (struct((TOK, D), bf16), struct((TOK, D), f32), struct((SLOTS, D), bf16)),
+        (struct((TOK, D), f32), struct((SLOTS, D), bf16)),
         2 * TOK * D * (D + SLOTS),
         8e6,
+        scratch_shapes=[pltpu.VMEM((TOK, D), bf16)],
         name="middle",
     )(att, x, wo, gain.reshape(1, D), pick)
 
 
+def raw_kernel(top_ref, down_ref, raw_ref):
+    raw_ref[...] = branch_scale * dot_rows(top_ref[...].reshape(768, D), down_ref[...])
+
+
+def raw_grads(top, down):
+    per = pl.BlockSpec((16, None, CAP, D), lambda n: (0, n, 0, 0))
+    return call(
+        raw_kernel, struct((2, 768, F), f32), 2 * SLOTS * D * F, 8e6, grid=(2,), in_specs=[per, owned(F, D)],
+        out_specs=owned(768, F), name="raw",
+    )(top, down)
+
+
 def expert_kernel(
-    first_ref, x_ref, top_ref, gu_ref, down_ref, wr_ref, back_ref, hidden_ref, mixed_ref, gate_ref, logit_ref
+    first_ref, x_ref, raw_ref, gu_ref, wr_ref, back_ref, hidden_ref, mixed_ref, gate_ref, logit_ref
 ):
     number = first_ref[0] + pl.program_id(0)
     wr = wr_ref[...]
@@ -292,7 +325,7 @@
         gate_value = jnp.sum(probs * chosen, axis=-1, keepdims=True)
         gate_ref[rows] = gate_value
         pre = dot(x, gu_ref[...])
-        raw = branch_scale * dot_rows(top_ref[take].reshape(384, D), down_ref[...])
+        raw = raw_ref[rows]
         gate = pre[:, :F]
         up = pre[:, F:]
         sig = 1.0 / (1.0 + jnp.exp(-gate))
@@ -317,7 +350,7 @@
     return pl.BlockSpec((None, *shape), lambda n: (n, *([0] * len(shape))))
 
 
-def experts(first, x, top, gate_up, down, wr):
+def experts(first, x, raw, gate_up, wr):
     per = pl.BlockSpec((16, None, CAP, D), lambda n: (0, n, 0, 0))
     return call(
         expert_kernel,
@@ -334,14 +367,13 @@
         in_specs=[
             pl.BlockSpec(memory_space=pltpu.SMEM),
             per,
-            per,
+            owned(768, F),
             owned(D, D),
-            owned(F, D),
             pl.BlockSpec((D, EXPERTS), lambda n: (0, 0)),
         ],
         out_specs=(per, owned(768, F), owned(768, D), owned(768, 1), owned(768, EXPERTS)),
         name="experts",
-    )(first, x, top, gate_up, down, wr)
+    )(first, x, raw, gate_up, wr)
 
 
 def expert_grads_kernel(
@@ -355,7 +387,7 @@
     ddown_ref[...] = dot_down(hidden, top).astype(bf16)
     dgu_ref[...] = dot_down(x, mixed_ref[...]).astype(bf16)
     hi, lo = split2(logit_ref[...])
-    router_ref[...] = dot_down(x, hi) + dot_down(x, lo)
+    router_ref[...] = dot_down(hi, x) + dot_down(lo, x)
 
 
 def expert_grads(x, top, gate, logits, hidden, mixed, down):
@@ -366,21 +398,15 @@
             struct((16, 2, CAP, D), bf16),
             struct((2, D, D), bf16),
             struct((2, F, D), bf16),
-            struct((2, D, EXPERTS), f32),
+            struct((2, EXPERTS, D), f32),
         ),
         2 * SLOTS * D * 2048,
         2.4e7,
         grid=(2,),
         in_specs=[per, per, owned(768, 1), owned(768, EXPERTS), owned(768, F), owned(768, D), owned(F, D)],
-        out_specs=(per, owned(D, D), owned(F, D), owned(D, EXPERTS)),
+        out_specs=(per, owned(D, D), owned(F, D), owned(EXPERTS, D)),
         name="expert_grads",
     )(x, top, gate, logits, hidden, mixed, down)
-
-
-def as_column(rows):
-    hi, lo = split2(rows)
-    ones = jnp.ones((TOK, LANES), bf16)
-    return dot_down(hi, ones) + dot_down(lo, ones)
 
 
 def turn_back_kernel(
@@ -399,7 +425,7 @@
     for j in range(PAIRS):
         for h in range(2):
             send_ref[2 * j + h] = attended[h * 64 : h * 64 + 64, j * LANES : (j + 1) * LANES]
-    norm_ref[...] = as_column(grad * normed)
+    norm_ref[...] = jnp.broadcast_to(jnp.sum(grad * normed, axis=0, keepdims=True), (8, D))
 
 
 def turn_back(back, spot, hidden, gain, top, wo):
@@ -409,7 +435,7 @@
             struct((TOK, D), f32),
             struct((TOK, D), bf16),
             struct((16, TOK // 2, LANES), bf16),
-            struct((D, LANES), f32),
+            struct((8, D), f32),
         ),
         2 * 256 * D * (D + SLOTS),
         8e6,
@@ -417,99 +443,127 @@
     )(back, spot, hidden, gain.reshape(1, D), top, wo)
 
 
-def core_half(core):
-    return pl.ds(pl.multiple_of(core * 512, 512), 512)
-
-
-def early_kernel(core_ref, attended_ref, attn_ref, extra_ref, mine_ref, other_ref):
+def unturn(v, cos, sin, first):
+    scaled = v * sin
+    return v * cos + jnp.where(first, pltpu.roll(scaled, LANES - 32, 1), pltpu.roll(scaled, 32, 1))
+
+
+def head_kernel(
+    core_ref, act_ref, attn_ref, o_ref, dq_ref, mine_in, other_in, cos_ref, sin_ref, mine_ref, other_ref, grads_ref,
+    all_ref,
+):
+    rows = 1024
+    lane = lane_index((rows, LANES))
+    first = lane % HEAD_DIM < HEAD_DIM // 2
+    cos = cos_ref[...]
+    sin = sin_ref[...]
+    grads_ref[:, :LANES] = unturn(dq_ref[...].astype(f32), cos, sin, first).astype(bf16)
+    both = (mine_in[...] + other_in[...].astype(f32)).astype(bf16).astype(f32)
+    grads_ref[:, LANES:] = jnp.where(lane < HEAD_DIM, unturn(both, cos, sin, first), both).astype(bf16)
+    all_ref[:D] = dot_down(act_ref[...], grads_ref[...]).astype(bf16)
+    out = dot_down(o_ref[...], attn_ref[...]).astype(bf16)
+    for b in range(4):
+        all_ref[D + LANES * b : D + LANES * (b + 1)] = out[:, 256 * b : 256 * (b + 1)]
     core = core_ref[0]
-    for which, out in ((core, mine_ref), (1 - core, other_ref)):
-        half = core_half(which)
-        out[:, :D] = dot_down(attended_ref[:, half], attn_ref[...]).astype(bf16)
-        out[:, D:] = extra_ref[half, :]
-
-
-def early_terms(core, attended, attn, extra):
+    mine_ref[...] = all_ref[pl.ds(pl.multiple_of(core * 768, 768), 768), :]
+    other_ref[...] = all_ref[pl.ds(pl.multiple_of((1 - core) * 768, 768), 768), :]
+
+
+def head_grads(core, act, attn, o, dq, mine, other, cos, sin):
     smem = pl.BlockSpec(memory_space=pltpu.SMEM)
     vmem = pl.BlockSpec(memory_space=pltpu.VMEM)
-    half = struct((512, D + LANES), bf16)
-    return call(
-        early_kernel, (half, half), 2 * TOK * D * D, 3e6, in_specs=[smem] + [vmem] * 3, out_specs=(vmem, vmem),
-        name="early",
-    )(core, attended, attn, extra)
-
-
-def finish_kernel(
-    core_ref, dq_ref, dkv_ref, cos_ref, sin_ref, x_ref, gain_ref, wq_ref, wk_ref, wv_ref, state_ref, act_ref,
-    out_ref, mine_ref, other_ref, flat_ref, product_ref,
-):
-    cos = cos_ref[...]
-    sin = sin_ref[...]
-    lane = lane_index((TOK, LANES))
-    first = lane % HEAD_DIM < HEAD_DIM // 2
-    left = lane < HEAD_DIM
-
-    def back(v):
-        scaled = v * sin
-        return v * cos + jnp.where(first, pltpu.roll(scaled, LANES - 32, 1), pltpu.roll(scaled, 32, 1))
-
-    for j in range(PAIRS):
-        rows = jnp.concatenate([dq_ref[2 * j], dq_ref[2 * j + 1]], axis=0).astype(f32)
-        flat_ref[:, j * LANES : (j + 1) * LANES] = back(rows).astype(bf16)
-    for b in range(PAIRS // 2):
-        even = dkv_ref[4 * b].astype(f32) + dkv_ref[4 * b + 1].astype(f32)
-        odd = dkv_ref[4 * b + 2].astype(f32) + dkv_ref[4 * b + 3].astype(f32)
-        k = jnp.where(left, even, pltpu.roll(odd, HEAD_DIM, 1))
-        v = jnp.where(left, pltpu.roll(even, HEAD_DIM, 1), odd)
-        flat_ref[:, D + b * LANES : D + (b + 1) * LANES] = back(k).astype(bf16)
-        flat_ref[:, D + 512 + b * LANES : D + 512 + (b + 1) * LANES] = v.astype(bf16)
+    half = struct((768, 256), bf16)
+    return call(
+        head_kernel,
+        (half, half, struct((1024, 256), bf16)),
+        2 * 1024 * 1024 * 512,
+        8e6,
+        in_specs=[smem] + [vmem] * 8,
+        out_specs=(vmem,) * 3,
+        scratch_shapes=[pltpu.VMEM((1536, 256), bf16)],
+        name="head_grads",
+    )(core, act, attn, o, dq, mine, other, cos, sin)
+
+
+def finish_kernel(grads_ref, x_ref, gain_ref, wq_ref, wk_ref, wv_ref, state_ref, out_ref, flat_ref):
+    left = lane_index((TOK // 2, LANES)) < HEAD_DIM
+    for h in range(2):
+        rows = slice(64 * h, 64 * h + 64)
+        for j in range(PAIRS):
+            flat_ref[rows, j * LANES : (j + 1) * LANES] = grads_ref[2 * j + h, :, :LANES]
+        for b in range(PAIRS // 2):
+            even = grads_ref[4 * b + h, :, LANES:].astype(f32)
+            odd = grads_ref[4 * b + 2 + h, :, LANES:].astype(f32)
+            k = jnp.where(left, even, pltpu.roll(odd, HEAD_DIM, 1))
+            v = jnp.where(left, pltpu.roll(even, HEAD_DIM, 1), odd)
+            flat_ref[rows, D + b * LANES : D + (b + 1) * LANES] = k.astype(bf16)
+            flat_ref[rows, D + 512 + b * LANES : D + 512 + (b + 1) * LANES] = v.astype(bf16)
     grad = dot_rows(flat_ref[:, :D], wq_ref[...])
     grad = grad + dot_rows(flat_ref[:, D : D + 512], wk_ref[...])
     grad = grad + dot_rows(flat_ref[:, D + 512 :], wv_ref[...])
     x = x_ref[...].astype(f32)
     inverse = lax.rsqrt(jnp.mean(x * x, axis=-1, keepdims=True) + norm_eps)
     normed = x * inverse
-    product_ref[...] = grad * normed
     scaled = grad * gain_ref[...]
     out_ref[...] = state_ref[...] + inverse * (scaled - normed * jnp.mean(scaled * normed, axis=-1, keepdims=True))
-    core = core_ref[0]
-    for which, out in ((1 - core, other_ref), (core, mine_ref)):
-        half = core_half(which)
-        out[:, :2048] = dot_down(act_ref[:, half], flat_ref[...]).astype(bf16)
-        out[:, 2048:] = as_column(product_ref[:, half]).astype(bf16)
-
-
-def finish(core, dq, dkv, cos, sin, x, gain, wq, wk, wv, state, act):
-    smem = pl.BlockSpec(memory_space=pltpu.SMEM)
-    vmem = pl.BlockSpec(memory_space=pltpu.VMEM)
-    half = struct((512, 2048 + LANES), bf16)
+
+
+def finish(grads, x, gain, wq, wk, wv, state):
     return call(
         finish_kernel,
-        (struct((TOK, D), f32), half, half),
-        2 * 2 * 256 * D * 2048,
-        1.2e7,
-        in_specs=[smem] + [vmem] * 11,
-        out_specs=(vmem, vmem, vmem),
-        scratch_shapes=[pltpu.VMEM((TOK, 2048), bf16), pltpu.VMEM((TOK, D), f32)],
+        struct((TOK, D), f32),
+        2 * 256 * D * 2048,
+        8e6,
+        scratch_shapes=[pltpu.VMEM((TOK, 2048), bf16)],
         name="finish",
-    )(core, dq, dkv, cos, sin, x, gain.reshape(1, D), wq, wk, wv, state, act)
-
-
-def assemble_kernel(
-    core_ref, late_ref, late_other_ref, early_ref, early_other_ref, q_ref, k_ref, v_ref, o_ref, late_extra, early_extra
-):
-    core = core_ref[0]
-    for which, late, early in ((core, late_ref, early_ref), (1 - core, late_other_ref, early_other_ref)):
-        half = core_half(which)
-        q_ref[half, :] = late[:, :D].astype(f32)
-        k_ref[half, :] = late[:, D : D + 512].astype(f32)
-        v_ref[half, :] = late[:, D + 512 : 2048].astype(f32)
-        late_extra[half, :] = late[:, 2048:].astype(f32)
-        o_ref[half, :] = early[:, :D].astype(f32)
-        early_extra[half, :] = early[:, D:].astype(f32)
-
-
-def assemble(core, late, late_other, early, early_other):
+    )(grads, x, gain.reshape(1, D), wq, wk, wv, state)
+
+
+def assemble_kernel(core_ref, own_ref, other_ref, wq_ref, wk_ref, wv_ref, q_ref, k_ref, v_ref, o_ref, norm_ref):
+    left = lane_index((384, LANES)) < HEAD_DIM
+
+    def write(pieces):
+        for core in range(2):
+            piece = pieces[core]
+            for h in range(2):
+                start = 768 * core + 384 * h
+                count = min(384, max(0, D - start))
+                if count:
+                    rows = slice(start, start + count)
+                    total = jnp.zeros((count, LANES), f32)
+                    for j in range(PAIRS):
+                        lanes = slice(j * LANES, (j + 1) * LANES)
+                        value = piece[2 * j + h, :count, :LANES].astype(f32)
+                        q_ref[rows, lanes] = value
+                        total = total + value * wq_ref[rows, lanes].astype(f32)
+                    for b in range(PAIRS // 2):
+                        lanes = slice(b * LANES, (b + 1) * LANES)
+                        even = piece[4 * b + h, :count, LANES:].astype(f32)
+                        odd = piece[4 * b + 2 + h, :count, LANES:].astype(f32)
+                        k = jnp.where(left[:count], even, pltpu.roll(odd, HEAD_DIM, 1))
+                        v = jnp.where(left[:count], pltpu.roll(even, HEAD_DIM, 1), odd)
+                        k_ref[rows, lanes] = k
+                        v_ref[rows, lanes] = v
+                        total = total + k * wk_ref[rows, lanes].astype(f32) + v * wv_ref[rows, lanes].astype(f32)
+                    norm_ref[rows] = jnp.sum(total, axis=-1, keepdims=True)
+                for b in range(4):
+                    at = D + LANES * b - start
+                    if 0 <= at < 384:
+                        for j in range(PAIRS):
+                            o_ref[j * LANES : (j + 1) * LANES, 256 * b : 256 * (b + 1)] = piece[
+                                2 * j + h, at : at + LANES, :
+                            ].astype(f32)
+
+    @pl.when(core_ref[0] == 0)
+    def _():
+        write((own_ref, other_ref))
+
+    @pl.when(core_ref[0] == 1)
+    def _():
+        write((other_ref, own_ref))
+
+
+def assemble(core, own, other, wq, wk, wv):
     smem = pl.BlockSpec(memory_space=pltpu.SMEM)
     vmem = pl.BlockSpec(memory_space=pltpu.VMEM)
     return call(
@@ -519,15 +573,14 @@
             struct((D, 512), f32),
             struct((D, 512), f32),
             struct((D, D), f32),
-            struct((D, LANES), f32),
-            struct((D, LANES), f32),
+            struct((D, 1), f32),
         ),
         1e6,
-        1.9e7,
-        in_specs=[smem] + [vmem] * 4,
-        out_specs=(vmem,) * 6,
+        2.2e7,
+        in_specs=[smem] + [vmem] * 5,
+        out_specs=(vmem,) * 5,
         name="assemble",
-    )(core, late, late_other, early, early_other)
+    )(core, own, other, wq, wk, wv)
 
 
 def after(x, *earlier):
@@ -552,9 +605,8 @@
 
 def sum_context(x, context):
     parts = x.reshape(4, x.shape[0] // 4, x.shape[1])
-    pick = lambda by: lax.dynamic_index_in_dim(parts, (context + by) % 4, 0, False)
-    got = [shift(pick(by), by) for by in (1, 2, 3)]
-    total = pick(0).astype(f32)
+    got = [shift(pick(parts, (context + by) % 4), by) for by in (1, 2, 3)]
+    total = pick(parts, context).astype(f32)
     for piece in got:
         total = total + piece.astype(f32)
     return total.astype(bf16)
@@ -567,10 +619,19 @@
     return lax.dynamic_slice_in_dim(wide, (3 - context) * rows, 4 * rows, 0)
 
 
-def reduce_half(half, context):
-    rows, columns = half.shape
-    pieces = to_owners(half.reshape(16, rows // 16, columns))
-    return sum_context(jnp.sum(pieces.astype(f32), 0).astype(bf16), context)
+def swap_halves(x):
+    return lax.ppermute(x, "expert", [(i, i ^ 1) for i in range(16)])
+
+
+def pick(x, index, axis=0):
+    return lax.dynamic_index_in_dim(x, index, axis, False)
+
+
+def rope_tables(positions):
+    frequency = rope_base ** (-jnp.arange(0, HEAD_DIM, 2, dtype=f32) / HEAD_DIM)
+    angles = positions.astype(f32)[:, None] * frequency[None, :]
+    cos, sin = jnp.cos(angles), jnp.sin(angles)
+    return jnp.concatenate([cos] * 4, -1), jnp.concatenate([-sin, sin] * 2, -1)
 
 
 def local(
@@ -581,12 +642,11 @@
     x = layer_input[0, 0]
     top = grad_output[0, 0]
 
-    positions = context * BLOCK + expert * TOK + jnp.arange(TOK, dtype=jnp.int32)
-    frequency = rope_base ** (-jnp.arange(0, HEAD_DIM, 2, dtype=f32) / HEAD_DIM)
-    angles = positions.astype(f32)[:, None] * frequency[None, :]
-    cos, sin = jnp.cos(angles), jnp.sin(angles)
-    cos = jnp.concatenate([cos] * 4, -1)
-    sin = jnp.concatenate([-sin, sin] * 2, -1)
+    half = expert % 2
+
+    cos, sin = rope_tables(context * BLOCK + expert * TOK + jnp.arange(TOK, dtype=jnp.int32))
+    order = jnp.arange(1024, dtype=jnp.int32)
+    half_cos, half_sin = rope_tables(context * BLOCK + order + (order // 64) * 64 + half * 64)
 
     hits = jnp.sum((routes[0, 0][:, :, None] == jnp.arange(EXPERTS, dtype=jnp.int32)).astype(f32), 1)
     lower = np.tril(np.ones((TOK, TOK), np.float32), -1)
@@ -596,82 +656,112 @@
     slot_number = jnp.arange(SLOTS, dtype=jnp.int32) % CAP
     marked = jnp.where(hits > 0.5, place, 255.0).astype(bf16)
     spot = (dot_rows(marked, owner16) == slot_number[None, :].astype(f32)).astype(bf16)
-    pick = (dot_rows(owner16, marked) == slot_number[:, None].astype(f32)).astype(bf16)
-
-    core = lax.axis_index("dp").astype(jnp.int32).reshape(1)
+    selector = (dot_rows(owner16, marked) == slot_number[:, None].astype(f32)).astype(bf16)
+
+    core_index = lax.axis_index("dp")
+    core = core_index.astype(jnp.int32).reshape(1)
     act1, q_send, kv_send = project(x, norm1_gain, w_query, w_key, w_value, cos, sin)
-    kv_block = to_owners(kv_send)
-    kv = lax.all_gather(kv_block.reshape(BLOCK, LANES), "context", axis=0, tiled=True)
+    kv_block = to_owners(kv_send).reshape(BLOCK, LANES)
+    kv_left = shift(kv_block, 1)
+    kv_right = shift(kv_block, 3)
+    kv_far_a = shift(kv_left[: BLOCK // 2], 1)
+    kv_far_b = shift(kv_right[BLOCK // 2 :], 3)
     q_own = to_owners(after(q_send, kv_block)).reshape(2, CHUNK, LANES)
     q = jnp.stack([q_own[0], mirror(q_own[1])], 0)
 
-    gate_up = lax.all_gather(w_gate_up, ("context", "dp"), axis=1, tiled=True)
+    gate_up = lax.all_gather(after(w_gate_up, kv_far_a, kv_far_b), ("context", "dp"), axis=1, tiled=True)
     down = lax.all_gather(w_down, ("context", "dp"), axis=1, tiled=True)
-    top_send = dot(pick, top).astype(bf16).reshape(16, 2, CAP, D)
+    top_send = dot(selector, top).astype(bf16).reshape(16, 2, CAP, D)
     top_rows = to_owners(after(top_send, q_own))
 
-    seat = jnp.stack([context, expert % 2]).astype(jnp.int32)
-    o, o_low, lse = attend_forward(seat, q, kv)
+    seat = jnp.stack([context, half]).astype(jnp.int32)
+    o, o_low, lse, kv = attend_forward(seat, q, (kv_block, kv_left, kv_far_a, kv_far_b, kv_right))
     o_low = after(o_low, top_rows)
-    o_own = jnp.stack([o_low[0], mirror(o_low[1])], 0)
+    o_own = jnp.stack([o_low[0], mirror(o_low[1])], 0).reshape(1024, LANES)
     att = to_owners(o_own.reshape(16, TOK // 2, LANES))
 
-    attended, hidden, send = middle(att, x, w_out, norm2_gain, pick)
+    hidden, send = middle(att, x, w_out, norm2_gain, selector)
     rows = to_owners(send.reshape(16, 2, CAP, D))
+    raw = raw_grads(top_rows, down)
     first = (2 * expert).astype(jnp.int32).reshape(1)
-    grad_rows, expert_hidden, mixed, gates, logits = experts(first, rows, top_rows, gate_up, down, w_router)
-    back = to_owners(grad_rows)
+    act_send = jnp.broadcast_to(after(act1, rows).reshape(1, 2, 64, D), (8, 2, 64, D)).reshape(16, 64, D)
+    act_rows = to_owners(act_send).reshape(1024, D)
+    grad_rows, expert_hidden, mixed, gates, logits = experts(first, rows, raw, gate_up, w_router)
+    back = to_owners(after(grad_rows, act_rows))
     out_rows, dgu, ddown, router_grad = expert_grads(rows, top_rows, gates, logits, expert_hidden, mixed, down)
-    back = after(back, dgu)
-    grad_gate_up = lax.psum_scatter(dgu, ("context", "dp"), scatter_dimension=1, tiled=True)
-    grad_down = lax.psum_scatter(ddown, ("context", "dp"), scatter_dimension=1, tiled=True)
-
-    state, attn, do_send, norm2_column = turn_back(
-        back.reshape(SLOTS, D), spot, hidden, norm2_gain, top, w_out
-    )
+
+    state, attn, do_send, norm2_grad = turn_back(back.reshape(SLOTS, D), spot, hidden, norm2_gain, top, w_out)
     do_own = to_owners(do_send).reshape(2, CHUNK, LANES)
     do = jnp.stack([do_own[0], mirror(do_own[1])], 0)
-
-    returned = to_owners(after(out_rows, do))
-    router_wide = jnp.pad(router_grad[0] + router_grad[1], ((0, 0), (0, LANES - EXPERTS)))
-    extra = jnp.where(lane_index((D, LANES)) < EXPERTS, router_wide, norm2_column).astype(bf16)
-    early_mine, early_other = early_terms(core, attended, attn, extra)
-    early_half = (early_mine.astype(f32) + swap_cores(early_other).astype(f32)).astype(bf16)
-
-    dq, dkv = attend_backward(seat, q, do, o, lse, kv)
-    dq, dkv, returned, grad_gate_up, grad_down = lax.optimization_barrier(
-        (dq, dkv, returned, grad_gate_up, grad_down)
+    grad_gate_up = lax.psum_scatter(
+        after(dgu, do_own), ("context", "dp"), scatter_dimension=1, tiled=True
+    ).astype(f32)
+
+    returned = to_owners(after(out_rows, do_own))
+    small = jnp.concatenate([router_grad[0] + router_grad[1], norm2_grad, jnp.zeros((24, D), f32)], 0)
+    small = small.reshape(64, 4, 256).transpose(1, 0, 2).reshape(2, 128, 256).astype(bf16)
+
+    dq, d0, d1a, d1b, d2a, d2b, d3a, d3b = attend_backward(seat, q, do, o, lse, kv)
+    dq, d0, d1a, d1b, d2a, d2b, d3a, d3b, returned = lax.optimization_barrier(
+        (dq, d0, d1a, d1b, d2a, d2b, d3a, d3b, returned)
     )
-    dq_own = jnp.stack([dq[0], mirror(dq[1])], 0).reshape(16, TOK // 2, LANES)
-    dq_back = to_owners(dq_own)
-    dkv_own = lax.psum_scatter(dkv, "context", scatter_dimension=0, tiled=True)
-    early_piece = reduce_half(after(early_half, dq_back), context)
-    dkv_back = to_owners(after(dkv_own, early_piece).reshape(16, TOK, LANES))
-    early_block = gather_context(early_piece, context)
-    early = lax.all_gather(early_block, "expert", axis=0, tiled=True)
-
-    grad_input, late_mine, late_other = finish(
-        core, dq_back, dkv_back, cos, sin, x, norm1_gain, w_query, w_key, w_value, state, act1
+    block_out = hidden + branch_scale * dot(spot, returned.reshape(SLOTS, D))
+    attn_send = jnp.broadcast_to(after(attn, returned).reshape(1, 2, 64, D), (8, 2, 64, D)).reshape(16, 64, D)
+    attn_rows = to_owners(attn_send).reshape(1024, D)
+
+    far_a, far_b = shift(d2a, 1), shift(d2b, 3)
+    from_left_b, from_right_a = shift(d3b, 1), shift(d1a, 3)
+    dq_own = jnp.stack([dq[0], mirror(dq[1])], 0).reshape(1024, LANES)
+    from_left_a = shift((d3a.astype(f32) + far_a.astype(f32)).astype(bf16), 1)
+    from_right_b = shift((d1b.astype(f32) + far_b.astype(f32)).astype(bf16), 3)
+    from_left = jnp.stack([from_left_a, from_left_b], 0).reshape(16, 2, 64, LANES)
+    from_right = jnp.stack([from_right_a, from_right_b], 0).reshape(16, 2, 64, LANES)
+    pieces = (d0.reshape(16, 2, 64, LANES), from_left, from_right)
+    keep = sum(pick(piece, half, 1).astype(f32) for piece in pieces)
+    give = sum(pick(piece, 1 - half, 1).astype(f32) for piece in pieces).astype(bf16)
+    got = swap_halves(give)
+
+    small_other = swap_cores(pick(small, 1 - core_index))
+    small_half = (pick(small, core_index).astype(f32) + small_other.astype(f32)).astype(bf16)
+    small_piece = jnp.sum(to_owners(after(small_half, attn_rows).reshape(16, 8, 256)).astype(f32), 0).astype(bf16)
+    small_sum = small_piece.astype(f32)
+    for by in (1, 2, 3):
+        small_sum = small_sum + shift(small_piece, by).astype(f32)
+
+    mine, other, grads = head_grads(
+        core, act_rows, attn_rows, o_own, dq_own, keep.reshape(1024, LANES), got.reshape(1024, LANES), half_cos, half_sin
     )
-    late_half = (late_mine.astype(f32) + swap_cores(late_other).astype(f32)).astype(bf16)
-    late_block = gather_context(reduce_half(late_half, context), context)
-    late = to_owners(jnp.broadcast_to(late_block[None], (16, *late_block.shape))).reshape(512, 2048 + LANES)
-
-    mixture = dot(spot, returned.reshape(SLOTS, D))
-    block_out = hidden + branch_scale * mixture
-    dwq, dwk, dwv, dwo, late_extra, early_extra = assemble(core, late, swap_cores(late), early, swap_cores(early))
+    grads_back = to_owners(after(grads, small_piece).reshape(16, 64, 256))
+    grad_input = finish(grads_back, x, norm1_gain, w_query, w_key, w_value, state)
+    grad_down = lax.psum_scatter(
+        after(ddown, got), ("context", "dp"), scatter_dimension=1, tiled=True
+    ).astype(f32)
+
+    total = (mine.astype(f32) + swap_cores(other).astype(f32)).astype(bf16).reshape(2, 384, 256)
+    total = pick(total, half).astype(f32) + swap_halves(pick(total, 1 - half)).astype(f32)
+    block = gather_context(sum_context(total.astype(bf16), context), context)
+    block = jnp.concatenate([block, small_sum.astype(bf16), jnp.zeros((8, 256), bf16)], 0)
+    block, grad_input, block_out, grad_gate_up = lax.optimization_barrier(
+        (block, grad_input, block_out, grad_gate_up)
+    )
+    whole = to_owners(jnp.broadcast_to(block[None], (16, *block.shape)))
+    whole_other = swap_cores(whole)
+    dwq, dwk, dwv, dwo, norm1_sum = assemble(core, whole, whole_other, w_query, w_key, w_value)
+    smalls = jnp.stack([whole[:, 384:392], whole_other[:, 384:392]], 0).reshape(2, 128, 256)
+    smalls = jnp.concatenate([pick(smalls, core_index), pick(smalls, 1 - core_index)], 0)
+    smalls = smalls.reshape(4, 64, 256).transpose(1, 0, 2).reshape(64, D).astype(f32)
     return (
         block_out.reshape(1, 1, TOK, D),
         grad_input.reshape(1, 1, TOK, D),
-        late_extra[:, 0],
-        early_extra[:, EXPERTS],
+        norm1_sum[:, 0] / norm1_gain,
+        smalls[EXPERTS],
         dwq,
         dwk,
         dwv,
         dwo,
-        early_extra[:, :EXPERTS],
-        grad_gate_up.astype(f32),
-        grad_down.astype(f32),
+        smalls[:EXPERTS].T,
+        grad_gate_up,
+        grad_down,
     )
 
 

time: 565 us -> 484 us (0.86)
  the two profiles are of different devices: /device:TPU:1 before, /device:TPU:69 now
where the time goes in v3:
time: 484 us; the launch traced here: 474 us
  starting transfers between devices  130 us (27%)
  Pallas kernels  127 us (26%)
  waiting for transfers between devices  83 us (17%)
  blocking collectives  67.6 us (14%)
  other arithmetic  24.6 us (5%)
  local copies, waits for them, and re-layouts  22 us (5%)
  between operations  14.7 us (3%)
  matrix products  5.58 us (1%)
    all_to_all x11, starting transfers between devices, to_owners(): return lax.all_to_all(x, 'expert', split_axis=0, concat_axis=0, tiled=True)  74.7 us
    all_to_all x2, blocking collectives, to_owners(): return lax.all_to_all(x, 'expert', split_axis=0, concat_axis=0, tiled=True)  67.6 us
    all_to_all x11, waiting for transfers between devices, to_owners(): return lax.all_to_all(x, 'expert', split_axis=0, concat_axis=0, tiled=True)  51.3 us
    pallas_call x1, Pallas kernels, attend_backward(): call(backward_kernel, (struct((2, CHUNK, LANES), bf16), struct((BLOCK, LA...  31.7 us
    pallas_call x1, Pallas kernels, attend_forward(): call(forward_kernel, (struct((2, CHUNK, LANES), f32), struct((2, CHUNK, L...  25.8 us
    ppermute x19, starting transfers between devices, shift(): return lax.ppermute(x, 'context', [(i, (i + by) % 4) for i in range(4)])  22 us
    ppermute x3, starting transfers between devices, swap_cores(): return lax.ppermute(x, 'dp', [(0, 1), (1, 0)])  19.9 us
    pallas_call x1, Pallas kernels, experts(): call(expert_kernel, (struct((16, 2, CAP, D), bf16), struct((2, 768, F), b...  16 us
  transfers between devices with their start and end apart: 43, of which 16 were waited for; matrix products, arithmetic and copies ran while one was open for 9% of the time, Pallas kernels for 23%

profile of v3, /device:TPU:69, one launch (start us, length us, event | category | flops | bytes accessed | tf_op | source)
XLA Modules:
  0.0 474.4 jit_solution(4365817087583786719)
XLA Ops:
  13.2 6.8 %all-to-all-start = ((bf16[16,128,128]{2,1,0:T(8,128)(2,1)}), bf16[16,128,128]{2,1,0:T(8,128)(2,1)}, u32[]{:S(2)}, u32[]{:S(2)}) async-start(bf16[16,128,128]{2,1,0:T(8,128)(2,1)} %get-tuple-element.75), calls=%async_computation | async-start | bytes 1048576 | tf_op jit(solution)/shard_map/all_to_all | solution.py:591
  20.6 6.7 %all-to-all-done = bf16[16,128,128]{2,1,0:T(8,128)(2,1)} async-done(((bf16[16,128,128]{2,1,0:T(8,128)(2,1)}), bf16[16,128,128]{2,1,0:T(8,128)(2,1)}, u32[]{:S(2)}, u32[]{:S(2)}) %all-to-all-start) | async-done | bytes 524320 | tf_op jit(solution)/shard_map/all_to_all | solution.py:591
  30.0 6.7 %all-to-all-start.1 = ((bf16[16,64,128]{2,1,0:T(8,128)(2,1)}), bf16[16,64,128]{2,1,0:T(8,128)(2,1)S(1)}, u32[]{:S(2)}, u32[]{:S(2)}) async-start(bf16[16,64,128]{2,1,0:T(8,128)(2,1)} %get-tuple-element.76), calls=%async_computation.1 | async-start | bytes 524288 | tf_op jit(solution)/shard_map/all_to_all | solution.py:591
  41.9 6.7 %all-to-all-start.2 = ((bf16[16,2,48,1024]{3,2,1,0:T(8,128)(2,1)}), bf16[16,2,48,1024]{3,2,1,0:T(8,128)(2,1)S(1)}, u32[]{:S(2)}, u32[]{:S(2)}) async-start(bf16[16,2,48,1024]{3,2,1,0:T(8,128)(2,1)} %bitcast.11), calls=%async_computation.2 | async-start | bytes 6291456 | tf_op jit(solution)/shard_map/all_to_all | solution.py:591
  66.1 25.8 %attend.1 = (f32[2,512,128]{2,1,0:T(8,128)}, bf16[2,512,128]{2,1,0:T(8,128)(2,1)}, f32[4,8,512]{2,1,0:T(8,128)}, bf16[8192,128]{1,0:T(8,128)(2,1)}) custom-call(s32[2]{0:T(128)} %pad_add_fusion.place_ref, bf16[2,512,128]{2,1,0:T(8,128)(2,1)} %pad_maximum_fusion.4.q_ref, bf16[2048,128]{1,0:T(8,128)(2,1)} %bitcast.5.own_ref, ...), custom_call_target="tpu_custom_call" | custom-call | flops 20000000000 | bytes 4000000 | tf_op jit(solution)/shard_map/attend/pallas_call | solution.py:178
  99.0 6.7 %all-to-all-start.3 = ((bf16[16,64,128]{2,1,0:T(8,128)(2,1)}), bf16[16,64,128]{2,1,0:T(8,128)(2,1)}, u32[]{:S(2)}, u32[]{:S(2)}) async-start(bf16[16,64,128]{2,1,0:T(8,128)(2,1)} %bitcast.14), calls=%async_computation.3 | async-start | bytes 524288 | tf_op jit(solution)/shard_map/all_to_all | solution.py:591
  114.9 35.2 %all_to_all.65.x_ref = bf16[16,2,48,1024]{3,2,1,0:T(8,128)(2,1)} all-to-all(bf16[16,2,48,1024]{3,2,1,0:T(8,128)(2,1)} %bitcast.133), channel_id=1, replica_groups=mesh['expert'=16,'context'=4,'dp'=2] {'expert'}, dimensions={0} | all-to-all | bytes 6291456 | tf_op jit(solution)/shard_map/all_to_all | solution.py:591
  151.7 7.2 %all-to-all-start.5 = ((bf16[16,64,1024]{2,1,0:T(8,128)(2,1)}), bf16[16,64,1024]{2,1,0:T(8,128)(2,1)S(1)}, u32[]{:S(2)}, u32[]{:S(2)}) async-start(bf16[16,64,1024]{2,1,0:T(8,128)(2,1)} %bitcast.132), calls=%async_computation.5 | async-start | bytes 4194304 | tf_op jit(solution)/shard_map/all_to_all | solution.py:591
  164.6 16.0 %experts.1 = (bf16[16,2,48,1024]{3,2,1,0:T(8,128)(2,1)}, bf16[2,768,512]{2,1,0:T(8,128)(2,1)}, bf16[2,768,1024]{2,1,0:T(8,128)(2,1)}, f32[2,768,1]{2,1,0:T(8,128)}, f32[2,768,32]{2,1,0:T(8,128)}) custom-call(s32[1]{0:T(128)} %bitcast.21.first_ref, bf16[16,2,48,1024]{3,2,1,0:T(8,128)(2,1)} %all_to_all.65.x_ref, f32[2,768,512]{2,1,0:T(8,128)} %raw.1.raw_ref, ...), custom_call_target="tpu_custom_call" | custom-call | flops 8053063680 | bytes 20000000 | tf_op jit(solution)/shard_map/experts/pallas_call | solution.py:355
  180.6 32.3 %all_to_all.66 = bf16[16,2,48,1024]{3,2,1,0:T(8,128)(2,1)} all-to-all(bf16[16,2,48,1024]{3,2,1,0:T(8,128)(2,1)} %get-tuple-element.83), channel_id=1, replica_groups=mesh['expert'=16,'context'=4,'dp'=2] {'expert'}, dimensions={0} | all-to-all | bytes 6291456 | tf_op jit(solution)/shard_map/all_to_all | solution.py:591
  218.1 7.1 %all-to-all-start.7 = ((bf16[16,64,128]{2,1,0:T(8,128)(2,1)}), bf16[16,64,128]{2,1,0:T(8,128)(2,1)S(1)}, u32[]{:S(2)}, u32[]{:S(2)}) async-start(bf16[16,64,128]{2,1,0:T(8,128)(2,1)} %get-tuple-element.86), calls=%async_computation.7 | async-start | bytes 524288 | tf_op jit(solution)/shard_map/all_to_all | solution.py:591
  232.0 13.4 %expert_grads.1 = (bf16[16,2,48,1024]{3,2,1,0:T(8,128)(2,1)}, bf16[2,1024,1024]{2,1,0:T(8,128)(2,1)}, bf16[2,512,1024]{2,1,0:T(8,128)(2,1)}, f32[2,32,1024]{2,1,0:T(8,128)}) custom-call(bf16[16,2,48,1024]{3,2,1,0:T(8,128)(2,1)} %all_to_all.65.x_ref, bf16[16,2,48,1024]{3,2,1,0:T(8,128)(2,1)} %copy-done.1, f32[2,768,1]{2,1,0:T(8,128)} %get-tuple-element.98.gate_ref, ...), custom_call_target="tpu_custom_call" | custom-call | flops 6442450944 | bytes 24000000 | tf_op jit(solution)/shard_map/expert_grads/pallas_call | solution.py:395
  245.3 7.0 %all-to-all-start.8 = ((bf16[16,2,48,1024]{3,2,1,0:T(8,128)(2,1)}), bf16[16,2,48,1024]{3,2,1,0:T(8,128)(2,1)S(1)}, u32[]{:S(2)}, u32[]{:S(2)}) async-start(bf16[16,2,48,1024]{3,2,1,0:T(8,128)(2,1)} %get-tuple-element.103), calls=%async_computation.8 | async-start | bytes 6291456 | tf_op jit(solution)/shard_map/all_to_all | solution.py:591
  254.7 31.7 %attend_back.1 = (bf16[2,512,128]{2,1,0:T(8,128)(2,1)}, f32[2048,128]{1,0:T(8,128)}, bf16[1024,128]{1,0:T(8,128)(2,1)}, bf16[1024,128]{1,0:T(8,128)(2,1)}, bf16[...) custom-call(s32[2]{0:T(128)} %pad_add_fusion.place_ref, ...), custom_call_target="tpu_custom_call" | custom-call | flops 49999998976 | bytes 8000000 | tf_op jit(solution)/shard_map/attend_back/pallas_call | solution.py:259
  289.0 6.7 %all-to-all-start.9 = ((bf16[16,64,1024]{2,1,0:T(8,128)(2,1)}), bf16[16,64,1024]{2,1,0:T(8,128)(2,1)}, u32[]{:S(2)}, u32[]{:S(2)}) async-start(bf16[16,64,1024]{2,1,0:T(8,128)(2,1)} %bitcast.131), calls=%async_computation.9 | async-start | bytes 4194304 | tf_op jit(solution)/shard_map/all_to_all | solution.py:591
  320.9 7.0 %collective-permute-done.14 = bf16[16,64,128]{2,1,0:T(8,128)(2,1)} collective-permute-done((bf16[16,64,128]{2,1,0:T(8,128)(2,1)S(1)}, bf16[16,64,128]{2,1,0:T(8,128)(2,1)}, u32[]{:S(2)}, u32[]{:S(2)}) %collective-permute-start.14) | collective-permute-done | bytes 262176 | tf_op jit(solution)/shard_map/ppermute | solution.py:623
  327.9 5.6 %head_grads.1 = (bf16[768,256]{1,0:T(8,128)(2,1)}, bf16[768,256]{1,0:T(8,128)(2,1)}, bf16[1024,256]{1,0:T(8,128)(2,1)}) custom-call(s32[1]{0:T(128)} %bitcast.core_ref, bf16[1024,1024]{1,0:T(8,128)(2,1)} %bitcast.130, bf16[1024,1024]{1,0:T(8,128)(2,1)} %bitcast.29.attn_ref, bf16[1024,128]{1,0:T(8,128)(2,1)} %bitcast.30.o_ref, bf16[1024,128]{1,0:T(8,128)(2,1)} %bitcast.144, ...), custom_call_target="tpu_custom_call" | custom-call | flops 1073741824 | bytes 8000000 | tf_op jit(solution)/shard_map/head_grads/pallas_call | solution.py:476
  333.5 11.5 %collective-permute-start.15 = (bf16[768,256]{1,0:T(8,128)(2,1)}, bf16[768,256]{1,0:T(8,128)(2,1)}, u32[]{:S(2)}, u32[]{:S(2)}) collective-permute-start(bf16[768,256]{1,0:T(8,128)(2,1)} %get-tuple-element.115), channel_id=1, source_target_pairs={{0,1},{1,0},{2,3},{3,2},{4,5},{5,4},{6,7},{7,6},{8,9},{9,8},{10,11... | collective-permute-start | bytes 1179656 | tf_op jit(solution)/shard_map/ppermute | solution.py:599
  347.7 6.7 %all-to-all-start.10 = ((bf16[16,8,256]{2,1,0:T(8,128)(2,1)}), bf16[16,8,256]{2,1,0:T(8,128)(2,1)S(1)}, u32[]{:S(2)}, u32[]{:S(2)}) async-start(bf16[16,8,256]{2,1,0:T(8,128)(2,1)} %bitcast.58), calls=%async_computation.10 | async-start | bytes 131072 | tf_op jit(solution)/shard_map/all_to_all | solution.py:591
  361.9 6.7 %all-to-all-start.11 = ((bf16[16,64,256]{2,1,0:T(8,128)(2,1)}), bf16[16,64,256]{2,1,0:T(8,128)(2,1)S(1)}, u32[]{:S(2)}, u32[]{:S(2)}) async-start(bf16[16,64,256]{2,1,0:T(8,128)(2,1)} %bitcast.152), calls=%async_computation.11 | async-start | bytes 1048576 | tf_op jit(solution)/shard_map/all_to_all | solution.py:591
  393.8 6.7 %all-to-all-start.12 = ((bf16[16,400,256]{2,1,0:T(8,128)(2,1)}), bf16[16,400,256]{2,1,0:T(8,128)(2,1)S(1)}, u32[]{:S(2)}, u32[]{:S(2)}) async-start(bf16[16,400,256]{2,1,0:T(8,128)(2,1)} %broadcast_in_dim.44), calls=%async_computation.13 | async-start | bytes 6553600 | tf_op jit(solution)/shard_map/all_to_all | solution.py:591
  401.1 37.4 %all-to-all-done.12.own_ref = bf16[16,400,256]{2,1,0:T(8,128)(2,1)S(1)} async-done(((bf16[16,400,256]{2,1,0:T(8,128)(2,1)}), bf16[16,400,256]{2,1,0:T(8,128)(2,1)S(1)}, u32[]{:S(2)}, u32[]{:S(2)}) %all-to-all-start.12) | async-done | bytes 3276832 | tf_op jit(solution)/shard_map/all_to_all | solution.py:591
  438.5 8.4 %collective-permute-start.27 = (bf16[16,400,256]{2,1,0:T(8,128)(2,1)S(1)}, bf16[16,400,256]{2,1,0:T(8,128)(2,1)}, u32[]{:S(2)}, u32[]{:S(2)}) collective-permute-start(bf16[16,400,256]{2,1,0:T(8,128)(2,1)S(1)} %all-to-all-done.12.own_ref), channel_id=1, source_target_pairs={{0,1},{1,0},{2,3},{3,2},{4,5},{5,4},{6,7},{7,6},{8,9},{9,8},{10,11... | collective-permute-start | bytes 9830408 | tf_op jit(solution)/shard_map/ppermute | solution.py:599
  454.1 10.8 %assemble.1 = (f32[1024,1024]{1,0:T(8,128)}, f32[1024,512]{1,0:T(8,128)}, f32[1024,512]{1,0:T(8,128)}, f32[1024,1024]{1,0:T(8,128)}, f32[1024,1]{1,0:T(8,128)}) custom-call(s32[1]{0:T(128)} %bitcast.core_ref, bf16[16,400,256]{2,1,0:T(8,128)(2,1)} %copy-done, bf16[16,400,256]{2,1,0:T(8,128)(2,1)} %collective-permute-done.27.other_ref, ...), custom_call_target="tpu_custom_call" | custom-call | flops 1000000 | bytes 22000000 | tf_op jit(solution)/shard_map/assemble/pallas_call | solution.py:569
  (183 shorter events, 143.2 us)
Async XLA Ops:
  7.2 152.5 %all-gather.3.cloned.1.call-start = ((), (), s32[]{:S(2)}) async-start(), calls=%async_computation.15 | async-start | bytes 2359296 | tf_op jit(solution)/shard_map/all_gather | solution.py:673
  13.2 14.1 %all-to-all-start = ((bf16[16,128,128]{2,1,0:T(8,128)(2,1)}), bf16[16,128,128]{2,1,0:T(8,128)(2,1)}, u32[]{:S(2)}, u32[]{:S(2)}) async-start(bf16[16,128,128]{2,1,0:T(8,128)(2,1)} %get-tuple-element.75), calls=%async_computation | async-start | bytes 1048576 | tf_op jit(solution)/shard_map/all_to_all | solution.py:591
  27.3 21.3 %collective-permute-start.1 = (bf16[2048,128]{1,0:T(8,128)(2,1)}, bf16[2048,128]{1,0:T(8,128)(2,1)}, u32[]{:S(2)}, u32[]{:S(2)}) collective-permute-start(bf16[2048,128]{1,0:T(8,128)(2,1)} %bitcast.5.own_ref), channel_id=1, source_target_pairs={{0,2},{2,4},{4,6},{6,0},{1,3},{3,5},{5,7},{7,1},{8,10},{10,12},{12... | collective-permute-start | bytes 1572872 | tf_op jit(solution)/shard_map/ppermute | solution.py:603
  28.6 21.0 %collective-permute-start.3 = (bf16[2048,128]{1,0:T(8,128)(2,1)}, bf16[2048,128]{1,0:T(8,128)(2,1)}, u32[]{:S(2)}, u32[]{:S(2)}) collective-permute-start(bf16[2048,128]{1,0:T(8,128)(2,1)} %bitcast.5.own_ref), channel_id=1, source_target_pairs={{0,6},{2,0},{4,2},{6,4},{1,7},{3,1},{5,3},{7,5},{8,14},{10,8},{12,... | collective-permute-start | bytes 1572872 | tf_op jit(solution)/shard_map/ppermute | solution.py:603
  30.0 11.1 %all-to-all-start.1 = ((bf16[16,64,128]{2,1,0:T(8,128)(2,1)}), bf16[16,64,128]{2,1,0:T(8,128)(2,1)S(1)}, u32[]{:S(2)}, u32[]{:S(2)}) async-start(bf16[16,64,128]{2,1,0:T(8,128)(2,1)} %get-tuple-element.76), calls=%async_computation.1 | async-start | bytes 524288 | tf_op jit(solution)/shard_map/all_to_all | solution.py:591
  41.9 50.0 %all-to-all-start.2 = ((bf16[16,2,48,1024]{3,2,1,0:T(8,128)(2,1)}), bf16[16,2,48,1024]{3,2,1,0:T(8,128)(2,1)S(1)}, u32[]{:S(2)}, u32[]{:S(2)}) async-start(bf16[16,2,48,1024]{3,2,1,0:T(8,128)(2,1)} %bitcast.11), calls=%async_computation.2 | async-start | bytes 6291456 | tf_op jit(solution)/shard_map/all_to_all | solution.py:591
  48.5 116.1 %all-gather.5.cloned.1.call-start = ((), (), s32[]{:S(2)}) async-start(), calls=%async_computation.16 | async-start | bytes 4718592 | tf_op jit(solution)/shard_map/all_gather | solution.py:672
  151.7 28.9 %all-to-all-start.5 = ((bf16[16,64,1024]{2,1,0:T(8,128)(2,1)}), bf16[16,64,1024]{2,1,0:T(8,128)(2,1)S(1)}, u32[]{:S(2)}, u32[]{:S(2)}) async-start(bf16[16,64,1024]{2,1,0:T(8,128)(2,1)} %bitcast.132), calls=%async_computation.5 | async-start | bytes 4194304 | tf_op jit(solution)/shard_map/all_to_all | solution.py:591
  218.1 11.1 %all-to-all-start.7 = ((bf16[16,64,128]{2,1,0:T(8,128)(2,1)}), bf16[16,64,128]{2,1,0:T(8,128)(2,1)S(1)}, u32[]{:S(2)}, u32[]{:S(2)}) async-start(bf16[16,64,128]{2,1,0:T(8,128)(2,1)} %get-tuple-element.86), calls=%async_computation.7 | async-start | bytes 524288 | tf_op jit(solution)/shard_map/all_to_all | solution.py:591
  229.9 23.2 %collective-permute-start.6 = (bf16[512,128]{1,0:T(8,128)(2,1)}, bf16[512,128]{1,0:T(8,128)(2,1)}, u32[]{:S(2)}, u32[]{:S(2)}) collective-permute-start(bf16[512,128]{1,0:T(8,128)(2,1)} %bitcast.24), channel_id=1, source_target_pairs={{0,6},{2,4},{4,2},{6,0},{1,7},{3,5},{5,3},{7,1},{8,14},{10,12},{12... | collective-permute-start | bytes 393224 | tf_op jit(solution)/shard_map/ppermute | solution.py:595
  245.3 41.1 %all-to-all-start.8 = ((bf16[16,2,48,1024]{3,2,1,0:T(8,128)(2,1)}), bf16[16,2,48,1024]{3,2,1,0:T(8,128)(2,1)S(1)}, u32[]{:S(2)}, u32[]{:S(2)}) async-start(bf16[16,2,48,1024]{3,2,1,0:T(8,128)(2,1)} %get-tuple-element.103), calls=%async_computation.8 | async-start | bytes 6291456 | tf_op jit(solution)/shard_map/all_to_all | solution.py:591
  252.3 137.5 %reduce-scatter.3.cloned.1.call-start = ((), (), s32[]{:S(2)}) async-start(), calls=%async_computation.17 | async-start | bytes 4718592 | tf_op jit(solution)/shard_map/reduce_scatter | solution.py:696
  289.0 39.0 %all-to-all-start.9 = ((bf16[16,64,1024]{2,1,0:T(8,128)(2,1)}), bf16[16,64,1024]{2,1,0:T(8,128)(2,1)}, u32[]{:S(2)}, u32[]{:S(2)}) async-start(bf16[16,64,1024]{2,1,0:T(8,128)(2,1)} %bitcast.131), calls=%async_computation.9 | async-start | bytes 4194304 | tf_op jit(solution)/shard_map/all_to_all | solution.py:591
  303.0 11.6 %collective-permute-start.11 = (bf16[1024,128]{1,0:T(8,128)(2,1)}, bf16[1024,128]{1,0:T(8,128)(2,1)S(1)}, u32[]{:S(2)}, u32[]{:S(2)}) collective-permute-start(bf16[1024,128]{1,0:T(8,128)(2,1)} %get-tuple-element.111), channel_id=1, source_target_pairs={{0,6},{2,0},{4,2},{6,4},{1,7},{3,1},{5,3},{7,5},{8,14},{10,8},{12,... | collective-permute-start | bytes 786440 | tf_op jit(solution)/shard_map/ppermute | solution.py:603
  333.5 20.9 %collective-permute-start.15 = (bf16[768,256]{1,0:T(8,128)(2,1)}, bf16[768,256]{1,0:T(8,128)(2,1)}, u32[]{:S(2)}, u32[]{:S(2)}) collective-permute-start(bf16[768,256]{1,0:T(8,128)(2,1)} %get-tuple-element.115), channel_id=1, source_target_pairs={{0,1},{1,0},{2,3},{3,2},{4,5},{5,4},{6,7},{7,6},{8,9},{9,8},{10,11... | collective-permute-start | bytes 1179656 | tf_op jit(solution)/shard_map/ppermute | solution.py:599
  347.7 12.7 %all-to-all-start.10 = ((bf16[16,8,256]{2,1,0:T(8,128)(2,1)}), bf16[16,8,256]{2,1,0:T(8,128)(2,1)S(1)}, u32[]{:S(2)}, u32[]{:S(2)}) async-start(bf16[16,8,256]{2,1,0:T(8,128)(2,1)} %bitcast.58), calls=%async_computation.10 | async-start | bytes 131072 | tf_op jit(solution)/shard_map/all_to_all | solution.py:591
  357.1 11.6 %collective-permute-start.16 = (bf16[384,256]{1,0:T(8,128)(2,1)}, bf16[384,256]{1,0:T(8,128)(2,1)}, u32[]{:S(2)}, u32[]{:S(2)}) collective-permute-start(bf16[384,256]{1,0:T(8,128)(2,1)} %dynamic-slice_bitcast_fusion), channel_id=1, source_target_pairs={{0,8},{8,0},{16,24},{24,16},{32,40},{40,32},{48,56},{56,48},{64,72... | collective-permute-start | bytes 589832 | tf_op jit(solution)/shard_map/ppermute | solution.py:623
  360.4 13.1 %collective-permute-start.26 = (bf16[8,256]{1,0:T(8,128)(2,1)S(1)}, bf16[8,256]{1,0:T(8,128)(2,1)S(1)}, u32[]{:S(2)}, u32[]{:S(2)}) collective-permute-start(bf16[8,256]{1,0:T(8,128)(2,1)S(1)} %reduce_sum.22), channel_id=1, source_target_pairs={{0,6},{2,0},{4,2},{6,4},{1,7},{3,1},{5,3},{7,5},{8,14},{10,8},{12,... | collective-permute-start | bytes 12296 | tf_op jit(solution)/shard_map/ppermute | solution.py:603
  360.5 13.7 %collective-permute-start.25 = (bf16[8,256]{1,0:T(8,128)(2,1)S(1)}, bf16[8,256]{1,0:T(8,128)(2,1)S(1)}, u32[]{:S(2)}, u32[]{:S(2)}) collective-permute-start(bf16[8,256]{1,0:T(8,128)(2,1)S(1)} %reduce_sum.22), channel_id=1, source_target_pairs={{0,4},{2,6},{4,0},{6,2},{1,5},{3,7},{5,1},{7,3},{8,12},{10,14},{12... | collective-permute-start | bytes 12296 | tf_op jit(solution)/shard_map/ppermute | solution.py:603
  360.8 13.5 %collective-permute-start.24 = (bf16[8,256]{1,0:T(8,128)(2,1)S(1)}, bf16[8,256]{1,0:T(8,128)(2,1)S(1)}, u32[]{:S(2)}, u32[]{:S(2)}) collective-permute-start(bf16[8,256]{1,0:T(8,128)(2,1)S(1)} %reduce_sum.22), channel_id=1, source_target_pairs={{0,2},{2,4},{4,6},{6,0},{1,3},{3,5},{5,7},{7,1},{8,10},{10,12},{12... | collective-permute-start | bytes 12296 | tf_op jit(solution)/shard_map/ppermute | solution.py:603
  361.9 16.5 %all-to-all-start.11 = ((bf16[16,64,256]{2,1,0:T(8,128)(2,1)}), bf16[16,64,256]{2,1,0:T(8,128)(2,1)S(1)}, u32[]{:S(2)}, u32[]{:S(2)}) async-start(bf16[16,64,256]{2,1,0:T(8,128)(2,1)} %bitcast.152), calls=%async_computation.11 | async-start | bytes 1048576 | tf_op jit(solution)/shard_map/all_to_all | solution.py:591
  393.8 44.7 %all-to-all-start.12 = ((bf16[16,400,256]{2,1,0:T(8,128)(2,1)}), bf16[16,400,256]{2,1,0:T(8,128)(2,1)S(1)}, u32[]{:S(2)}, u32[]{:S(2)}) async-start(bf16[16,400,256]{2,1,0:T(8,128)(2,1)} %broadcast_in_dim.44), calls=%async_computation.13 | async-start | bytes 6553600 | tf_op jit(solution)/shard_map/all_to_all | solution.py:591
  400.5 46.4 %reduce-scatter.5.cloned.1.call-start = ((), (), s32[]{:S(2)}) async-start(), calls=%async_computation.18 | async-start | bytes 2359296 | tf_op jit(solution)/shard_map/reduce_scatter | solution.py:736
  438.5 14.0 %collective-permute-start.27 = (bf16[16,400,256]{2,1,0:T(8,128)(2,1)S(1)}, bf16[16,400,256]{2,1,0:T(8,128)(2,1)}, u32[]{:S(2)}, u32[]{:S(2)}) collective-permute-start(bf16[16,400,256]{2,1,0:T(8,128)(2,1)S(1)} %all-to-all-done.12.own_ref), channel_id=1, source_target_pairs={{0,1},{1,0},{2,3},{3,2},{4,5},{5,4},{6,7},{7,6},{8,9},{9,8},{10,11... | collective-permute-start | bytes 9830408 | tf_op jit(solution)/shard_map/ppermute | solution.py:599
  (35 other events, 340.4 us)
Sparse Core Ops, SparseCore 0:
  9.7 28.7 all-gather.2
  56.9 38.8 all-gather.4
  256.1 47.2 reduce-scatter.2
  404.0 36.0 reduce-scatter.4

commit v4 on v3

--- a/solution.py
+++ b/solution.py
@@ -67,7 +67,8 @@
     x = x_ref[...].astype(f32)
     inverse = lax.rsqrt(jnp.mean(x * x, axis=-1, keepdims=True) + norm_eps)
     act = (x * inverse * gain_ref[...]).astype(bf16)
-    act_ref[...] = act
+    for e in range(16):
+        act_ref[e] = act[64 * (e % 2) : 64 * (e % 2) + 64]
     cos = cos_ref[...]
     sin = sin_ref[...]
     lane = lane_index((TOK, LANES))
@@ -99,7 +100,7 @@
 def project(x, gain, wq, wk, wv, cos, sin):
     return call(
         project_kernel,
-        (struct((TOK, D), bf16), struct((16, TOK // 2, LANES), bf16), struct((16, TOK, LANES), bf16)),
+        (struct((16, 64, D), bf16), struct((16, 64, LANES), bf16), struct((16, TOK, LANES), bf16)),
         2 * TOK * D * 2048,
         6e6,
         name="project",
@@ -114,27 +115,32 @@
 
 
 def forward_kernel(
-    place_ref, q_ref, own_ref, left_ref, far_a_ref, far_b_ref, right_ref,
-    o_ref, low_ref, lse_ref, kv_ref, qm_ref, top_ref, acc_ref,
+    place_ref, q_ref, q_far_ref, own_ref, left_a_ref, left_b_ref, far_a_ref, far_b_ref, right_a_ref, right_b_ref,
+    o_ref, low_ref, low_far_ref, lse_ref, kv_ref, qm_ref, top_ref, acc_ref,
 ):
     tile = 1024
     context = place_ref[0]
     half = place_ref[1]
 
-    def block(back):
-        return pl.multiple_of(lax.rem(context + 4 - back, 4) * BLOCK, BLOCK)
-
-    kv_ref[pl.ds(block(0), BLOCK), :] = own_ref[...]
-    kv_ref[pl.ds(block(1), BLOCK), :] = left_ref[...]
-    kv_ref[pl.ds(block(2), BLOCK // 2), :] = far_a_ref[...]
-    kv_ref[pl.ds(pl.multiple_of(block(2) + BLOCK // 2, BLOCK // 2), BLOCK // 2), :] = far_b_ref[...]
-    kv_ref[pl.ds(block(3), BLOCK), :] = right_ref[...]
+    def put(back, part, ref):
+        start = lax.rem(context + 4 - back, 4) * BLOCK + part * (BLOCK // 2)
+        rows = ref.shape[0] * TOK
+        kv_ref[pl.ds(pl.multiple_of(start, BLOCK // 2), rows), :] = ref[...].reshape(rows, LANES)
+
+    put(0, 0, own_ref)
+    put(1, 0, left_a_ref)
+    put(1, 1, left_b_ref)
+    put(2, 0, far_a_ref)
+    put(2, 1, far_b_ref)
+    put(3, 0, right_a_ref)
+    put(3, 1, right_b_ref)
     left = lane_index((CHUNK, LANES)) < HEAD_DIM
     left_keys = lane_index((tile, LANES)) < HEAD_DIM
     for chunk in range(2):
         whole = 2 * (context if chunk == 0 else 3 - context) + chunk
+        queries = (q_far_ref[...] if chunk else q_ref[:8]).reshape(CHUNK, LANES)
         for head in range(2):
-            qm_ref[head] = query_of_head(q_ref[chunk], head, left)
+            qm_ref[head] = query_of_head(queries, head, left)
             top_ref[head] = jnp.full((CHUNK, LANES), huge_negative, f32)
             acc_ref[head] = jnp.zeros((CHUNK, LANES), f32)
 
@@ -169,36 +175,37 @@
             lse_ref[2 * chunk + head] = jnp.transpose(total)[0:8]
         o = jnp.where(left, outs[0], pltpu.roll(outs[1], HEAD_DIM, 1))
         o_ref[chunk] = o
-        low_ref[chunk] = o.astype(bf16)
-
-
-def attend_forward(place, q, kv_parts):
+        (low_far_ref if chunk else low_ref)[...] = o.astype(bf16).reshape(8, 64, LANES)
+
+
+def attend_forward(place, q, q_far, kv_parts):
     smem = pl.BlockSpec(memory_space=pltpu.SMEM)
     vmem = pl.BlockSpec(memory_space=pltpu.VMEM)
     return call(
         forward_kernel,
         (
             struct((2, CHUNK, LANES), f32),
-            struct((2, CHUNK, LANES), bf16),
+            struct((8, 64, LANES), bf16),
+            struct((8, 64, LANES), bf16),
             struct((4, 8, CHUNK), f32),
             struct((4 * BLOCK, LANES), bf16),
         ),
         2e10,
         4e6,
-        in_specs=[smem] + [vmem] * 6,
-        out_specs=(vmem,) * 4,
+        in_specs=[smem] + [vmem] * 9,
+        out_specs=(vmem,) * 5,
         scratch_shapes=[
             pltpu.VMEM((2, CHUNK, LANES), bf16),
             pltpu.VMEM((2, CHUNK, LANES), f32),
             pltpu.VMEM((2, CHUNK, LANES), f32),
         ],
         name="attend",
-    )(place, q, *kv_parts)
+    )(place, q, q_far, *kv_parts)
 
 
 def backward_kernel(
-    place_ref, q_ref, do_ref, o_ref, lse_ref, kv_ref,
-    dq_ref, d0_ref, d1a_ref, d1b_ref, d2a_ref, d2b_ref, d3a_ref, d3b_ref,
+    place_ref, q_ref, q_far_ref, do_ref, do_far_ref, o_ref, lse_ref, kv_ref,
+    dq_ref, dq_far_ref, d0_ref, d1a_ref, d1b_ref, d2a_ref, d2b_ref, d3a_ref, d3b_ref,
     qm_ref, dom_ref, row_ref, dqt_ref, acc_ref,
 ):
     tile = 512
@@ -208,10 +215,11 @@
     acc_ref[...] = jnp.zeros_like(acc_ref)
     for chunk in range(2):
         whole = 2 * (2 * (context if chunk == 0 else 3 - context) + chunk)
-        do = do_ref[chunk].astype(f32)
+        queries = (q_far_ref[...] if chunk else q_ref[:8]).reshape(CHUNK, LANES)
+        do = (do_far_ref[...] if chunk else do_ref[:8]).reshape(CHUNK, LANES).astype(f32)
         product = jnp.transpose(do * o_ref[chunk])
         for head in range(2):
-            qm_ref[head] = query_of_head(q_ref[chunk], head, left)
+            qm_ref[head] = query_of_head(queries, head, left)
             moved = do if head else pltpu.roll(do, HEAD_DIM, 1)
             dom_ref[head] = jnp.where(left, 0.0, moved).astype(bf16)
             dqt_ref[head] = jnp.zeros((LANES, CHUNK), f32)
@@ -244,7 +252,8 @@
         step(whole, 0)
         step(whole + 1, tile)
         parts = [jnp.transpose(dqt_ref[head]) * score_scale for head in range(2)]
-        dq_ref[chunk] = jnp.where(left, parts[0], pltpu.roll(parts[1], HEAD_DIM, 1)).astype(bf16)
+        dq = jnp.where(left, parts[0], pltpu.roll(parts[1], HEAD_DIM, 1)).astype(bf16)
+        (dq_far_ref if chunk else dq_ref)[...] = dq.reshape(8, 64, LANES)
     d0_ref[...] = acc_ref[pl.ds(pl.multiple_of(context * BLOCK, BLOCK), BLOCK), :]
     for back, first, second in ((1, d1a_ref, d1b_ref), (2, d2a_ref, d2b_ref), (3, d3a_ref, d3b_ref)):
         start = pl.multiple_of(lax.rem(context + 4 - back, 4) * BLOCK, BLOCK)
@@ -252,18 +261,18 @@
         second[...] = acc_ref[pl.ds(pl.multiple_of(start + BLOCK // 2, BLOCK // 2), BLOCK // 2), :].astype(bf16)
 
 
-def attend_backward(place, q, do, o, lse, kv):
+def attend_backward(place, q, q_far, do, do_far, o, lse, kv):
     smem = pl.BlockSpec(memory_space=pltpu.SMEM)
     vmem = pl.BlockSpec(memory_space=pltpu.VMEM)
     rows = kv.shape[0]
     return call(
         backward_kernel,
-        (struct((2, CHUNK, LANES), bf16), struct((BLOCK, LANES), f32))
+        (struct((8, 64, LANES), bf16), struct((8, 64, LANES), bf16), struct((BLOCK, LANES), f32))
         + (struct((BLOCK // 2, LANES), bf16),) * 6,
         5e10,
         8e6,
-        in_specs=[smem] + [vmem] * 5,
-        out_specs=(vmem,) * 8,
+        in_specs=[smem] + [vmem] * 7,
+        out_specs=(vmem,) * 9,
         scratch_shapes=[
             pltpu.VMEM((2, CHUNK, LANES), bf16),
             pltpu.VMEM((2, CHUNK, LANES), bf16),
@@ -272,7 +281,7 @@
             pltpu.VMEM((rows, LANES), f32),
         ],
         name="attend_back",
-    )(place, q, do, o, lse, kv)
+    )(place, q, q_far, do, do_far, o, lse, kv)
 
 
 def middle_kernel(att_ref, x_ref, wo_ref, gain_ref, pick_ref, hidden_ref, send_ref, attended_ref):
@@ -420,7 +429,8 @@
     state = top_ref[...].astype(f32) + inverse * (scaled - normed * jnp.mean(scaled * normed, axis=-1, keepdims=True))
     state_ref[...] = state
     attn = (branch_scale * state).astype(bf16)
-    attn_ref[...] = attn
+    for e in range(16):
+        attn_ref[e] = attn[64 * (e % 2) : 64 * (e % 2) + 64]
     attended = dot_rows(attn, wo_ref[...]).astype(bf16)
     for j in range(PAIRS):
         for h in range(2):
@@ -433,7 +443,7 @@
         turn_back_kernel,
         (
             struct((TOK, D), f32),
-            struct((TOK, D), bf16),
+            struct((16, 64, D), bf16),
             struct((16, TOK // 2, LANES), bf16),
             struct((8, D), f32),
         ),
@@ -519,7 +529,9 @@
     )(grads, x, gain.reshape(1, D), wq, wk, wv, state)
 
 
-def assemble_kernel(core_ref, own_ref, other_ref, wq_ref, wk_ref, wv_ref, q_ref, k_ref, v_ref, o_ref, norm_ref):
+def assemble_kernel(
+    core_ref, own_ref, other_ref, wq_ref, wk_ref, wv_ref, gain_ref, q_ref, k_ref, v_ref, o_ref, norm_ref
+):
     left = lane_index((384, LANES)) < HEAD_DIM
 
     def write(pieces):
@@ -545,7 +557,8 @@
                         k_ref[rows, lanes] = k
                         v_ref[rows, lanes] = v
                         total = total + k * wk_ref[rows, lanes].astype(f32) + v * wv_ref[rows, lanes].astype(f32)
-                    norm_ref[rows] = jnp.sum(total, axis=-1, keepdims=True)
+                    summed = jnp.sum(jnp.transpose(total), axis=0, keepdims=True)
+                    norm_ref[:, rows] = summed / gain_ref[:, rows]
                 for b in range(4):
                     at = D + LANES * b - start
                     if 0 <= at < 384:
@@ -563,7 +576,7 @@
         write((other_ref, own_ref))
 
 
-def assemble(core, own, other, wq, wk, wv):
+def assemble(core, own, other, wq, wk, wv, gain):
     smem = pl.BlockSpec(memory_space=pltpu.SMEM)
     vmem = pl.BlockSpec(memory_space=pltpu.VMEM)
     return call(
@@ -573,14 +586,14 @@
             struct((D, 512), f32),
             struct((D, 512), f32),
             struct((D, D), f32),
-            struct((D, 1), f32),
+            struct((1, D), f32),
         ),
         1e6,
         2.2e7,
-        in_specs=[smem] + [vmem] * 5,
+        in_specs=[smem] + [vmem] * 6,
         out_specs=(vmem,) * 5,
         name="assemble",
-    )(core, own, other, wq, wk, wv)
+    )(core, own, other, wq, wk, wv, gain.reshape(1, D))
 
 
 def after(x, *earlier):
@@ -603,20 +616,8 @@
     return lax.ppermute(x, "context", [(i, (i + by) % 4) for i in range(4)])
 
 
-def sum_context(x, context):
-    parts = x.reshape(4, x.shape[0] // 4, x.shape[1])
-    got = [shift(pick(parts, (context + by) % 4), by) for by in (1, 2, 3)]
-    total = pick(parts, context).astype(f32)
-    for piece in got:
-        total = total + piece.astype(f32)
-    return total.astype(bf16)
-
-
-def gather_context(x, context):
-    got = [x] + [shift(x, by) for by in (1, 2, 3)]
-    rows = x.shape[0]
-    wide = jnp.concatenate([got[i] for i in (3, 2, 1, 0, 3, 2, 1)], 0)
-    return lax.dynamic_slice_in_dim(wide, (3 - context) * rows, 4 * rows, 0)
+def neighbour(x):
+    return lax.ppermute(x, "context", [(0, 1), (1, 0), (2, 3), (3, 2)])
 
 
 def swap_halves(x):
@@ -660,106 +661,107 @@
 
     core_index = lax.axis_index("dp")
     core = core_index.astype(jnp.int32).reshape(1)
-    act1, q_send, kv_send = project(x, norm1_gain, w_query, w_key, w_value, cos, sin)
-    kv_block = to_owners(kv_send).reshape(BLOCK, LANES)
-    kv_left = shift(kv_block, 1)
-    kv_right = shift(kv_block, 3)
-    kv_far_a = shift(kv_left[: BLOCK // 2], 1)
-    kv_far_b = shift(kv_right[BLOCK // 2 :], 3)
-    q_own = to_owners(after(q_send, kv_block)).reshape(2, CHUNK, LANES)
-    q = jnp.stack([q_own[0], mirror(q_own[1])], 0)
-
-    gate_up = lax.all_gather(after(w_gate_up, kv_far_a, kv_far_b), ("context", "dp"), axis=1, tiled=True)
+    act_send, q_send, kv_send = project(x, norm1_gain, w_query, w_key, w_value, cos, sin)
+    kv_own = to_owners(kv_send)
+    kv_a, kv_b = kv_own[:8], kv_own[8:]
+    left_a, right_b = shift(kv_a, 1), shift(kv_b, 3)
+    left_b, right_a = shift(kv_b, 1), shift(kv_a, 3)
+    q_own = to_owners(after(q_send, kv_own))
+    q_far = mirror(q_own[8:])
+    far_a, far_b = shift(left_a, 1), shift(right_b, 3)
+
+    gate_up = lax.all_gather(after(w_gate_up, far_a, far_b), ("context", "dp"), axis=1, tiled=True)
     down = lax.all_gather(w_down, ("context", "dp"), axis=1, tiled=True)
     top_send = dot(selector, top).astype(bf16).reshape(16, 2, CAP, D)
-    top_rows = to_owners(after(top_send, q_own))
+    top_rows = to_owners(after(top_send, q_far))
 
     seat = jnp.stack([context, half]).astype(jnp.int32)
-    o, o_low, lse, kv = attend_forward(seat, q, (kv_block, kv_left, kv_far_a, kv_far_b, kv_right))
-    o_low = after(o_low, top_rows)
-    o_own = jnp.stack([o_low[0], mirror(o_low[1])], 0).reshape(1024, LANES)
-    att = to_owners(o_own.reshape(16, TOK // 2, LANES))
+    o, o_low, o_far, lse, kv = attend_forward(
+        seat, q_own, q_far, (kv_own, left_a, left_b, far_a, far_b, right_a, right_b)
+    )
+    o_far = after(o_far, top_rows)
+    o_own = jnp.concatenate([o_low, mirror(o_far)], 0)
+    att = to_owners(o_own)
+    raw = raw_grads(top_rows, down)
+    att = after(att, raw)
 
     hidden, send = middle(att, x, w_out, norm2_gain, selector)
     rows = to_owners(send.reshape(16, 2, CAP, D))
-    raw = raw_grads(top_rows, down)
     first = (2 * expert).astype(jnp.int32).reshape(1)
-    act_send = jnp.broadcast_to(after(act1, rows).reshape(1, 2, 64, D), (8, 2, 64, D)).reshape(16, 64, D)
-    act_rows = to_owners(act_send).reshape(1024, D)
+    act_rows = to_owners(after(act_send, rows)).reshape(1024, D)
     grad_rows, expert_hidden, mixed, gates, logits = experts(first, rows, raw, gate_up, w_router)
     back = to_owners(after(grad_rows, act_rows))
     out_rows, dgu, ddown, router_grad = expert_grads(rows, top_rows, gates, logits, expert_hidden, mixed, down)
-
-    state, attn, do_send, norm2_grad = turn_back(back.reshape(SLOTS, D), spot, hidden, norm2_gain, top, w_out)
-    do_own = to_owners(do_send).reshape(2, CHUNK, LANES)
-    do = jnp.stack([do_own[0], mirror(do_own[1])], 0)
+    back = after(back, dgu)
+
+    state, attn_send, do_send, norm2_grad = turn_back(back.reshape(SLOTS, D), spot, hidden, norm2_gain, top, w_out)
+    do_own = to_owners(do_send)
+    do_far = mirror(do_own[8:])
+    attn_rows = to_owners(after(attn_send, do_own)).reshape(1024, D)
+    small = lax.psum(
+        jnp.concatenate([router_grad[0] + router_grad[1], norm2_grad], 0), ("expert", "context", "dp")
+    )
     grad_gate_up = lax.psum_scatter(
         after(dgu, do_own), ("context", "dp"), scatter_dimension=1, tiled=True
     ).astype(f32)
 
-    returned = to_owners(after(out_rows, do_own))
-    small = jnp.concatenate([router_grad[0] + router_grad[1], norm2_grad, jnp.zeros((24, D), f32)], 0)
-    small = small.reshape(64, 4, 256).transpose(1, 0, 2).reshape(2, 128, 256).astype(bf16)
-
-    dq, d0, d1a, d1b, d2a, d2b, d3a, d3b = attend_backward(seat, q, do, o, lse, kv)
-    dq, d0, d1a, d1b, d2a, d2b, d3a, d3b, returned = lax.optimization_barrier(
-        (dq, d0, d1a, d1b, d2a, d2b, d3a, d3b, returned)
-    )
-    block_out = hidden + branch_scale * dot(spot, returned.reshape(SLOTS, D))
-    attn_send = jnp.broadcast_to(after(attn, returned).reshape(1, 2, 64, D), (8, 2, 64, D)).reshape(16, 64, D)
-    attn_rows = to_owners(attn_send).reshape(1024, D)
+    dq, dq_far, d0, d1a, d1b, d2a, d2b, d3a, d3b = attend_backward(seat, q_own, q_far, do_own, do_far, o, lse, kv)
+    dq, dq_far, d0, d1a, d1b, d2a, d2b, d3a, d3b, attn_rows = lax.optimization_barrier(
+        (dq, dq_far, d0, d1a, d1b, d2a, d2b, d3a, d3b, attn_rows)
+    )
 
     far_a, far_b = shift(d2a, 1), shift(d2b, 3)
     from_left_b, from_right_a = shift(d3b, 1), shift(d1a, 3)
-    dq_own = jnp.stack([dq[0], mirror(dq[1])], 0).reshape(1024, LANES)
+    dq_far = mirror(dq_far)
+    dq_own = jnp.concatenate([dq, dq_far], 0).reshape(1024, LANES)
+    returned = to_owners(after(out_rows, dq_far))
     from_left_a = shift((d3a.astype(f32) + far_a.astype(f32)).astype(bf16), 1)
     from_right_b = shift((d1b.astype(f32) + far_b.astype(f32)).astype(bf16), 3)
-    from_left = jnp.stack([from_left_a, from_left_b], 0).reshape(16, 2, 64, LANES)
-    from_right = jnp.stack([from_right_a, from_right_b], 0).reshape(16, 2, 64, LANES)
-    pieces = (d0.reshape(16, 2, 64, LANES), from_left, from_right)
-    keep = sum(pick(piece, half, 1).astype(f32) for piece in pieces)
-    give = sum(pick(piece, 1 - half, 1).astype(f32) for piece in pieces).astype(bf16)
-    got = swap_halves(give)
-
-    small_other = swap_cores(pick(small, 1 - core_index))
-    small_half = (pick(small, core_index).astype(f32) + small_other.astype(f32)).astype(bf16)
-    small_piece = jnp.sum(to_owners(after(small_half, attn_rows).reshape(16, 8, 256)).astype(f32), 0).astype(bf16)
-    small_sum = small_piece.astype(f32)
-    for by in (1, 2, 3):
-        small_sum = small_sum + shift(small_piece, by).astype(f32)
-
+    own = d0.reshape(2, 8, 2, 64, LANES)
+
+    def half_sum(which):
+        first_part = pick(own[0], which, 1)
+        second_part = pick(own[1], which, 1)
+        for piece in (from_left_a, from_right_a):
+            first_part = first_part + pick(piece.reshape(8, 2, 64, LANES), which, 1).astype(f32)
+        for piece in (from_left_b, from_right_b):
+            second_part = second_part + pick(piece.reshape(8, 2, 64, LANES), which, 1).astype(f32)
+        return jnp.concatenate([first_part, second_part], 0).reshape(1024, LANES)
+
+    got = swap_halves(half_sum(1 - half).astype(bf16))
     mine, other, grads = head_grads(
-        core, act_rows, attn_rows, o_own, dq_own, keep.reshape(1024, LANES), got.reshape(1024, LANES), half_cos, half_sin
-    )
-    grads_back = to_owners(after(grads, small_piece).reshape(16, 64, 256))
+        core, act_rows, attn_rows, o_own.reshape(1024, LANES), dq_own, half_sum(half), got, half_cos, half_sin
+    )
+    other = swap_cores(other).reshape(2, 384, 256)
+    mine = mine.reshape(2, 384, 256)
+    give = (pick(mine, 1 - half).astype(f32) + pick(other, 1 - half).astype(f32)).astype(bf16)
+    keep = pick(mine, half).astype(f32) + pick(other, half).astype(f32)
+    grads_back = to_owners(after(grads, returned).reshape(16, 64, 256))
+    total = (keep + swap_halves(give).astype(f32)).astype(bf16)
+    total = (total.astype(f32) + neighbour(total).astype(f32)).astype(bf16)
+    total = (total.astype(f32) + mirror(total).astype(f32)).astype(bf16)
+    block = after(jnp.broadcast_to(total[None], (16, 384, 256)), grads_back, small)
+    whole = to_owners(block)
+
     grad_input = finish(grads_back, x, norm1_gain, w_query, w_key, w_value, state)
-    grad_down = lax.psum_scatter(
-        after(ddown, got), ("context", "dp"), scatter_dimension=1, tiled=True
-    ).astype(f32)
-
-    total = (mine.astype(f32) + swap_cores(other).astype(f32)).astype(bf16).reshape(2, 384, 256)
-    total = pick(total, half).astype(f32) + swap_halves(pick(total, 1 - half)).astype(f32)
-    block = gather_context(sum_context(total.astype(bf16), context), context)
-    block = jnp.concatenate([block, small_sum.astype(bf16), jnp.zeros((8, 256), bf16)], 0)
-    block, grad_input, block_out, grad_gate_up = lax.optimization_barrier(
-        (block, grad_input, block_out, grad_gate_up)
-    )
-    whole = to_owners(jnp.broadcast_to(block[None], (16, *block.shape)))
-    whole_other = swap_cores(whole)
-    dwq, dwk, dwv, dwo, norm1_sum = assemble(core, whole, whole_other, w_query, w_key, w_value)
-    smalls = jnp.stack([whole[:, 384:392], whole_other[:, 384:392]], 0).reshape(2, 128, 256)
-    smalls = jnp.concatenate([pick(smalls, core_index), pick(smalls, 1 - core_index)], 0)
-    smalls = smalls.reshape(4, 64, 256).transpose(1, 0, 2).reshape(64, D).astype(f32)
+    block_out = hidden + branch_scale * dot(spot, returned.reshape(SLOTS, D))
+    grad_down = lax.psum_scatter(after(ddown, got), ("context", "dp"), scatter_dimension=1, tiled=True).astype(f32)
+    whole, grad_input, block_out, grad_gate_up = lax.optimization_barrier(
+        (whole, grad_input, block_out, grad_gate_up)
+    )
+    dwq, dwk, dwv, dwo, norm1_grad = assemble(
+        core, whole, swap_cores(whole), w_query, w_key, w_value, norm1_gain
+    )
     return (
         block_out.reshape(1, 1, TOK, D),
         grad_input.reshape(1, 1, TOK, D),
-        norm1_sum[:, 0] / norm1_gain,
-        smalls[EXPERTS],
+        norm1_grad[0],
+        small[EXPERTS],
         dwq,
         dwk,
         dwv,
         dwo,
-        smalls[:EXPERTS].T,
+        small[:EXPERTS].T,
         grad_gate_up,
         grad_down,
     )

time: 484 us -> 532 us (1.099)
  the two profiles are of different devices: /device:TPU:69 before, /device:TPU:27 now
where the time goes in v4:
time: 532 us; the launch traced here: 522 us
  waiting for transfers between devices  199 us (37%)
  Pallas kernels  129 us (24%)
  starting transfers between devices  95.3 us (18%)
  blocking collectives  34.6 us (7%)
  other arithmetic  25.3 us (5%)
  local copies, waits for them, and re-layouts  18.8 us (4%)
  between operations  14.5 us (3%)
  matrix products  5.59 us (1%)
    all_to_all x11, starting transfers between devices, to_owners(): return lax.all_to_all(x, 'expert', split_axis=0, concat_axis=0, tiled=True)  72.4 us
    psum x1, waiting for transfers between devices, local(): lax.psum(jnp.concatenate([router_grad[0] + router_grad[1], norm2_grad], 0...  47 us
    all_to_all x11, waiting for transfers between devices, to_owners(): return lax.all_to_all(x, 'expert', split_axis=0, concat_axis=0, tiled=True)  44.1 us
    all_to_all x1, blocking collectives, to_owners(): return lax.all_to_all(x, 'expert', split_axis=0, concat_axis=0, tiled=True)  34.6 us
    pallas_call x1, Pallas kernels, attend_backward(): call(backward_kernel, (struct((8, 64, LANES), bf16), struct((8, 64, LANES...  31.8 us
    pallas_call x1, Pallas kernels, attend_forward(): call(forward_kernel, (struct((2, CHUNK, LANES), f32), struct((8, 64, LANE...  26.8 us
    reduce_scatter x1, waiting for transfers between devices, local(): lax.psum_scatter(after(ddown, got), ('context', 'dp'), scatter_dimension=...  25.5 us
    ppermute x12, waiting for transfers between devices, shift(): return lax.ppermute(x, 'context', [(i, (i + by) % 4) for i in range(4)])  23.7 us
  transfers between devices with their start and end apart: 38, of which 22 were waited for; matrix products, arithmetic and copies ran while one was open for 8% of the time, Pallas kernels for 22%

profile of v4, /device:TPU:27, one launch (start us, length us, event | category | flops | bytes accessed | tf_op | source)
XLA Modules:
  0.0 521.9 jit_solution(14533732011473988246)
XLA Ops:
  13.4 7.8 %all-to-all-start = ((bf16[16,128,128]{2,1,0:T(8,128)(2,1)}), bf16[16,128,128]{2,1,0:T(8,128)(2,1)S(1)}, u32[]{:S(2)}, u32[]{:S(2)}) async-start(bf16[16,128,128]{2,1,0:T(8,128)(2,1)} %get-tuple-element.81), calls=%async_computation | async-start | bytes 1048576 | tf_op jit(solution)/shard_map/all_to_all | solution.py:604
  21.2 8.3 %all-to-all-done.own_ref = bf16[16,128,128]{2,1,0:T(8,128)(2,1)S(1)} async-done(((bf16[16,128,128]{2,1,0:T(8,128)(2,1)}), bf16[16,128,128]{2,1,0:T(8,128)(2,1)S(1)}, u32[]{:S(2)}, u32[]{:S(2)}) %all-to-all-start) | async-done | bytes 524320 | tf_op jit(solution)/shard_map/all_to_all | solution.py:604
  60.6 6.4 %collective-permute-done.3.far_a_ref = bf16[8,128,128]{2,1,0:T(8,128)(2,1)S(1)} collective-permute-done((bf16[8,128,128]{2,1,0:T(8,128)(2,1)S(1)}, bf16[8,128,128]{2,1,0:T(8,128)(2,1)S(1)}, u32[]{:S(2)}, u32[]{:S(2)}) %collective-permute-start.3) | collective-permute-done | bytes 262176 | tf_op jit(solution)/shard_map/ppermute | solution.py:616
  77.9 26.8 %attend.1 = (f32[2,512,128]{2,1,0:T(8,128)}, bf16[8,64,128]{2,1,0:T(8,128)(2,1)}, bf16[8,64,128]{2,1,0:T(8,128)(2,1)}, f32[4,8,512]{2,1,0:T(8,128)}, bf16[8192,128]{1,0:T(8,128)(2,1)}) custom-call(s32[2]{0:T(128)} %pad_add_fusion.place_ref, bf16[16,64,128]{2,1,0:T(8,128)(2,1)} %copy-done.10, bf16[8,64,128]{2,1,0:T(8,128)(2,1)} %copy-done.22, ...), custom_call_target="tpu_custom_call" | custom-call | flops 20000000000 | bytes 4000000 | tf_op jit(solution)/shard_map/attend/pallas_call | solution.py:184
  110.7 6.6 %all-to-all-start.3 = ((bf16[16,64,128]{2,1,0:T(8,128)(2,1)}), bf16[16,64,128]{2,1,0:T(8,128)(2,1)}, u32[]{:S(2)}, u32[]{:S(2)}) async-start(bf16[16,64,128]{2,1,0:T(8,128)(2,1)} %constant_dynamic-update-slice_fusion), calls=%async_computation.3 | async-start | bytes 524288 | tf_op jit(solution)/shard_map/all_to_all | solution.py:604
  130.1 34.6 %all_to_all.60.x_ref = bf16[16,2,48,1024]{3,2,1,0:T(8,128)(2,1)} all-to-all(bf16[16,2,48,1024]{3,2,1,0:T(8,128)(2,1)} %bitcast.107), channel_id=1, replica_groups=mesh['expert'=16,'context'=4,'dp'=2] {'expert'}, dimensions={0} | all-to-all | bytes 6291456 | tf_op jit(solution)/shard_map/all_to_all | solution.py:604
  164.7 5.8 %all-to-all-start.5 = ((bf16[16,64,1024]{2,1,0:T(8,128)(2,1)}), bf16[16,64,1024]{2,1,0:T(8,128)(2,1)S(1)}, u32[]{:S(2)}, u32[]{:S(2)}) async-start(bf16[16,64,1024]{2,1,0:T(8,128)(2,1)} %get-tuple-element.89), calls=%async_computation.5 | async-start | bytes 4194304 | tf_op jit(solution)/shard_map/all_to_all | solution.py:604
  171.4 16.0 %experts.1 = (bf16[16,2,48,1024]{3,2,1,0:T(8,128)(2,1)}, bf16[2,768,512]{2,1,0:T(8,128)(2,1)}, bf16[2,768,1024]{2,1,0:T(8,128)(2,1)}, f32[2,768,1]{2,1,0:T(8,128)}, f32[2,768,32]{2,1,0:T(8,128)}) custom-call(s32[1]{0:T(128)} %bitcast.12.first_ref, bf16[16,2,48,1024]{3,2,1,0:T(8,128)(2,1)} %all_to_all.60.x_ref, f32[2,768,512]{2,1,0:T(8,128)} %raw.1.raw_ref, ...), custom_call_target="tpu_custom_call" | custom-call | flops 8053063680 | bytes 20000000 | tf_op jit(solution)/shard_map/experts/pallas_call | solution.py:364
  188.9 8.2 %all-to-all-start.6 = ((bf16[16,2,48,1024]{3,2,1,0:T(8,128)(2,1)}), bf16[16,2,48,1024]{3,2,1,0:T(8,128)(2,1)S(1)}, u32[]{:S(2)}, u32[]{:S(2)}) async-start(bf16[16,2,48,1024]{3,2,1,0:T(8,128)(2,1)} %get-tuple-element.92), calls=%async_computation.6 | async-start | bytes 6291456 | tf_op jit(solution)/shard_map/all_to_all | solution.py:604
  197.1 13.4 %expert_grads.1 = (bf16[16,2,48,1024]{3,2,1,0:T(8,128)(2,1)}, bf16[2,1024,1024]{2,1,0:T(8,128)(2,1)}, bf16[2,512,1024]{2,1,0:T(8,128)(2,1)}, f32[2,32,1024]{2,1,0:T(8,128)}) custom-call(bf16[16,2,48,1024]{3,2,1,0:T(8,128)(2,1)} %all_to_all.60.x_ref, bf16[16,2,48,1024]{3,2,1,0:T(8,128)(2,1)} %copy-done, f32[2,768,1]{2,1,0:T(8,128)} %get-tuple-element.93.gate_ref, ...), custom_call_target="tpu_custom_call" | custom-call | flops 6442450944 | bytes 24000000 | tf_op jit(solution)/shard_map/expert_grads/pallas_call | solution.py:404
  210.5 16.5 %all-to-all-done.6 = bf16[16,2,48,1024]{3,2,1,0:T(8,128)(2,1)S(1)} async-done(((bf16[16,2,48,1024]{3,2,1,0:T(8,128)(2,1)}), bf16[16,2,48,1024]{3,2,1,0:T(8,128)(2,1)S(1)}, u32[]{:S(2)}, u32[]{:S(2)}) %all-to-all-start.6) | async-done | bytes 3145760 | tf_op jit(solution)/shard_map/all_to_all | solution.py:604
  228.7 5.5 %turn_back.1 = (f32[128,1024]{1,0:T(8,128)}, bf16[16,64,1024]{2,1,0:T(8,128)(2,1)}, bf16[16,64,128]{2,1,0:T(8,128)(2,1)}, f32[8,1024]{1,0:T(8,128)}) custom-call(bf16[1536,1024]{1,0:T(8,128)(2,1)} %bitcast.104, bf16[128,1536]{1,0:T(8,128)(2,1)} %get-tuple-element.155.spot_ref, f32[128,1024]{1,0:T(8,128)} %get-tuple-element.99.hidden_ref, ...), custom_call_target="tpu_custom_call" | custom-call | flops 1342177280 | bytes 8000000 | tf_op jit(solution)/shard_map/turn_back/pallas_call | solution.py:442
  234.2 7.6 %all-to-all-start.7 = ((bf16[16,64,128]{2,1,0:T(8,128)(2,1)}), bf16[16,64,128]{2,1,0:T(8,128)(2,1)S(1)}, u32[]{:S(2)}, u32[]{:S(2)}) async-start(bf16[16,64,128]{2,1,0:T(8,128)(2,1)} %get-tuple-element.100), calls=%async_computation.7 | async-start | bytes 524288 | tf_op jit(solution)/shard_map/all_to_all | solution.py:604
  256.0 31.8 %attend_back.1 = (bf16[8,64,128]{2,1,0:T(8,128)(2,1)}, bf16[8,64,128]{2,1,0:T(8,128)(2,1)}, f32[2048,128]{1,0:T(8,128)}, bf16[1024,128]{1,0:T(8,128)(2,1)}, bf16...) custom-call(s32[2]{0:T(128)} %pad_add_fusion.place_ref, ...), custom_call_target="tpu_custom_call" | custom-call | flops 49999998976 | bytes 8000000 | tf_op jit(solution)/shard_map/attend_back/pallas_call | solution.py:268
  293.8 6.7 %all-to-all-start.9 = ((bf16[16,2,48,1024]{3,2,1,0:T(8,128)(2,1)}), bf16[16,2,48,1024]{3,2,1,0:T(8,128)(2,1)S(1)}, u32[]{:S(2)}, u32[]{:S(2)}) async-start(bf16[16,2,48,1024]{3,2,1,0:T(8,128)(2,1)} %get-tuple-element.129), calls=%async_computation.9 | async-start | bytes 6291456 | tf_op jit(solution)/shard_map/all_to_all | solution.py:604
  326.4 15.9 %collective-permute-done.16.other_in = bf16[1024,128]{1,0:T(8,128)(2,1)} collective-permute-done((bf16[1024,128]{1,0:T(8,128)(2,1)}, bf16[1024,128]{1,0:T(8,128)(2,1)}, u32[]{:S(2)}, u32[]{:S(2)}) %collective-permute-start.16) | collective-permute-done | bytes 262176 | tf_op jit(solution)/shard_map/ppermute | solution.py:624
  342.3 5.6 %head_grads.1 = (bf16[768,256]{1,0:T(8,128)(2,1)}, bf16[768,256]{1,0:T(8,128)(2,1)}, bf16[1024,256]{1,0:T(8,128)(2,1)}) custom-call(s32[1]{0:T(128)} %bitcast.core_ref, bf16[1024,1024]{1,0:T(8,128)(2,1)} %bitcast.105, bf16[1024,1024]{1,0:T(8,128)(2,1)} %bitcast.106, bf16[1024,128]{1,0:T(8,128)(2,1)} %bitcast.15.o_ref, bf16[1024,128]{1,0:T(8,128)(2,1)} %bitcast.115, ...), custom_call_target="tpu_custom_call" | custom-call | flops 1073741824 | bytes 8000000 | tf_op jit(solution)/shard_map/head_grads/pallas_call | solution.py:486
  352.6 5.8 %collective-permute-done.18 = bf16[384,256]{1,0:T(8,128)(2,1)S(1)} collective-permute-done((bf16[384,256]{1,0:T(8,128)(2,1)S(1)}, bf16[384,256]{1,0:T(8,128)(2,1)S(1)}, u32[]{:S(2)}, u32[]{:S(2)}) %collective-permute-start.18) | collective-permute-done | bytes 196640 | tf_op jit(solution)/shard_map/ppermute | solution.py:624
  359.5 8.8 %all-to-all-start.10 = ((bf16[16,64,256]{2,1,0:T(8,128)(2,1)}), bf16[16,64,256]{2,1,0:T(8,128)(2,1)}, u32[]{:S(2)}, u32[]{:S(2)}) async-start(bf16[16,64,256]{2,1,0:T(8,128)(2,1)} %bitcast.118), calls=%async_computation.10 | async-start | bytes 1048576 | tf_op jit(solution)/shard_map/all_to_all | solution.py:604
  376.4 47.0 %all-reduce.2.cloned.1.call-done = f32[40,1024]{1,0:T(8,128)} async-done(((f32[40,1024]{1,0:T(8,128)}), f32[40,1024]{1,0:T(8,128)}) %all-reduce.2.cloned.1.call-update) | async-done | bytes 163856 | tf_op jit(solution)/shard_map/psum | solution.py:701
  439.0 23.6 %reduce-scatter.3.cloned.1.call-done = bf16[2,128,1024]{2,1,0:T(8,128)(2,1)} async-done(((bf16[2,1024,1024]{2,1,0:T(8,128)(2,1)}), bf16[2,128,1024]{2,1,0:T(8,128)(2,1)}) %reduce-scatter.3.cloned.1.call-update) | async-done | bytes 524304 | tf_op jit(solution)/shard_map/reduce_scatter | solution.py:704
  464.7 8.7 %all-to-all-done.11.own_ref = bf16[16,384,256]{2,1,0:T(8,128)(2,1)} async-done(((bf16[16,384,256]{2,1,0:T(8,128)(2,1)}), bf16[16,384,256]{2,1,0:T(8,128)(2,1)}, u32[]{:S(2)}, u32[]{:S(2)}) %all-to-all-start.11) | async-done | bytes 3145760 | tf_op jit(solution)/shard_map/all_to_all | solution.py:604
  475.4 25.5 %reduce-scatter.5.cloned.1.call-done = bf16[2,64,1024]{2,1,0:T(8,128)(2,1)} async-done(((bf16[2,512,1024]{2,1,0:T(8,128)(2,1)}), bf16[2,64,1024]{2,1,0:T(8,128)(2,1)}) %reduce-scatter.5.cloned.1.call-update) | async-done | bytes 262160 | tf_op jit(solution)/shard_map/reduce_scatter | solution.py:748
  504.4 10.6 %assemble.1 = (f32[1024,1024]{1,0:T(8,128)}, f32[1024,512]{1,0:T(8,128)}, f32[1024,512]{1,0:T(8,128)}, f32[1024,1024]{1,0:T(8,128)}, f32[1,1024]{1,0:T(1,128)}) custom-call(s32[1]{0:T(128)} %bitcast.core_ref, bf16[16,384,256]{2,1,0:T(8,128)(2,1)} %all-to-all-done.11.own_ref, bf16[16,384,256]{2,1,0:T(8,128)(2,1)} %copy-done.4, bf16[1024,1024]{1,0:T(8,128)(2,1)} %wq_ref.5, ...), custom_call_target="tpu_custom_call" | custom-call | flops 1000000 | bytes 22000000 | tf_op jit(solution)/shard_map/assemble/pallas_call | solution.py:582
  (161 shorter events, 153.9 us)
Async XLA Ops:
  7.2 113.0 %all-gather.3.cloned.1.call-start = ((), (), s32[]{:S(2)}) async-start(), calls=%async_computation.14 | async-start | bytes 2359296 | tf_op jit(solution)/shard_map/all_gather | solution.py:674
  13.4 16.1 %all-to-all-start = ((bf16[16,128,128]{2,1,0:T(8,128)(2,1)}), bf16[16,128,128]{2,1,0:T(8,128)(2,1)S(1)}, u32[]{:S(2)}, u32[]{:S(2)}) async-start(bf16[16,128,128]{2,1,0:T(8,128)(2,1)} %get-tuple-element.81), calls=%async_computation | async-start | bytes 1048576 | tf_op jit(solution)/shard_map/all_to_all | solution.py:604
  29.5 11.4 %all-to-all-start.1 = ((bf16[16,64,128]{2,1,0:T(8,128)(2,1)}), bf16[16,64,128]{2,1,0:T(8,128)(2,1)S(1)}, u32[]{:S(2)}, u32[]{:S(2)}) async-start(bf16[16,64,128]{2,1,0:T(8,128)(2,1)} %get-tuple-element.82), calls=%async_computation.1 | async-start | bytes 524288 | tf_op jit(solution)/shard_map/all_to_all | solution.py:604
  46.7 58.0 %all-to-all-start.2 = ((bf16[16,2,48,1024]{3,2,1,0:T(8,128)(2,1)}), bf16[16,2,48,1024]{3,2,1,0:T(8,128)(2,1)S(1)}, u32[]{:S(2)}, u32[]{:S(2)}) async-start(bf16[16,2,48,1024]{3,2,1,0:T(8,128)(2,1)} %bitcast.7), calls=%async_computation.2 | async-start | bytes 6291456 | tf_op jit(solution)/shard_map/all_to_all | solution.py:604
  51.8 119.7 %all-gather.5.cloned.1.call-start = ((), (), s32[]{:S(2)}) async-start(), calls=%async_computation.15 | async-start | bytes 4718592 | tf_op jit(solution)/shard_map/all_gather | solution.py:673
  110.7 14.5 %all-to-all-start.3 = ((bf16[16,64,128]{2,1,0:T(8,128)(2,1)}), bf16[16,64,128]{2,1,0:T(8,128)(2,1)}, u32[]{:S(2)}, u32[]{:S(2)}) async-start(bf16[16,64,128]{2,1,0:T(8,128)(2,1)} %constant_dynamic-update-slice_fusion), calls=%async_computation.3 | async-start | bytes 524288 | tf_op jit(solution)/shard_map/all_to_all | solution.py:604
  164.7 22.9 %all-to-all-start.5 = ((bf16[16,64,1024]{2,1,0:T(8,128)(2,1)}), bf16[16,64,1024]{2,1,0:T(8,128)(2,1)S(1)}, u32[]{:S(2)}, u32[]{:S(2)}) async-start(bf16[16,64,1024]{2,1,0:T(8,128)(2,1)} %get-tuple-element.89), calls=%async_computation.5 | async-start | bytes 4194304 | tf_op jit(solution)/shard_map/all_to_all | solution.py:604
  188.9 38.1 %all-to-all-start.6 = ((bf16[16,2,48,1024]{3,2,1,0:T(8,128)(2,1)}), bf16[16,2,48,1024]{3,2,1,0:T(8,128)(2,1)S(1)}, u32[]{:S(2)}, u32[]{:S(2)}) async-start(bf16[16,2,48,1024]{3,2,1,0:T(8,128)(2,1)} %get-tuple-element.92), calls=%async_computation.6 | async-start | bytes 6291456 | tf_op jit(solution)/shard_map/all_to_all | solution.py:604
  234.2 13.6 %all-to-all-start.7 = ((bf16[16,64,128]{2,1,0:T(8,128)(2,1)}), bf16[16,64,128]{2,1,0:T(8,128)(2,1)S(1)}, u32[]{:S(2)}, u32[]{:S(2)}) async-start(bf16[16,64,128]{2,1,0:T(8,128)(2,1)} %get-tuple-element.100), calls=%async_computation.7 | async-start | bytes 524288 | tf_op jit(solution)/shard_map/all_to_all | solution.py:604
  241.8 181.6 %all-reduce.2.cloned.1.call-start = ((), (), s32[]{:S(2)}) async-start(), calls=%async_computation.16 | async-start | bytes 327680 | tf_op jit(solution)/shard_map/psum | solution.py:701
  249.8 38.1 %all-to-all-start.8 = ((bf16[16,64,1024]{2,1,0:T(8,128)(2,1)}), bf16[16,64,1024]{2,1,0:T(8,128)(2,1)S(1)}, u32[]{:S(2)}, u32[]{:S(2)}) async-start(bf16[16,64,1024]{2,1,0:T(8,128)(2,1)} %get-tuple-element.114), calls=%async_computation.8 | async-start | bytes 4194304 | tf_op jit(solution)/shard_map/all_to_all | solution.py:604
  254.8 207.8 %reduce-scatter.3.cloned.1.call-start = ((), (), s32[]{:S(2)}) async-start(), calls=%async_computation.17 | async-start | bytes 4718592 | tf_op jit(solution)/shard_map/reduce_scatter | solution.py:704
  290.1 15.8 %collective-permute-start.14 = (bf16[1024,128]{1,0:T(8,128)(2,1)}, bf16[1024,128]{1,0:T(8,128)(2,1)}, u32[]{:S(2)}, u32[]{:S(2)}) collective-permute-start(bf16[1024,128]{1,0:T(8,128)(2,1)} %get-tuple-element.124), channel_id=1, source_target_pairs={{0,6},{2,0},{4,2},{6,4},{1,7},{3,1},{5,3},{7,5},{8,14},{10,8},{12,... | collective-permute-start | bytes 786440 | tf_op jit(solution)/shard_map/ppermute | solution.py:616
  290.1 17.0 %collective-permute-start.10 = (bf16[1024,128]{1,0:T(8,128)(2,1)}, bf16[1024,128]{1,0:T(8,128)(2,1)}, u32[]{:S(2)}, u32[]{:S(2)}) collective-permute-start(bf16[1024,128]{1,0:T(8,128)(2,1)} %get-tuple-element.120), channel_id=1, source_target_pairs={{0,2},{2,4},{4,6},{6,0},{1,3},{3,5},{5,7},{7,1},{8,10},{10,12},{12... | collective-permute-start | bytes 786440 | tf_op jit(solution)/shard_map/ppermute | solution.py:616
  293.8 65.7 %all-to-all-start.9 = ((bf16[16,2,48,1024]{3,2,1,0:T(8,128)(2,1)}), bf16[16,2,48,1024]{3,2,1,0:T(8,128)(2,1)S(1)}, u32[]{:S(2)}, u32[]{:S(2)}) async-start(bf16[16,2,48,1024]{3,2,1,0:T(8,128)(2,1)} %get-tuple-element.129), calls=%async_computation.9 | async-start | bytes 6291456 | tf_op jit(solution)/shard_map/all_to_all | solution.py:604
  303.7 8.9 %collective-permute-start.13 = (bf16[1024,128]{1,0:T(8,128)(2,1)}, bf16[1024,128]{1,0:T(8,128)(2,1)S(1)}, u32[]{:S(2)}, u32[]{:S(2)}) collective-permute-start(bf16[1024,128]{1,0:T(8,128)(2,1)} %get-tuple-element.122), channel_id=1, source_target_pairs={{0,2},{2,4},{4,6},{6,0},{1,3},{3,5},{5,7},{7,1},{8,10},{10,12},{12... | collective-permute-start | bytes 786440 | tf_op jit(solution)/shard_map/ppermute | solution.py:616
  305.9 12.8 %collective-permute-start.12 = (bf16[1024,128]{1,0:T(8,128)(2,1)}, bf16[1024,128]{1,0:T(8,128)(2,1)S(1)}, u32[]{:S(2)}, u32[]{:S(2)}) collective-permute-start(bf16[1024,128]{1,0:T(8,128)(2,1)} %get-tuple-element.121), channel_id=1, source_target_pairs={{0,6},{2,0},{4,2},{6,4},{1,7},{3,1},{5,3},{7,5},{8,14},{10,8},{12,... | collective-permute-start | bytes 786440 | tf_op jit(solution)/shard_map/ppermute | solution.py:616
  307.0 10.9 %collective-permute-start.15 = (bf16[1024,128]{1,0:T(8,128)(2,1)S(1)}, bf16[1024,128]{1,0:T(8,128)(2,1)S(1)}, u32[]{:S(2)}, u32[]{:S(2)}) collective-permute-start(bf16[1024,128]{1,0:T(8,128)(2,1)S(1)} %add_convert_fusion), channel_id=1, source_target_pairs={{0,6},{2,0},{4,2},{6,4},{1,7},{3,1},{5,3},{7,5},{8,14},{10,8},{12,... | collective-permute-start | bytes 786440 | tf_op jit(solution)/shard_map/ppermute | solution.py:616
  308.3 10.4 %collective-permute-start.11 = (bf16[1024,128]{1,0:T(8,128)(2,1)S(1)}, bf16[1024,128]{1,0:T(8,128)(2,1)S(1)}, u32[]{:S(2)}, u32[]{:S(2)}) collective-permute-start(bf16[1024,128]{1,0:T(8,128)(2,1)S(1)} %add_convert_fusion.1), channel_id=1, source_target_pairs={{0,2},{2,4},{4,6},{6,0},{1,3},{3,5},{5,7},{7,1},{8,10},{10,12},{12... | collective-permute-start | bytes 786440 | tf_op jit(solution)/shard_map/ppermute | solution.py:616
  320.3 22.0 %collective-permute-start.16 = (bf16[1024,128]{1,0:T(8,128)(2,1)}, bf16[1024,128]{1,0:T(8,128)(2,1)}, u32[]{:S(2)}, u32[]{:S(2)}) collective-permute-start(bf16[1024,128]{1,0:T(8,128)(2,1)} %bitcast.28), channel_id=1, source_target_pairs={{0,8},{8,0},{16,24},{24,16},{32,40},{40,32},{48,56},{56,48},{64,72... | collective-permute-start | bytes 786440 | tf_op jit(solution)/shard_map/ppermute | solution.py:624
  359.5 63.9 %all-to-all-start.10 = ((bf16[16,64,256]{2,1,0:T(8,128)(2,1)}), bf16[16,64,256]{2,1,0:T(8,128)(2,1)}, u32[]{:S(2)}, u32[]{:S(2)}) async-start(bf16[16,64,256]{2,1,0:T(8,128)(2,1)} %bitcast.118), calls=%async_computation.10 | async-start | bytes 1048576 | tf_op jit(solution)/shard_map/all_to_all | solution.py:604
  425.4 48.1 %all-to-all-start.11 = ((bf16[16,384,256]{2,1,0:T(8,128)(2,1)}), bf16[16,384,256]{2,1,0:T(8,128)(2,1)}, u32[]{:S(2)}, u32[]{:S(2)}) async-start(bf16[16,384,256]{2,1,0:T(8,128)(2,1)} %broadcast_in_dim.7), calls=%async_computation.11 | async-start | bytes 6291456 | tf_op jit(solution)/shard_map/all_to_all | solution.py:604
  430.6 70.2 %reduce-scatter.5.cloned.1.call-start = ((), (), s32[]{:S(2)}) async-start(), calls=%async_computation.18 | async-start | bytes 2359296 | tf_op jit(solution)/shard_map/reduce_scatter | solution.py:748
  473.5 29.2 %collective-permute-start.21 = (bf16[16,384,256]{2,1,0:T(8,128)(2,1)}, bf16[16,384,256]{2,1,0:T(8,128)(2,1)S(1)}, u32[]{:S(2)}, u32[]{:S(2)}) collective-permute-start(bf16[16,384,256]{2,1,0:T(8,128)(2,1)} %all-to-all-done.11.own_ref), channel_id=1, source_target_pairs={{0,1},{1,0},{2,3},{3,2},{4,5},{5,4},{6,7},{7,6},{8,9},{9,8},{10,11... | collective-permute-start | bytes 9437192 | tf_op jit(solution)/shard_map/ppermute | solution.py:612
  (40 other events, 361.3 us)
Sparse Core Ops, SparseCore 0:
  9.7 26.3 all-gather.2
  68.6 39.7 all-gather.4
  249.9 173.4 all-reduce.1
  426.4 36.1 reduce-scatter.2
  465.5 35.3 reduce-scatter.4

commit v5 on v4

--- a/solution.py
+++ b/solution.py
@@ -115,7 +115,7 @@
 
 
 def forward_kernel(
-    place_ref, q_ref, q_far_ref, own_ref, left_a_ref, left_b_ref, far_a_ref, far_b_ref, right_a_ref, right_b_ref,
+    place_ref, q_ref, q_far_ref, own_ref, left_ref, far_a_ref, far_b_ref, right_ref,
     o_ref, low_ref, low_far_ref, lse_ref, kv_ref, qm_ref, top_ref, acc_ref,
 ):
     tile = 1024
@@ -124,16 +124,14 @@
 
     def put(back, part, ref):
         start = lax.rem(context + 4 - back, 4) * BLOCK + part * (BLOCK // 2)
-        rows = ref.shape[0] * TOK
-        kv_ref[pl.ds(pl.multiple_of(start, BLOCK // 2), rows), :] = ref[...].reshape(rows, LANES)
+        rows = ref.shape[0]
+        kv_ref[pl.ds(pl.multiple_of(start, BLOCK // 2), rows), :] = ref[...]
 
     put(0, 0, own_ref)
-    put(1, 0, left_a_ref)
-    put(1, 1, left_b_ref)
+    put(1, 0, left_ref)
     put(2, 0, far_a_ref)
     put(2, 1, far_b_ref)
-    put(3, 0, right_a_ref)
-    put(3, 1, right_b_ref)
+    put(3, 0, right_ref)
     left = lane_index((CHUNK, LANES)) < HEAD_DIM
     left_keys = lane_index((tile, LANES)) < HEAD_DIM
     for chunk in range(2):
@@ -192,7 +190,7 @@
         ),
         2e10,
         4e6,
-        in_specs=[smem] + [vmem] * 9,
+        in_specs=[smem] + [vmem] * 7,
         out_specs=(vmem,) * 5,
         scratch_shapes=[
             pltpu.VMEM((2, CHUNK, LANES), bf16),
@@ -419,7 +417,7 @@
 
 
 def turn_back_kernel(
-    back_ref, spot_ref, hidden_ref, gain_ref, top_ref, wo_ref, state_ref, attn_ref, send_ref, norm_ref
+    back_ref, spot_ref, hidden_ref, gain_ref, top_ref, wo_ref, router_ref, state_ref, attn_ref, send_ref
 ):
     grad = dot(spot_ref[...], back_ref[...])
     hidden = hidden_ref[...]
@@ -429,28 +427,35 @@
     state = top_ref[...].astype(f32) + inverse * (scaled - normed * jnp.mean(scaled * normed, axis=-1, keepdims=True))
     state_ref[...] = state
     attn = (branch_scale * state).astype(bf16)
+    router = router_ref[0] + router_ref[1]
+    norm = jnp.sum(grad * normed, axis=0, keepdims=True)
     for e in range(16):
-        attn_ref[e] = attn[64 * (e % 2) : 64 * (e % 2) + 64]
+        attn_ref[e, :64] = attn[64 * (e % 2) : 64 * (e % 2) + 64]
+        if e < 8:
+            extra = jnp.concatenate([router[4 * e : 4 * e + 4], jnp.zeros((12, D), f32)], axis=0)
+        elif e == 8:
+            extra = jnp.concatenate([norm, jnp.zeros((15, D), f32)], axis=0)
+        else:
+            extra = jnp.zeros((16, D), f32)
+        attn_ref[e, 64:] = extra.astype(bf16)
     attended = dot_rows(attn, wo_ref[...]).astype(bf16)
     for j in range(PAIRS):
         for h in range(2):
             send_ref[2 * j + h] = attended[h * 64 : h * 64 + 64, j * LANES : (j + 1) * LANES]
-    norm_ref[...] = jnp.broadcast_to(jnp.sum(grad * normed, axis=0, keepdims=True), (8, D))
-
-
-def turn_back(back, spot, hidden, gain, top, wo):
+
+
+def turn_back(back, spot, hidden, gain, top, wo, router):
     return call(
         turn_back_kernel,
         (
             struct((TOK, D), f32),
-            struct((16, 64, D), bf16),
+            struct((16, 80, D), bf16),
             struct((16, TOK // 2, LANES), bf16),
-            struct((8, D), f32),
         ),
         2 * 256 * D * (D + SLOTS),
         8e6,
         name="turn_back",
-    )(back, spot, hidden, gain.reshape(1, D), top, wo)
+    )(back, spot, hidden, gain.reshape(1, D), top, wo, router)
 
 
 def unturn(v, cos, sin, first):
@@ -458,41 +463,105 @@
     return v * cos + jnp.where(first, pltpu.roll(scaled, LANES - 32, 1), pltpu.roll(scaled, 32, 1))
 
 
-def head_kernel(
-    core_ref, act_ref, attn_ref, o_ref, dq_ref, mine_in, other_in, cos_ref, sin_ref, mine_ref, other_ref, grads_ref,
-    all_ref,
+def merge_kernel(
+    place_ref, d0_ref, left_a_ref, left_b_ref, right_a_ref, right_b_ref, keep_ref, give_ref, sum_ref
 ):
-    rows = 1024
-    lane = lane_index((rows, LANES))
+    half = place_ref[1]
+    for part, left, right in ((0, left_a_ref, right_a_ref), (1, left_b_ref, right_b_ref)):
+        rows = slice(part * 1024, part * 1024 + 1024)
+        total = d0_ref[rows] + left[...].astype(f32) + right[...].astype(f32)
+        sum_ref[8 * part : 8 * part + 8] = total.reshape(8, TOK, LANES)
+    keep_ref[...] = sum_ref[:, pl.ds(pl.multiple_of(half * 64, 64), 64), :]
+    give_ref[...] = sum_ref[:, pl.ds(pl.multiple_of((1 - half) * 64, 64), 64), :].astype(bf16)
+
+
+def merge(place, *pieces):
+    smem = pl.BlockSpec(memory_space=pltpu.SMEM)
+    vmem = pl.BlockSpec(memory_space=pltpu.VMEM)
+    return call(
+        merge_kernel,
+        (struct((16, 64, LANES), f32), struct((16, 64, LANES), bf16)),
+        1e6,
+        3e6,
+        in_specs=[smem] + [vmem] * 5,
+        out_specs=(vmem, vmem),
+        scratch_shapes=[pltpu.VMEM((16, TOK, LANES), f32)],
+        name="merge",
+    )(place, *pieces)
+
+
+def unturn_kernel(dq_ref, dq_far_ref, keep_ref, got_ref, cos_ref, sin_ref, grads_ref):
+    lane = lane_index((512, LANES))
     first = lane % HEAD_DIM < HEAD_DIM // 2
-    cos = cos_ref[...]
-    sin = sin_ref[...]
-    grads_ref[:, :LANES] = unturn(dq_ref[...].astype(f32), cos, sin, first).astype(bf16)
-    both = (mine_in[...] + other_in[...].astype(f32)).astype(bf16).astype(f32)
-    grads_ref[:, LANES:] = jnp.where(lane < HEAD_DIM, unturn(both, cos, sin, first), both).astype(bf16)
+    for part, dq in ((0, dq_ref), (1, dq_far_ref)):
+        rows = slice(512 * part, 512 * part + 512)
+        take = slice(8 * part, 8 * part + 8)
+        cos = cos_ref[rows]
+        sin = sin_ref[rows]
+        grads_ref[rows, :LANES] = unturn(dq[...].reshape(512, LANES).astype(f32), cos, sin, first).astype(bf16)
+        both = (keep_ref[take] + got_ref[take].astype(f32)).reshape(512, LANES).astype(bf16).astype(f32)
+        grads_ref[rows, LANES:] = jnp.where(lane < HEAD_DIM, unturn(both, cos, sin, first), both).astype(bf16)
+
+
+def unturn_rows(dq, dq_far, keep, got, cos, sin):
+    return call(unturn_kernel, struct((1024, 256), bf16), 1e6, 3e6, name="unturn")(dq, dq_far, keep, got, cos, sin)
+
+
+def head_kernel(core_ref, act_ref, attn_ref, o_ref, grads_ref, mine_ref, other_ref, all_ref):
     all_ref[:D] = dot_down(act_ref[...], grads_ref[...]).astype(bf16)
-    out = dot_down(o_ref[...], attn_ref[...]).astype(bf16)
+    out = dot_down(o_ref[...], attn_ref[:, :64, :].reshape(1024, D)).astype(bf16)
     for b in range(4):
         all_ref[D + LANES * b : D + LANES * (b + 1)] = out[:, 256 * b : 256 * (b + 1)]
+    extra = attn_ref[0, 64:].astype(f32)
+    for e in range(1, 16):
+        extra = extra + attn_ref[e, 64:].astype(f32)
+    packed = extra[:, :256]
+    for b in range(1, 4):
+        packed = packed + pltpu.roll(extra[:, 256 * b : 256 * (b + 1)], 4 * b, 0)
+    packed = packed.astype(bf16)
     core = core_ref[0]
-    mine_ref[...] = all_ref[pl.ds(pl.multiple_of(core * 768, 768), 768), :]
-    other_ref[...] = all_ref[pl.ds(pl.multiple_of((1 - core) * 768, 768), 768), :]
-
-
-def head_grads(core, act, attn, o, dq, mine, other, cos, sin):
+    for which, out_ref in ((1 - core, other_ref), (core, mine_ref)):
+        out_ref[:768] = all_ref[pl.ds(pl.multiple_of(which * 768, 768), 768), :]
+        out_ref[768:] = packed
+
+
+def head_grads(core, act, attn, o, grads):
     smem = pl.BlockSpec(memory_space=pltpu.SMEM)
     vmem = pl.BlockSpec(memory_space=pltpu.VMEM)
-    half = struct((768, 256), bf16)
+    half = struct((784, 256), bf16)
     return call(
         head_kernel,
-        (half, half, struct((1024, 256), bf16)),
+        (half, half),
         2 * 1024 * 1024 * 512,
         8e6,
-        in_specs=[smem] + [vmem] * 8,
-        out_specs=(vmem,) * 3,
+        in_specs=[smem] + [vmem] * 4,
+        out_specs=(vmem,) * 2,
         scratch_shapes=[pltpu.VMEM((1536, 256), bf16)],
         name="head_grads",
-    )(core, act, attn, o, dq, mine, other, cos, sin)
+    )(core, act, attn, o, grads)
+
+
+def split_kernel(place_ref, mine_ref, other_ref, keep_ref, give_ref):
+    half = place_ref[1]
+    rows = pl.ds(pl.multiple_of(half * 384, 384), 384)
+    keep_ref[:384] = mine_ref[rows, :].astype(f32) + other_ref[rows, :].astype(f32)
+    keep_ref[384:] = mine_ref[768:, :].astype(f32) + other_ref[768:, :].astype(f32)
+    rows = pl.ds(pl.multiple_of((1 - half) * 384, 384), 384)
+    give_ref[...] = (mine_ref[rows, :].astype(f32) + other_ref[rows, :].astype(f32)).astype(bf16)
+
+
+def split_halves(place, mine, other):
+    smem = pl.BlockSpec(memory_space=pltpu.SMEM)
+    vmem = pl.BlockSpec(memory_space=pltpu.VMEM)
+    return call(
+        split_kernel,
+        (struct((400, 256), f32), struct((384, 256), bf16)),
+        1e6,
+        2e6,
+        in_specs=[smem, vmem, vmem],
+        out_specs=(vmem, vmem),
+        name="split",
+    )(place, mine, other)
 
 
 def finish_kernel(grads_ref, x_ref, gain_ref, wq_ref, wk_ref, wv_ref, state_ref, out_ref, flat_ref):
@@ -662,13 +731,11 @@
     core_index = lax.axis_index("dp")
     core = core_index.astype(jnp.int32).reshape(1)
     act_send, q_send, kv_send = project(x, norm1_gain, w_query, w_key, w_value, cos, sin)
-    kv_own = to_owners(kv_send)
-    kv_a, kv_b = kv_own[:8], kv_own[8:]
-    left_a, right_b = shift(kv_a, 1), shift(kv_b, 3)
-    left_b, right_a = shift(kv_b, 1), shift(kv_a, 3)
+    kv_own = to_owners(kv_send).reshape(BLOCK, LANES)
+    kv_left, kv_right = shift(kv_own, 1), shift(kv_own, 3)
     q_own = to_owners(after(q_send, kv_own))
     q_far = mirror(q_own[8:])
-    far_a, far_b = shift(left_a, 1), shift(right_b, 3)
+    far_a, far_b = shift(kv_left[: BLOCK // 2], 1), shift(kv_right[BLOCK // 2 :], 3)
 
     gate_up = lax.all_gather(after(w_gate_up, far_a, far_b), ("context", "dp"), axis=1, tiled=True)
     down = lax.all_gather(w_down, ("context", "dp"), axis=1, tiled=True)
@@ -677,7 +744,7 @@
 
     seat = jnp.stack([context, half]).astype(jnp.int32)
     o, o_low, o_far, lse, kv = attend_forward(
-        seat, q_own, q_far, (kv_own, left_a, left_b, far_a, far_b, right_a, right_b)
+        seat, q_own, q_far, (kv_own, kv_left, far_a, far_b, kv_right)
     )
     o_far = after(o_far, top_rows)
     o_own = jnp.concatenate([o_low, mirror(o_far)], 0)
@@ -694,13 +761,12 @@
     out_rows, dgu, ddown, router_grad = expert_grads(rows, top_rows, gates, logits, expert_hidden, mixed, down)
     back = after(back, dgu)
 
-    state, attn_send, do_send, norm2_grad = turn_back(back.reshape(SLOTS, D), spot, hidden, norm2_gain, top, w_out)
+    state, attn_send, do_send = turn_back(
+        back.reshape(SLOTS, D), spot, hidden, norm2_gain, top, w_out, router_grad
+    )
     do_own = to_owners(do_send)
     do_far = mirror(do_own[8:])
-    attn_rows = to_owners(after(attn_send, do_own)).reshape(1024, D)
-    small = lax.psum(
-        jnp.concatenate([router_grad[0] + router_grad[1], norm2_grad], 0), ("expert", "context", "dp")
-    )
+    attn_rows = to_owners(after(attn_send, do_own))
     grad_gate_up = lax.psum_scatter(
         after(dgu, do_own), ("context", "dp"), scatter_dimension=1, tiled=True
     ).astype(f32)
@@ -713,34 +779,20 @@
     far_a, far_b = shift(d2a, 1), shift(d2b, 3)
     from_left_b, from_right_a = shift(d3b, 1), shift(d1a, 3)
     dq_far = mirror(dq_far)
-    dq_own = jnp.concatenate([dq, dq_far], 0).reshape(1024, LANES)
     returned = to_owners(after(out_rows, dq_far))
     from_left_a = shift((d3a.astype(f32) + far_a.astype(f32)).astype(bf16), 1)
     from_right_b = shift((d1b.astype(f32) + far_b.astype(f32)).astype(bf16), 3)
-    own = d0.reshape(2, 8, 2, 64, LANES)
-
-    def half_sum(which):
-        first_part = pick(own[0], which, 1)
-        second_part = pick(own[1], which, 1)
-        for piece in (from_left_a, from_right_a):
-            first_part = first_part + pick(piece.reshape(8, 2, 64, LANES), which, 1).astype(f32)
-        for piece in (from_left_b, from_right_b):
-            second_part = second_part + pick(piece.reshape(8, 2, 64, LANES), which, 1).astype(f32)
-        return jnp.concatenate([first_part, second_part], 0).reshape(1024, LANES)
-
-    got = swap_halves(half_sum(1 - half).astype(bf16))
-    mine, other, grads = head_grads(
-        core, act_rows, attn_rows, o_own.reshape(1024, LANES), dq_own, half_sum(half), got, half_cos, half_sin
-    )
-    other = swap_cores(other).reshape(2, 384, 256)
-    mine = mine.reshape(2, 384, 256)
-    give = (pick(mine, 1 - half).astype(f32) + pick(other, 1 - half).astype(f32)).astype(bf16)
-    keep = pick(mine, half).astype(f32) + pick(other, half).astype(f32)
+    keep, give = merge(seat, d0, from_left_a, from_left_b, from_right_a, from_right_b)
+    got = swap_halves(give)
+    grads = unturn_rows(dq, dq_far, keep, got, half_cos, half_sin)
+    mine, other = head_grads(core, act_rows, attn_rows, o_own.reshape(1024, LANES), grads)
+    keep, give = split_halves(seat, mine, swap_cores(other))
     grads_back = to_owners(after(grads, returned).reshape(16, 64, 256))
-    total = (keep + swap_halves(give).astype(f32)).astype(bf16)
+    total = keep + jnp.pad(swap_halves(give), ((0, 16), (0, 0))).astype(f32)
+    total = total.astype(bf16)
     total = (total.astype(f32) + neighbour(total).astype(f32)).astype(bf16)
     total = (total.astype(f32) + mirror(total).astype(f32)).astype(bf16)
-    block = after(jnp.broadcast_to(total[None], (16, 384, 256)), grads_back, small)
+    block = after(jnp.broadcast_to(total[None], (16, 400, 256)), grads_back)
     whole = to_owners(block)
 
     grad_input = finish(grads_back, x, norm1_gain, w_query, w_key, w_value, state)
@@ -752,6 +804,7 @@
     dwq, dwk, dwv, dwo, norm1_grad = assemble(
         core, whole, swap_cores(whole), w_query, w_key, w_value, norm1_gain
     )
+    small = whole[:, 384:].reshape(16, 4, 4, 256).transpose(0, 2, 1, 3).reshape(64, D).astype(f32)
     return (
         block_out.reshape(1, 1, TOK, D),
         grad_input.reshape(1, 1, TOK, D),

time: 532 us -> 480 us (0.902)
  the two profiles are of different devices: /device:TPU:27 before, /device:TPU:1 now
where the time goes in v5:
time: 480 us; the launch traced here: 470 us
  Pallas kernels  136 us (28%)
  waiting for transfers between devices  120 us (25%)
  starting transfers between devices  95.2 us (20%)
  blocking collectives  58.2 us (12%)
  other arithmetic  21.9 us (5%)
  local copies, waits for them, and re-layouts  18.6 us (4%)
  between operations  14.5 us (3%)
  matrix products  6.52 us (1%)
    all_to_all x10, waiting for transfers between devices, to_owners(): return lax.all_to_all(x, 'expert', split_axis=0, concat_axis=0, tiled=True)  69.7 us
    all_to_all x10, starting transfers between devices, to_owners(): return lax.all_to_all(x, 'expert', split_axis=0, concat_axis=0, tiled=True)  60.3 us
    all_to_all x2, blocking collectives, to_owners(): return lax.all_to_all(x, 'expert', split_axis=0, concat_axis=0, tiled=True)  58.2 us
    pallas_call x1, Pallas kernels, attend_backward(): call(backward_kernel, (struct((8, 64, LANES), bf16), struct((8, 64, LANES...  31.8 us
    pallas_call x1, Pallas kernels, attend_forward(): call(forward_kernel, (struct((2, CHUNK, LANES), f32), struct((8, 64, LANE...  26.8 us
    ppermute x2, waiting for transfers between devices, swap_halves(): return lax.ppermute(x, 'expert', [(i, i ^ 1) for i in range(16)])  17.6 us
    ppermute x5, waiting for transfers between devices, mirror(): return lax.ppermute(x, 'context', [(0, 3), (1, 2), (2, 1), (3, 0)])  17.2 us
    pallas_call x1, Pallas kernels, experts(): call(expert_kernel, (struct((16, 2, CAP, D), bf16), struct((2, 768, F), b...  16 us
  transfers between devices with their start and end apart: 34, of which 20 were waited for; matrix products, arithmetic and copies ran while one was open for 9% of the time, Pallas kernels for 25%

profile of v5, /device:TPU:1, one launch (start us, length us, event | category | flops | bytes accessed | tf_op | source)
XLA Modules:
  0.0 470.4 jit_solution(4798253416810822048)
XLA Ops:
  13.4 8.5 %all-to-all-start = ((bf16[16,128,128]{2,1,0:T(8,128)(2,1)}), bf16[16,128,128]{2,1,0:T(8,128)(2,1)}, u32[]{:S(2)}, u32[]{:S(2)}) async-start(bf16[16,128,128]{2,1,0:T(8,128)(2,1)} %get-tuple-element.83), calls=%async_computation | async-start | bytes 1048576 | tf_op jit(solution)/shard_map/all_to_all | solution.py:673
  21.9 10.3 %all-to-all-done = bf16[16,128,128]{2,1,0:T(8,128)(2,1)} async-done(((bf16[16,128,128]{2,1,0:T(8,128)(2,1)}), bf16[16,128,128]{2,1,0:T(8,128)(2,1)}, u32[]{:S(2)}, u32[]{:S(2)}) %all-to-all-start) | async-done | bytes 524320 | tf_op jit(solution)/shard_map/all_to_all | solution.py:673
  52.7 6.3 %all-to-all-start.2 = ((bf16[16,2,48,1024]{3,2,1,0:T(8,128)(2,1)}), bf16[16,2,48,1024]{3,2,1,0:T(8,128)(2,1)S(1)}, u32[]{:S(2)}, u32[]{:S(2)}) async-start(bf16[16,2,48,1024]{3,2,1,0:T(8,128)(2,1)} %bitcast.8), calls=%async_computation.2 | async-start | bytes 6291456 | tf_op jit(solution)/shard_map/all_to_all | solution.py:673
  68.3 26.8 %attend.1 = (f32[2,512,128]{2,1,0:T(8,128)}, bf16[8,64,128]{2,1,0:T(8,128)(2,1)}, bf16[8,64,128]{2,1,0:T(8,128)(2,1)}, f32[4,8,512]{2,1,0:T(8,128)}, bf16[8192,128]{1,0:T(8,128)(2,1)}) custom-call(s32[2]{0:T(128)} %pad_add_fusion.place_ref, bf16[16,64,128]{2,1,0:T(8,128)(2,1)} %copy-done.7, bf16[8,64,128]{2,1,0:T(8,128)(2,1)} %copy-done.14, ...), custom_call_target="tpu_custom_call" | custom-call | flops 20000000000 | bytes 4000000 | tf_op jit(solution)/shard_map/attend/pallas_call | solution.py:182
  104.6 7.9 %all-to-all-start.3 = ((bf16[16,64,128]{2,1,0:T(8,128)(2,1)}), bf16[16,64,128]{2,1,0:T(8,128)(2,1)}, u32[]{:S(2)}, u32[]{:S(2)}) async-start(bf16[16,64,128]{2,1,0:T(8,128)(2,1)} %constant_dynamic-update-slice_fusion), calls=%async_computation.3 | async-start | bytes 524288 | tf_op jit(solution)/shard_map/all_to_all | solution.py:673
  125.3 42.4 %all_to_all.60.x_ref = bf16[16,2,48,1024]{3,2,1,0:T(8,128)(2,1)} all-to-all(bf16[16,2,48,1024]{3,2,1,0:T(8,128)(2,1)} %bitcast.45), channel_id=1, replica_groups=mesh['expert'=16,'context'=4,'dp'=2] {'expert'}, dimensions={0} | all-to-all | bytes 6291456 | tf_op jit(solution)/shard_map/all_to_all | solution.py:673
  172.6 16.0 %experts.1 = (bf16[16,2,48,1024]{3,2,1,0:T(8,128)(2,1)}, bf16[2,768,512]{2,1,0:T(8,128)(2,1)}, bf16[2,768,1024]{2,1,0:T(8,128)(2,1)}, f32[2,768,1]{2,1,0:T(8,128)}, f32[2,768,32]{2,1,0:T(8,128)}) custom-call(s32[1]{0:T(128)} %bitcast.13.first_ref, bf16[16,2,48,1024]{3,2,1,0:T(8,128)(2,1)} %all_to_all.60.x_ref, f32[2,768,512]{2,1,0:T(8,128)} %raw.1.raw_ref, ...), custom_call_target="tpu_custom_call" | custom-call | flops 8053063680 | bytes 20000000 | tf_op jit(solution)/shard_map/experts/pallas_call | solution.py:362
  188.6 6.8 %all-to-all-done.5 = bf16[16,64,1024]{2,1,0:T(8,128)(2,1)S(1)} async-done(((bf16[16,64,1024]{2,1,0:T(8,128)(2,1)}), bf16[16,64,1024]{2,1,0:T(8,128)(2,1)S(1)}, u32[]{:S(2)}, u32[]{:S(2)}) %all-to-all-start.5) | async-done | bytes 2097184 | tf_op jit(solution)/shard_map/all_to_all | solution.py:673
  196.8 7.4 %all-to-all-start.6 = ((bf16[16,2,48,1024]{3,2,1,0:T(8,128)(2,1)}), bf16[16,2,48,1024]{3,2,1,0:T(8,128)(2,1)S(1)}, u32[]{:S(2)}, u32[]{:S(2)}) async-start(bf16[16,2,48,1024]{3,2,1,0:T(8,128)(2,1)} %get-tuple-element.94), calls=%async_computation.6 | async-start | bytes 6291456 | tf_op jit(solution)/shard_map/all_to_all | solution.py:673
  204.2 13.4 %expert_grads.1 = (bf16[16,2,48,1024]{3,2,1,0:T(8,128)(2,1)}, bf16[2,1024,1024]{2,1,0:T(8,128)(2,1)}, bf16[2,512,1024]{2,1,0:T(8,128)(2,1)}, f32[2,32,1024]{2,1,0:T(8,128)}) custom-call(bf16[16,2,48,1024]{3,2,1,0:T(8,128)(2,1)} %all_to_all.60.x_ref, bf16[16,2,48,1024]{3,2,1,0:T(8,128)(2,1)} %copy-done.3, f32[2,768,1]{2,1,0:T(8,128)} %get-tuple-element.95.gate_ref, ...), custom_call_target="tpu_custom_call" | custom-call | flops 6442450944 | bytes 24000000 | tf_op jit(solution)/shard_map/expert_grads/pallas_call | solution.py:402
  217.6 22.0 %all-to-all-done.6 = bf16[16,2,48,1024]{3,2,1,0:T(8,128)(2,1)S(1)} async-done(((bf16[16,2,48,1024]{3,2,1,0:T(8,128)(2,1)}), bf16[16,2,48,1024]{3,2,1,0:T(8,128)(2,1)S(1)}, u32[]{:S(2)}, u32[]{:S(2)}) %all-to-all-start.6) | async-done | bytes 3145760 | tf_op jit(solution)/shard_map/all_to_all | solution.py:673
  241.2 5.9 %turn_back.1 = (f32[128,1024]{1,0:T(8,128)}, bf16[16,80,1024]{2,1,0:T(8,128)(2,1)}, bf16[16,64,128]{2,1,0:T(8,128)(2,1)}) custom-call(bf16[1536,1024]{1,0:T(8,128)(2,1)} %bitcast.42, bf16[128,1536]{1,0:T(8,128)(2,1)} %get-tuple-element.153.spot_ref, f32[128,1024]{1,0:T(8,128)} %get-tuple-element.101.hidden_ref, f32[1,1024]{1,0:T(1,128)} %bitcast.61, ...), custom_call_target="tpu_custom_call" | custom-call | flops 1342177280 | bytes 8000000 | tf_op jit(solution)/shard_map/turn_back/pallas_call | solution.py:448
  247.2 15.8 %all_to_all.61.do_ref = bf16[16,64,128]{2,1,0:T(8,128)(2,1)S(1)} all-to-all(bf16[16,64,128]{2,1,0:T(8,128)(2,1)} %get-tuple-element.103), channel_id=1, replica_groups=mesh['expert'=16,'context'=4,'dp'=2] {'expert'}, dimensions={0} | all-to-all | bytes 524288 | tf_op jit(solution)/shard_map/all_to_all | solution.py:673
  268.7 31.8 %attend_back.1 = (bf16[8,64,128]{2,1,0:T(8,128)(2,1)}, bf16[8,64,128]{2,1,0:T(8,128)(2,1)}, f32[2048,128]{1,0:T(8,128)}, bf16[1024,128]{1,0:T(8,128)(2,1)}, bf16...) custom-call(s32[2]{0:T(128)} %pad_add_fusion.place_ref, ...), custom_call_target="tpu_custom_call" | custom-call | flops 49999998976 | bytes 8000000 | tf_op jit(solution)/shard_map/attend_back/pallas_call | solution.py:266
  308.1 6.7 %all-to-all-start.9 = ((bf16[16,2,48,1024]{3,2,1,0:T(8,128)(2,1)}), bf16[16,2,48,1024]{3,2,1,0:T(8,128)(2,1)S(1)}, u32[]{:S(2)}, u32[]{:S(2)}) async-start(bf16[16,2,48,1024]{3,2,1,0:T(8,128)(2,1)} %get-tuple-element.135), calls=%async_computation.9 | async-start | bytes 6291456 | tf_op jit(solution)/shard_map/all_to_all | solution.py:673
  327.7 5.4 %collective-permute-done.9.left_a_ref = bf16[1024,128]{1,0:T(8,128)(2,1)} collective-permute-done((bf16[1024,128]{1,0:T(8,128)(2,1)}, bf16[1024,128]{1,0:T(8,128)(2,1)}, u32[]{:S(2)}, u32[]{:S(2)}) %collective-permute-start.9) | collective-permute-done | bytes 262176 | tf_op jit(solution)/shard_map/ppermute | solution.py:685
  345.8 11.7 %collective-permute-done.14.got_ref = bf16[16,64,128]{2,1,0:T(8,128)(2,1)} collective-permute-done((bf16[16,64,128]{2,1,0:T(8,128)(2,1)}, bf16[16,64,128]{2,1,0:T(8,128)(2,1)}, u32[]{:S(2)}, u32[]{:S(2)}) %collective-permute-start.14) | collective-permute-done | bytes 262176 | tf_op jit(solution)/shard_map/ppermute | solution.py:693
  370.9 5.9 %collective-permute-done.16 = bf16[384,256]{1,0:T(8,128)(2,1)S(1)} collective-permute-done((bf16[384,256]{1,0:T(8,128)(2,1)}, bf16[384,256]{1,0:T(8,128)(2,1)S(1)}, u32[]{:S(2)}, u32[]{:S(2)}) %collective-permute-start.16) | collective-permute-done | bytes 196640 | tf_op jit(solution)/shard_map/ppermute | solution.py:693
  378.5 6.4 %all-to-all-start.10 = ((bf16[16,64,256]{2,1,0:T(8,128)(2,1)}), bf16[16,64,256]{2,1,0:T(8,128)(2,1)}, u32[]{:S(2)}, u32[]{:S(2)}) async-start(bf16[16,64,256]{2,1,0:T(8,128)(2,1)} %bitcast.44), calls=%async_computation.10 | async-start | bytes 1048576 | tf_op jit(solution)/shard_map/all_to_all | solution.py:673
  396.8 5.7 %all-to-all-start.11 = ((bf16[16,400,256]{2,1,0:T(8,128)(2,1)}), bf16[16,400,256]{2,1,0:T(8,128)(2,1)S(1)}, u32[]{:S(2)}, u32[]{:S(2)}) async-start(bf16[16,400,256]{2,1,0:T(8,128)(2,1)} %broadcast_in_dim.7), calls=%async_computation.11 | async-start | bytes 6553600 | tf_op jit(solution)/shard_map/all_to_all | solution.py:673
  406.5 5.0 %finish.1 = f32[128,1024]{1,0:T(8,128)} custom-call(bf16[16,64,256]{2,1,0:T(8,128)(2,1)} %all-to-all-done.10.grads_ref, bf16[128,1024]{1,0:T(8,128)(2,1)} %bitcast.48, f32[1,1024]{1,0:T(1,128)} %bitcast.58, bf16[1024,1024]{1,0:T(8,128)(2,1)} %wq_ref.5, bf16[1024,512]{1,0:T(8,128)(2,1)} %wk_ref.5, bf16[1024,512]{1,0:T(8,128)(2,1)} %wv_ref.5, ...), custom_call_target="tpu_custom_call" | custom-call | flops 1073741824 | bytes 8000000 | tf_op jit(solution)/shard_map/finish/pallas_call | solution.py:591
  413.7 25.9 %all-to-all-done.11.own_ref = bf16[16,400,256]{2,1,0:T(8,128)(2,1)S(1)} async-done(((bf16[16,400,256]{2,1,0:T(8,128)(2,1)}), bf16[16,400,256]{2,1,0:T(8,128)(2,1)S(1)}, u32[]{:S(2)}, u32[]{:S(2)}) %all-to-all-start.11) | async-done | bytes 3276832 | tf_op jit(solution)/shard_map/all_to_all | solution.py:673
  439.5 7.6 %collective-permute-start.19 = (bf16[16,400,256]{2,1,0:T(8,128)(2,1)S(1)}, bf16[16,400,256]{2,1,0:T(8,128)(2,1)}, u32[]{:S(2)}, u32[]{:S(2)}) collective-permute-start(bf16[16,400,256]{2,1,0:T(8,128)(2,1)S(1)} %all-to-all-done.11.own_ref), channel_id=1, source_target_pairs={{0,1},{1,0},{2,3},{3,2},{4,5},{5,4},{6,7},{7,6},{8,9},{9,8},{10,11... | collective-permute-start | bytes 9830408 | tf_op jit(solution)/shard_map/ppermute | solution.py:681
  452.8 10.6 %assemble.1 = (f32[1024,1024]{1,0:T(8,128)}, f32[1024,512]{1,0:T(8,128)}, f32[1024,512]{1,0:T(8,128)}, f32[1024,1024]{1,0:T(8,128)}, f32[1,1024]{1,0:T(1,128)}) custom-call(s32[1]{0:T(128)} %bitcast.2.core_ref, bf16[16,400,256]{2,1,0:T(8,128)(2,1)} %copy-done, bf16[16,400,256]{2,1,0:T(8,128)(2,1)} %collective-permute-done.19.other_ref, ...), custom_call_target="tpu_custom_call" | custom-call | flops 1000000 | bytes 22000000 | tf_op jit(solution)/shard_map/assemble/pallas_call | solution.py:651
  (137 shorter events, 143.4 us)
Async XLA Ops:
  7.2 108.2 %all-gather.3.cloned.1.call-start = ((), (), s32[]{:S(2)}) async-start(), calls=%async_computation.14 | async-start | bytes 2359296 | tf_op jit(solution)/shard_map/all_gather | solution.py:741
  13.4 18.8 %all-to-all-start = ((bf16[16,128,128]{2,1,0:T(8,128)(2,1)}), bf16[16,128,128]{2,1,0:T(8,128)(2,1)}, u32[]{:S(2)}, u32[]{:S(2)}) async-start(bf16[16,128,128]{2,1,0:T(8,128)(2,1)} %get-tuple-element.83), calls=%async_computation | async-start | bytes 1048576 | tf_op jit(solution)/shard_map/all_to_all | solution.py:673
  32.2 10.9 %all-to-all-start.1 = ((bf16[16,64,128]{2,1,0:T(8,128)(2,1)}), bf16[16,64,128]{2,1,0:T(8,128)(2,1)S(1)}, u32[]{:S(2)}, u32[]{:S(2)}) async-start(bf16[16,64,128]{2,1,0:T(8,128)(2,1)} %get-tuple-element.84), calls=%async_computation.1 | async-start | bytes 524288 | tf_op jit(solution)/shard_map/all_to_all | solution.py:673
  36.3 22.9 %collective-permute-start.1 = (bf16[2048,128]{1,0:T(8,128)(2,1)}, bf16[2048,128]{1,0:T(8,128)(2,1)}, u32[]{:S(2)}, u32[]{:S(2)}) collective-permute-start(bf16[2048,128]{1,0:T(8,128)(2,1)} %bitcast.5.own_ref), channel_id=1, source_target_pairs={{0,2},{2,4},{4,6},{6,0},{1,3},{3,5},{5,7},{7,1},{8,10},{10,12},{12... | collective-permute-start | bytes 1572872 | tf_op jit(solution)/shard_map/ppermute | solution.py:685
  37.6 23.5 %collective-permute-start.3 = (bf16[2048,128]{1,0:T(8,128)(2,1)}, bf16[2048,128]{1,0:T(8,128)(2,1)}, u32[]{:S(2)}, u32[]{:S(2)}) collective-permute-start(bf16[2048,128]{1,0:T(8,128)(2,1)} %bitcast.5.own_ref), channel_id=1, source_target_pairs={{0,6},{2,0},{4,2},{6,4},{1,7},{3,1},{5,3},{7,5},{8,14},{10,8},{12,... | collective-permute-start | bytes 1572872 | tf_op jit(solution)/shard_map/ppermute | solution.py:685
  43.1 9.0 %collective-permute-start = (bf16[8,64,128]{2,1,0:T(8,128)(2,1)S(1)}, bf16[8,64,128]{2,1,0:T(8,128)(2,1)S(1)}, u32[]{:S(2)}, u32[]{:S(2)}) collective-permute-start(bf16[8,64,128]{2,1,0:T(8,128)(2,1)S(1)} %slice.32), channel_id=1, source_target_pairs={{0,6},{2,4},{4,2},{6,0},{1,7},{3,5},{5,3},{7,1},{8,14},{10,12},{12... | collective-permute-start | bytes 393224 | tf_op jit(solution)/shard_map/ppermute | solution.py:677
  52.7 42.4 %all-to-all-start.2 = ((bf16[16,2,48,1024]{3,2,1,0:T(8,128)(2,1)}), bf16[16,2,48,1024]{3,2,1,0:T(8,128)(2,1)S(1)}, u32[]{:S(2)}, u32[]{:S(2)}) async-start(bf16[16,2,48,1024]{3,2,1,0:T(8,128)(2,1)} %bitcast.8), calls=%async_computation.2 | async-start | bytes 6291456 | tf_op jit(solution)/shard_map/all_to_all | solution.py:673
  59.1 113.6 %all-gather.5.cloned.1.call-start = ((), (), s32[]{:S(2)}) async-start(), calls=%async_computation.15 | async-start | bytes 4718592 | tf_op jit(solution)/shard_map/all_gather | solution.py:740
  95.1 8.8 %collective-permute-start.5 = (bf16[8,64,128]{2,1,0:T(8,128)(2,1)}, bf16[8,64,128]{2,1,0:T(8,128)(2,1)S(1)}, u32[]{:S(2)}, u32[]{:S(2)}) collective-permute-start(bf16[8,64,128]{2,1,0:T(8,128)(2,1)} %get-tuple-element.88), channel_id=1, source_target_pairs={{0,6},{2,4},{4,2},{6,0},{1,7},{3,5},{5,3},{7,1},{8,14},{10,12},{12... | collective-permute-start | bytes 393224 | tf_op jit(solution)/shard_map/ppermute | solution.py:677
  104.6 15.8 %all-to-all-start.3 = ((bf16[16,64,128]{2,1,0:T(8,128)(2,1)}), bf16[16,64,128]{2,1,0:T(8,128)(2,1)}, u32[]{:S(2)}, u32[]{:S(2)}) async-start(bf16[16,64,128]{2,1,0:T(8,128)(2,1)} %constant_dynamic-update-slice_fusion), calls=%async_computation.3 | async-start | bytes 524288 | tf_op jit(solution)/shard_map/all_to_all | solution.py:673
  167.7 27.7 %all-to-all-start.5 = ((bf16[16,64,1024]{2,1,0:T(8,128)(2,1)}), bf16[16,64,1024]{2,1,0:T(8,128)(2,1)S(1)}, u32[]{:S(2)}, u32[]{:S(2)}) async-start(bf16[16,64,1024]{2,1,0:T(8,128)(2,1)} %get-tuple-element.91), calls=%async_computation.5 | async-start | bytes 4194304 | tf_op jit(solution)/shard_map/all_to_all | solution.py:673
  196.8 42.8 %all-to-all-start.6 = ((bf16[16,2,48,1024]{3,2,1,0:T(8,128)(2,1)}), bf16[16,2,48,1024]{3,2,1,0:T(8,128)(2,1)S(1)}, u32[]{:S(2)}, u32[]{:S(2)}) async-start(bf16[16,2,48,1024]{3,2,1,0:T(8,128)(2,1)} %get-tuple-element.94), calls=%async_computation.6 | async-start | bytes 6291456 | tf_op jit(solution)/shard_map/all_to_all | solution.py:673
  263.5 37.0 %all-to-all-start.8 = ((bf16[16,80,1024]{2,1,0:T(8,128)(2,1)}), bf16[16,80,1024]{2,1,0:T(8,128)(2,1)S(1)}, u32[]{:S(2)}, u32[]{:S(2)}) async-start(bf16[16,80,1024]{2,1,0:T(8,128)(2,1)} %get-tuple-element.117), calls=%async_computation.8 | async-start | bytes 5242880 | tf_op jit(solution)/shard_map/all_to_all | solution.py:673
  267.2 144.3 %reduce-scatter.3.cloned.1.call-start = ((), (), s32[]{:S(2)}) async-start(), calls=%async_computation.16 | async-start | bytes 4718592 | tf_op jit(solution)/shard_map/reduce_scatter | solution.py:770
  308.1 70.4 %all-to-all-start.9 = ((bf16[16,2,48,1024]{3,2,1,0:T(8,128)(2,1)}), bf16[16,2,48,1024]{3,2,1,0:T(8,128)(2,1)S(1)}, u32[]{:S(2)}, u32[]{:S(2)}) async-start(bf16[16,2,48,1024]{3,2,1,0:T(8,128)(2,1)} %get-tuple-element.135), calls=%async_computation.9 | async-start | bytes 6291456 | tf_op jit(solution)/shard_map/all_to_all | solution.py:673
  317.5 10.1 %collective-permute-start.10 = (bf16[1024,128]{1,0:T(8,128)(2,1)}, bf16[1024,128]{1,0:T(8,128)(2,1)}, u32[]{:S(2)}, u32[]{:S(2)}) collective-permute-start(bf16[1024,128]{1,0:T(8,128)(2,1)} %get-tuple-element.124), channel_id=1, source_target_pairs={{0,2},{2,4},{4,6},{6,0},{1,3},{3,5},{5,7},{7,1},{8,10},{10,12},{12... | collective-permute-start | bytes 786440 | tf_op jit(solution)/shard_map/ppermute | solution.py:685
  317.5 10.1 %collective-permute-start.11 = (bf16[1024,128]{1,0:T(8,128)(2,1)}, bf16[1024,128]{1,0:T(8,128)(2,1)}, u32[]{:S(2)}, u32[]{:S(2)}) collective-permute-start(bf16[1024,128]{1,0:T(8,128)(2,1)} %get-tuple-element.125), channel_id=1, source_target_pairs={{0,6},{2,0},{4,2},{6,4},{1,7},{3,1},{5,3},{7,5},{8,14},{10,8},{12,... | collective-permute-start | bytes 786440 | tf_op jit(solution)/shard_map/ppermute | solution.py:685
  323.2 9.8 %collective-permute-start.9 = (bf16[1024,128]{1,0:T(8,128)(2,1)}, bf16[1024,128]{1,0:T(8,128)(2,1)}, u32[]{:S(2)}, u32[]{:S(2)}) collective-permute-start(bf16[1024,128]{1,0:T(8,128)(2,1)} %add_convert_fusion.1), channel_id=1, source_target_pairs={{0,2},{2,4},{4,6},{6,0},{1,3},{3,5},{5,7},{7,1},{8,10},{10,12},{12... | collective-permute-start | bytes 786440 | tf_op jit(solution)/shard_map/ppermute | solution.py:685
  325.0 9.2 %collective-permute-start.13 = (bf16[1024,128]{1,0:T(8,128)(2,1)}, bf16[1024,128]{1,0:T(8,128)(2,1)}, u32[]{:S(2)}, u32[]{:S(2)}) collective-permute-start(bf16[1024,128]{1,0:T(8,128)(2,1)} %add_convert_fusion), channel_id=1, source_target_pairs={{0,6},{2,0},{4,2},{6,4},{1,7},{3,1},{5,3},{7,5},{8,14},{10,8},{12,... | collective-permute-start | bytes 786440 | tf_op jit(solution)/shard_map/ppermute | solution.py:685
  336.8 20.8 %collective-permute-start.14 = (bf16[16,64,128]{2,1,0:T(8,128)(2,1)}, bf16[16,64,128]{2,1,0:T(8,128)(2,1)}, u32[]{:S(2)}, u32[]{:S(2)}) collective-permute-start(bf16[16,64,128]{2,1,0:T(8,128)(2,1)} %get-tuple-element.129), channel_id=1, source_target_pairs={{0,8},{8,0},{16,24},{24,16},{32,40},{40,32},{48,56},{56,48},{64,72... | collective-permute-start | bytes 786440 | tf_op jit(solution)/shard_map/ppermute | solution.py:693
  378.5 15.5 %all-to-all-start.10 = ((bf16[16,64,256]{2,1,0:T(8,128)(2,1)}), bf16[16,64,256]{2,1,0:T(8,128)(2,1)}, u32[]{:S(2)}, u32[]{:S(2)}) async-start(bf16[16,64,256]{2,1,0:T(8,128)(2,1)} %bitcast.44), calls=%async_computation.10 | async-start | bytes 1048576 | tf_op jit(solution)/shard_map/all_to_all | solution.py:673
  396.8 42.7 %all-to-all-start.11 = ((bf16[16,400,256]{2,1,0:T(8,128)(2,1)}), bf16[16,400,256]{2,1,0:T(8,128)(2,1)S(1)}, u32[]{:S(2)}, u32[]{:S(2)}) async-start(bf16[16,400,256]{2,1,0:T(8,128)(2,1)} %broadcast_in_dim.7), calls=%async_computation.11 | async-start | bytes 6553600 | tf_op jit(solution)/shard_map/all_to_all | solution.py:673
  402.6 44.6 %reduce-scatter.5.cloned.1.call-start = ((), (), s32[]{:S(2)}) async-start(), calls=%async_computation.17 | async-start | bytes 2359296 | tf_op jit(solution)/shard_map/reduce_scatter | solution.py:800
  439.5 13.2 %collective-permute-start.19 = (bf16[16,400,256]{2,1,0:T(8,128)(2,1)S(1)}, bf16[16,400,256]{2,1,0:T(8,128)(2,1)}, u32[]{:S(2)}, u32[]{:S(2)}) collective-permute-start(bf16[16,400,256]{2,1,0:T(8,128)(2,1)S(1)} %all-to-all-done.11.own_ref), channel_id=1, source_target_pairs={{0,1},{1,0},{2,3},{3,2},{4,5},{5,4},{6,7},{7,6},{8,9},{9,8},{10,11... | collective-permute-start | bytes 9830408 | tf_op jit(solution)/shard_map/ppermute | solution.py:681
  (28 other events, 248.5 us)
Sparse Core Ops, SparseCore 0:
  9.7 28.8 all-gather.2
  67.8 39.7 all-gather.4
  271.1 42.4 reduce-scatter.2
  406.1 33.7 reduce-scatter.4

commit v6 on v5

--- a/solution.py
+++ b/solution.py
@@ -304,20 +304,36 @@
     )(att, x, wo, gain.reshape(1, D), pick)
 
 
-def raw_kernel(top_ref, down_ref, raw_ref):
-    raw_ref[...] = branch_scale * dot_rows(top_ref[...].reshape(768, D), down_ref[...])
-
-
-def raw_grads(top, down):
-    per = pl.BlockSpec((16, None, CAP, D), lambda n: (0, n, 0, 0))
-    return call(
-        raw_kernel, struct((2, 768, F), f32), 2 * SLOTS * D * F, 8e6, grid=(2,), in_specs=[per, owned(F, D)],
-        out_specs=owned(768, F), name="raw",
-    )(top, down)
+def raw_kernel(first_ref, top_ref, down_ref, rows_ref, raw_ref):
+    number = first_ref[0] + pl.program_id(0)
+    chosen = (lane_index((8, LANES)) == number).astype(bf16)
+    slot = lax.broadcasted_iota(jnp.int32, (CAP, TOK), 0).astype(f32)
+    for n in range(16):
+        place = dot_rows(chosen, top_ref[n, :, D:])[0:1]
+        rows = dot((slot == place).astype(bf16), top_ref[n, :, :D])
+        rows_ref[CAP * n : CAP * n + CAP] = rows.astype(bf16)
+    raw_ref[...] = branch_scale * dot_rows(rows_ref[...], down_ref[...])
+
+
+def raw_grads(first, top, down):
+    return call(
+        raw_kernel,
+        (struct((2, 768, D), bf16), struct((2, 768, F), f32)),
+        2 * SLOTS * D * F,
+        1.2e7,
+        grid=(2,),
+        in_specs=[
+            pl.BlockSpec(memory_space=pltpu.SMEM),
+            pl.BlockSpec((16, TOK, D + LANES), lambda n: (0, 0, 0)),
+            owned(F, D),
+        ],
+        out_specs=(owned(768, D), owned(768, F)),
+        name="raw",
+    )(first, top, down)
 
 
 def expert_kernel(
-    first_ref, x_ref, raw_ref, gu_ref, wr_ref, back_ref, hidden_ref, mixed_ref, gate_ref, logit_ref
+    first_ref, x_ref, raw_ref, gu_ref, wr_ref, back_ref, hidden_ref, mixed_ref, gate_ref, logit_ref, norm_ref
 ):
     number = first_ref[0] + pl.program_id(0)
     wr = wr_ref[...]
@@ -351,6 +367,11 @@
         back = dot_rows(mixed_gate, gu_ref[:, :F]) + dot_rows(mixed_up, gu_ref[:, F:])
         back = back + dot_rows(hi, wr) + dot_rows(lo, wr)
         back_ref[take] = back.astype(bf16).reshape(8, CAP, D)
+        product = jnp.sum(back * x.astype(f32), axis=0, keepdims=True)
+        if part == 0:
+            norm_ref[...] = jnp.broadcast_to(product, (8, D))
+        else:
+            norm_ref[...] += product
 
 
 def owned(*shape):
@@ -367,6 +388,7 @@
             struct((2, 768, D), bf16),
             struct((2, 768, 1), f32),
             struct((2, 768, EXPERTS), f32),
+            struct((2, 8, D), f32),
         ),
         2 * SLOTS * D * 2560,
         2e7,
@@ -378,7 +400,7 @@
             owned(D, D),
             pl.BlockSpec((D, EXPERTS), lambda n: (0, 0)),
         ],
-        out_specs=(per, owned(768, F), owned(768, D), owned(768, 1), owned(768, EXPERTS)),
+        out_specs=(per, owned(768, F), owned(768, D), owned(768, 1), owned(768, EXPERTS), owned(8, D)),
         name="experts",
     )(first, x, raw, gate_up, wr)
 
@@ -390,7 +412,7 @@
     gate = gate_ref[...]
     x = x_ref[...].reshape(768, D)
     out_ref[...] = (gate * dot(hidden, down_ref[...])).astype(bf16).reshape(16, CAP, D)
-    top = (branch_scale * gate * top_ref[...].reshape(768, D).astype(f32)).astype(bf16)
+    top = (branch_scale * gate * top_ref[...].astype(f32)).astype(bf16)
     ddown_ref[...] = dot_down(hidden, top).astype(bf16)
     dgu_ref[...] = dot_down(x, mixed_ref[...]).astype(bf16)
     hi, lo = split2(logit_ref[...])
@@ -410,14 +432,14 @@
         2 * SLOTS * D * 2048,
         2.4e7,
         grid=(2,),
-        in_specs=[per, per, owned(768, 1), owned(768, EXPERTS), owned(768, F), owned(768, D), owned(F, D)],
+        in_specs=[per, owned(768, D), owned(768, 1), owned(768, EXPERTS), owned(768, F), owned(768, D), owned(F, D)],
         out_specs=(per, owned(D, D), owned(F, D), owned(EXPERTS, D)),
         name="expert_grads",
     )(x, top, gate, logits, hidden, mixed, down)
 
 
 def turn_back_kernel(
-    back_ref, spot_ref, hidden_ref, gain_ref, top_ref, wo_ref, router_ref, state_ref, attn_ref, send_ref
+    back_ref, spot_ref, hidden_ref, gain_ref, top_ref, wo_ref, state_ref, attn_ref, send_ref
 ):
     grad = dot(spot_ref[...], back_ref[...])
     hidden = hidden_ref[...]
@@ -427,35 +449,25 @@
     state = top_ref[...].astype(f32) + inverse * (scaled - normed * jnp.mean(scaled * normed, axis=-1, keepdims=True))
     state_ref[...] = state
     attn = (branch_scale * state).astype(bf16)
-    router = router_ref[0] + router_ref[1]
-    norm = jnp.sum(grad * normed, axis=0, keepdims=True)
-    for e in range(16):
-        attn_ref[e, :64] = attn[64 * (e % 2) : 64 * (e % 2) + 64]
-        if e < 8:
-            extra = jnp.concatenate([router[4 * e : 4 * e + 4], jnp.zeros((12, D), f32)], axis=0)
-        elif e == 8:
-            extra = jnp.concatenate([norm, jnp.zeros((15, D), f32)], axis=0)
-        else:
-            extra = jnp.zeros((16, D), f32)
-        attn_ref[e, 64:] = extra.astype(bf16)
+    attn_ref[...] = attn
     attended = dot_rows(attn, wo_ref[...]).astype(bf16)
     for j in range(PAIRS):
         for h in range(2):
             send_ref[2 * j + h] = attended[h * 64 : h * 64 + 64, j * LANES : (j + 1) * LANES]
 
 
-def turn_back(back, spot, hidden, gain, top, wo, router):
+def turn_back(back, spot, hidden, gain, top, wo):
     return call(
         turn_back_kernel,
         (
             struct((TOK, D), f32),
-            struct((16, 80, D), bf16),
+            struct((TOK, D), bf16),
             struct((16, TOK // 2, LANES), bf16),
         ),
         2 * 256 * D * (D + SLOTS),
         8e6,
         name="turn_back",
-    )(back, spot, hidden, gain.reshape(1, D), top, wo, router)
+    )(back, spot, hidden, gain.reshape(1, D), top, wo)
 
 
 def unturn(v, cos, sin, first):
@@ -507,38 +519,49 @@
     return call(unturn_kernel, struct((1024, 256), bf16), 1e6, 3e6, name="unturn")(dq, dq_far, keep, got, cos, sin)
 
 
-def head_kernel(core_ref, act_ref, attn_ref, o_ref, grads_ref, mine_ref, other_ref, all_ref):
-    all_ref[:D] = dot_down(act_ref[...], grads_ref[...]).astype(bf16)
-    out = dot_down(o_ref[...], attn_ref[:, :64, :].reshape(1024, D)).astype(bf16)
-    for b in range(4):
-        all_ref[D + LANES * b : D + LANES * (b + 1)] = out[:, 256 * b : 256 * (b + 1)]
-    extra = attn_ref[0, 64:].astype(f32)
+def head_kernel(place_ref, act_ref, attn_ref, o_ref, grads_ref, extra_ref, mine_ref, other_ref, all_ref):
+    grads = dot_down(act_ref[...], grads_ref[...]).astype(bf16)
+    out = dot_down(o_ref[...], attn_ref[...].reshape(1024, D)).astype(bf16)
+    for quarter in range(4):
+        start = 384 * quarter
+        all_ref[start : start + 256] = grads[256 * quarter : 256 * quarter + 256]
+        all_ref[start + 256 : start + 384] = out[:, 256 * quarter : 256 * quarter + 256]
+    extra = extra_ref[0].astype(f32)
     for e in range(1, 16):
-        extra = extra + attn_ref[e, 64:].astype(f32)
+        extra = extra + extra_ref[e].astype(f32)
     packed = extra[:, :256]
     for b in range(1, 4):
         packed = packed + pltpu.roll(extra[:, 256 * b : 256 * (b + 1)], 4 * b, 0)
     packed = packed.astype(bf16)
-    core = core_ref[0]
+    core = place_ref[2]
     for which, out_ref in ((1 - core, other_ref), (core, mine_ref)):
         out_ref[:768] = all_ref[pl.ds(pl.multiple_of(which * 768, 768), 768), :]
         out_ref[768:] = packed
 
 
-def head_grads(core, act, attn, o, grads):
-    smem = pl.BlockSpec(memory_space=pltpu.SMEM)
-    vmem = pl.BlockSpec(memory_space=pltpu.VMEM)
+def head_grads(place, act, attn, o, grads, returned):
+    whole = lambda *shape: pl.BlockSpec(shape, lambda i, place: (0,) * len(shape))
     half = struct((784, 256), bf16)
     return call(
         head_kernel,
         (half, half),
         2 * 1024 * 1024 * 512,
         8e6,
-        in_specs=[smem] + [vmem] * 4,
-        out_specs=(vmem,) * 2,
-        scratch_shapes=[pltpu.VMEM((1536, 256), bf16)],
+        grid_spec=pltpu.PrefetchScalarGridSpec(
+            num_scalar_prefetch=1,
+            grid=(1,),
+            in_specs=[
+                whole(1024, D),
+                pl.BlockSpec((16, None, 64, D), lambda i, place: (0, place[1], 0, 0)),
+                whole(1024, LANES),
+                whole(1024, 256),
+                pl.BlockSpec((16, None, 16, D), lambda i, place: (0, 6, 0, 0)),
+            ],
+            out_specs=(whole(784, 256), whole(784, 256)),
+            scratch_shapes=[pltpu.VMEM((1536, 256), bf16)],
+        ),
         name="head_grads",
-    )(core, act, attn, o, grads)
+    )(place, act, attn, o, grads, returned)
 
 
 def split_kernel(place_ref, mine_ref, other_ref, keep_ref, give_ref):
@@ -599,55 +622,45 @@
 
 
 def assemble_kernel(
-    core_ref, own_ref, other_ref, wq_ref, wk_ref, wv_ref, gain_ref, q_ref, k_ref, v_ref, o_ref, norm_ref
+    place_ref, own_ref, other_ref, wq_ref, wk_ref, wv_ref, gain_ref, q_ref, k_ref, v_ref, o_ref, norm_ref
 ):
-    left = lane_index((384, LANES)) < HEAD_DIM
-
-    def write(pieces):
-        for core in range(2):
-            piece = pieces[core]
-            for h in range(2):
-                start = 768 * core + 384 * h
-                count = min(384, max(0, D - start))
-                if count:
-                    rows = slice(start, start + count)
-                    total = jnp.zeros((count, LANES), f32)
-                    for j in range(PAIRS):
-                        lanes = slice(j * LANES, (j + 1) * LANES)
-                        value = piece[2 * j + h, :count, :LANES].astype(f32)
-                        q_ref[rows, lanes] = value
-                        total = total + value * wq_ref[rows, lanes].astype(f32)
-                    for b in range(PAIRS // 2):
-                        lanes = slice(b * LANES, (b + 1) * LANES)
-                        even = piece[4 * b + h, :count, LANES:].astype(f32)
-                        odd = piece[4 * b + 2 + h, :count, LANES:].astype(f32)
-                        k = jnp.where(left[:count], even, pltpu.roll(odd, HEAD_DIM, 1))
-                        v = jnp.where(left[:count], pltpu.roll(even, HEAD_DIM, 1), odd)
-                        k_ref[rows, lanes] = k
-                        v_ref[rows, lanes] = v
-                        total = total + k * wk_ref[rows, lanes].astype(f32) + v * wv_ref[rows, lanes].astype(f32)
-                    summed = jnp.sum(jnp.transpose(total), axis=0, keepdims=True)
-                    norm_ref[:, rows] = summed / gain_ref[:, rows]
-                for b in range(4):
-                    at = D + LANES * b - start
-                    if 0 <= at < 384:
-                        for j in range(PAIRS):
-                            o_ref[j * LANES : (j + 1) * LANES, 256 * b : 256 * (b + 1)] = piece[
-                                2 * j + h, at : at + LANES, :
-                            ].astype(f32)
-
-    @pl.when(core_ref[0] == 0)
+    left = lane_index((256, LANES)) < HEAD_DIM
+
+    def write(piece):
+        total = jnp.zeros((256, LANES), f32)
+        for j in range(PAIRS):
+            lanes = slice(j * LANES, (j + 1) * LANES)
+            value = piece[j, :256, :LANES].astype(f32)
+            q_ref[:, lanes] = value
+            total = total + value * wq_ref[:, lanes].astype(f32)
+            o_ref[lanes, :] = piece[j, 256:384, :].astype(f32)
+        for b in range(PAIRS // 2):
+            lanes = slice(b * LANES, (b + 1) * LANES)
+            even = piece[2 * b, :256, LANES:].astype(f32)
+            odd = piece[2 * b + 1, :256, LANES:].astype(f32)
+            k = jnp.where(left, even, pltpu.roll(odd, HEAD_DIM, 1))
+            v = jnp.where(left, pltpu.roll(even, HEAD_DIM, 1), odd)
+            k_ref[:, lanes] = k
+            v_ref[:, lanes] = v
+            total = total + k * wk_ref[:, lanes].astype(f32) + v * wv_ref[:, lanes].astype(f32)
+        norm_ref[...] = jnp.sum(jnp.transpose(total), axis=0, keepdims=True) / gain_ref[...]
+
+    @pl.when(pl.program_id(0) < 2)
     def _():
-        write((own_ref, other_ref))
-
-    @pl.when(core_ref[0] == 1)
+        write(own_ref)
+
+    @pl.when(pl.program_id(0) >= 2)
     def _():
-        write((other_ref, own_ref))
-
-
-def assemble(core, own, other, wq, wk, wv, gain):
-    smem = pl.BlockSpec(memory_space=pltpu.SMEM)
-    vmem = pl.BlockSpec(memory_space=pltpu.VMEM)
+        write(other_ref)
+
+
+def assemble(place, own, other, wq, wk, wv, gain):
+    def quarter(i, place):
+        return 2 * jnp.where(i < 2, place[2], 1 - place[2]) + i % 2
+
+    rows = lambda width: pl.BlockSpec((256, width), lambda i, place: (quarter(i, place), 0))
+    columns = lambda height: pl.BlockSpec((height, 256), lambda i, place: (0, quarter(i, place)))
+    piece = (PAIRS, None, 400, 256)
     return call(
         assemble_kernel,
         (
@@ -659,10 +672,31 @@
         ),
         1e6,
         2.2e7,
-        in_specs=[smem] + [vmem] * 6,
-        out_specs=(vmem,) * 5,
+        grid_spec=pltpu.PrefetchScalarGridSpec(
+            num_scalar_prefetch=1,
+            grid=(4,),
+            in_specs=[
+                pl.BlockSpec(piece, lambda i, place: (0, jnp.minimum(i, 1), 0, 0)),
+                pl.BlockSpec(piece, lambda i, place: (0, jnp.maximum(i - 2, 0), 0, 0)),
+                rows(D),
+                rows(512),
+                rows(512),
+                columns(1),
+            ],
+            out_specs=(rows(D), rows(512), rows(512), columns(D), columns(1)),
+        ),
         name="assemble",
-    )(core, own, other, wq, wk, wv, gain.reshape(1, D))
+    )(place, own.reshape(PAIRS, 2, 400, 256), other.reshape(PAIRS, 2, 400, 256), wq, wk, wv, gain.reshape(1, D))
+
+
+def spread_kernel(a_ref, b_ref, out_ref):
+    total = (a_ref[...].astype(f32) + b_ref[...].astype(f32)).astype(bf16)
+    for e in range(16):
+        out_ref[e] = total
+
+
+def add_and_spread(a, b):
+    return call(spread_kernel, struct((16, 400, 256), bf16), 1e6, 4e6, name="spread")(a, b)
 
 
 def after(x, *earlier):
@@ -728,8 +762,6 @@
     spot = (dot_rows(marked, owner16) == slot_number[None, :].astype(f32)).astype(bf16)
     selector = (dot_rows(owner16, marked) == slot_number[:, None].astype(f32)).astype(bf16)
 
-    core_index = lax.axis_index("dp")
-    core = core_index.astype(jnp.int32).reshape(1)
     act_send, q_send, kv_send = project(x, norm1_gain, w_query, w_key, w_value, cos, sin)
     kv_own = to_owners(kv_send).reshape(BLOCK, LANES)
     kv_left, kv_right = shift(kv_own, 1), shift(kv_own, 3)
@@ -737,72 +769,79 @@
     q_far = mirror(q_own[8:])
     far_a, far_b = shift(kv_left[: BLOCK // 2], 1), shift(kv_right[BLOCK // 2 :], 3)
 
-    gate_up = lax.all_gather(after(w_gate_up, far_a, far_b), ("context", "dp"), axis=1, tiled=True)
     down = lax.all_gather(w_down, ("context", "dp"), axis=1, tiled=True)
-    top_send = dot(selector, top).astype(bf16).reshape(16, 2, CAP, D)
-    top_rows = to_owners(after(top_send, q_far))
-
-    seat = jnp.stack([context, half]).astype(jnp.int32)
+    wide = jnp.concatenate([top, jnp.pad(marked, ((0, 0), (0, LANES - EXPERTS)))], 1)
+    top_all = lax.all_gather(after(wide, down), "expert", axis=0, tiled=True)
+    gate_up = lax.all_gather(after(w_gate_up, top_all), ("context", "dp"), axis=1, tiled=True)
+    act_rows = to_owners(after(act_send, q_far, far_a, far_b)).reshape(1024, D)
+
+    seat = jnp.stack([context, half, lax.axis_index("dp")]).astype(jnp.int32)
     o, o_low, o_far, lse, kv = attend_forward(
         seat, q_own, q_far, (kv_own, kv_left, far_a, far_b, kv_right)
     )
-    o_far = after(o_far, top_rows)
+    o_far = after(o_far, act_rows)
     o_own = jnp.concatenate([o_low, mirror(o_far)], 0)
     att = to_owners(o_own)
-    raw = raw_grads(top_rows, down)
+    first = (2 * expert).astype(jnp.int32).reshape(1)
+    top_rows, raw = raw_grads(first, top_all.reshape(16, TOK, D + LANES), down)
     att = after(att, raw)
 
     hidden, send = middle(att, x, w_out, norm2_gain, selector)
     rows = to_owners(send.reshape(16, 2, CAP, D))
-    first = (2 * expert).astype(jnp.int32).reshape(1)
-    act_rows = to_owners(after(act_send, rows)).reshape(1024, D)
-    grad_rows, expert_hidden, mixed, gates, logits = experts(first, rows, raw, gate_up, w_router)
-    back = to_owners(after(grad_rows, act_rows))
+    grad_rows, expert_hidden, mixed, gates, logits, norm2_sum = experts(first, rows, raw, gate_up, w_router)
+    back = to_owners(grad_rows)
     out_rows, dgu, ddown, router_grad = expert_grads(rows, top_rows, gates, logits, expert_hidden, mixed, down)
     back = after(back, dgu)
 
-    state, attn_send, do_send = turn_back(
-        back.reshape(SLOTS, D), spot, hidden, norm2_gain, top, w_out, router_grad
+    state, attn, do_send = turn_back(
+        back.reshape(SLOTS, D), spot, hidden, norm2_gain, top, w_out
     )
     do_own = to_owners(do_send)
     do_far = mirror(do_own[8:])
-    attn_rows = to_owners(after(attn_send, do_own))
+    attn_all = lax.all_gather(attn, "expert", axis=0, tiled=True)
+    norm2_row = (norm2_sum[0, :1] + norm2_sum[1, :1]) / norm2_gain[None]
+    extra = jnp.concatenate([router_grad[0] + router_grad[1], norm2_row, jnp.zeros((31, D), f32)], 0)
+    extra = jnp.pad(extra.reshape(16, 4, D), ((0, 0), (0, 12), (0, 0))).astype(bf16)
+    out_send = jnp.concatenate([out_rows.reshape(16, 96, D), extra], 1)
+    returned = to_owners(after(out_send, do_own))
     grad_gate_up = lax.psum_scatter(
-        after(dgu, do_own), ("context", "dp"), scatter_dimension=1, tiled=True
+        after(dgu, attn_all), ("context", "dp"), scatter_dimension=1, tiled=True
     ).astype(f32)
 
     dq, dq_far, d0, d1a, d1b, d2a, d2b, d3a, d3b = attend_backward(seat, q_own, q_far, do_own, do_far, o, lse, kv)
-    dq, dq_far, d0, d1a, d1b, d2a, d2b, d3a, d3b, attn_rows = lax.optimization_barrier(
-        (dq, dq_far, d0, d1a, d1b, d2a, d2b, d3a, d3b, attn_rows)
-    )
 
     far_a, far_b = shift(d2a, 1), shift(d2b, 3)
     from_left_b, from_right_a = shift(d3b, 1), shift(d1a, 3)
-    dq_far = mirror(dq_far)
-    returned = to_owners(after(out_rows, dq_far))
+    dq_far = mirror(after(dq_far, far_a, far_b))
     from_left_a = shift((d3a.astype(f32) + far_a.astype(f32)).astype(bf16), 1)
     from_right_b = shift((d1b.astype(f32) + far_b.astype(f32)).astype(bf16), 3)
-    keep, give = merge(seat, d0, from_left_a, from_left_b, from_right_a, from_right_b)
+    keep, give = merge(seat, after(d0, returned), from_left_a, from_left_b, from_right_a, from_right_b)
     got = swap_halves(give)
     grads = unturn_rows(dq, dq_far, keep, got, half_cos, half_sin)
-    mine, other = head_grads(core, act_rows, attn_rows, o_own.reshape(1024, LANES), grads)
+    mine, other = head_grads(
+        seat,
+        act_rows,
+        attn_all.reshape(16, 2, 64, D),
+        o_own.reshape(1024, LANES),
+        grads,
+        returned.reshape(16, 7, 16, D),
+    )
     keep, give = split_halves(seat, mine, swap_cores(other))
-    grads_back = to_owners(after(grads, returned).reshape(16, 64, 256))
+    grads_back = to_owners(grads.reshape(16, 64, 256))
     total = keep + jnp.pad(swap_halves(give), ((0, 16), (0, 0))).astype(f32)
     total = total.astype(bf16)
     total = (total.astype(f32) + neighbour(total).astype(f32)).astype(bf16)
-    total = (total.astype(f32) + mirror(total).astype(f32)).astype(bf16)
-    block = after(jnp.broadcast_to(total[None], (16, 400, 256)), grads_back)
+    block = after(add_and_spread(total, mirror(total)), grads_back)
     whole = to_owners(block)
 
     grad_input = finish(grads_back, x, norm1_gain, w_query, w_key, w_value, state)
-    block_out = hidden + branch_scale * dot(spot, returned.reshape(SLOTS, D))
-    grad_down = lax.psum_scatter(after(ddown, got), ("context", "dp"), scatter_dimension=1, tiled=True).astype(f32)
+    block_out = hidden + branch_scale * dot(spot, returned[:, :96].reshape(SLOTS, D))
+    grad_down = lax.psum_scatter(after(ddown, grad_gate_up), ("context", "dp"), scatter_dimension=1, tiled=True).astype(f32)
     whole, grad_input, block_out, grad_gate_up = lax.optimization_barrier(
         (whole, grad_input, block_out, grad_gate_up)
     )
     dwq, dwk, dwv, dwo, norm1_grad = assemble(
-        core, whole, swap_cores(whole), w_query, w_key, w_value, norm1_gain
+        seat, whole, swap_cores(whole), w_query, w_key, w_value, norm1_gain
     )
     small = whole[:, 384:].reshape(16, 4, 4, 256).transpose(0, 2, 1, 3).reshape(64, D).astype(f32)
     return (

time: 480 us -> 593 us (1.24)
  waiting for transfers between devices: 120 us -> 277 us
  blocking collectives: 58.2 us -> 0 us
  Pallas kernels: 136 us -> 145 us
    all_gather x1 -> x3, waiting for transfers between devices: 0.01 us -> 111 us  [the longest x1 63.5 us: local(): attn_all = lax.all_gather(attn, 'expert', axis=0, tiled=True)]
    all_to_all x2 -> x0, blocking collectives: 58.2 us -> none  [to_owners(): return lax.all_to_all(x, 'expert', split_axis=0, concat_axis=0, tiled=True)]
    all_gather x1, waiting for transfers between devices: 0.01 us -> 27.2 us  [local(): down = lax.all_gather(w_down, ('context', 'dp'), axis=1, tiled=True)]
    all_to_all x10, waiting for transfers between devices: 69.7 us -> 86.8 us  [to_owners(): return lax.all_to_all(x, 'expert', split_axis=0, concat_axis=0, tiled=True)]
    ppermute x2, waiting for transfers between devices: 17.6 us -> 6.28 us  [swap_halves(): return lax.ppermute(x, 'expert', [(i, i ^ 1) for i in range(16)])]
    pallas_call x3 -> x4, Pallas kernels: 15.3 us -> 24.3 us  [the longest x1 11 us: raw_grads(): call(raw_kernel, (struct((2, 768, D), bf16), struct((2, 768, F), f32)), 2...]
    ppermute x10, waiting for transfers between devices: 10.9 us -> 17.9 us  [shift(): return lax.ppermute(x, 'context', [(i, (i + by) % 4) for i in range(4)])]
    concatenate x0 -> x3, other arithmetic: none -> 6.08 us  [the longest x1 4.3 us: local(): out_send = jnp.concatenate([out_rows.reshape(16, 96, D), extra], 1)]
  transfers between devices with their start and end apart: 34 -> 36, of which waited for: 20 -> 18; matrix products, arithmetic and copies ran while one was open for 9% -> 6% of each run, Pallas kernels for 25% -> 21%
where the time goes in v6:
time: 593 us; the launch traced here: 583 us
  waiting for transfers between devices  277 us (47%)
  Pallas kernels  145 us (24%)
  starting transfers between devices  101 us (17%)
  other arithmetic  22.8 us (4%)
  local copies, waits for them, and re-layouts  18.3 us (3%)
  between operations  15 us (3%)
    all_to_all x10, waiting for transfers between devices, to_owners(): return lax.all_to_all(x, 'expert', split_axis=0, concat_axis=0, tiled=True)  86.8 us
    all_to_all x10, starting transfers between devices, to_owners(): return lax.all_to_all(x, 'expert', split_axis=0, concat_axis=0, tiled=True)  64.9 us
    all_gather x1, waiting for transfers between devices, local(): attn_all = lax.all_gather(attn, 'expert', axis=0, tiled=True)  63.5 us
    all_gather x1, waiting for transfers between devices, local(): top_all = lax.all_gather(after(wide, down), 'expert', axis=0, tiled=True)  47.2 us
    pallas_call x1, Pallas kernels, attend_backward(): call(backward_kernel, (struct((8, 64, LANES), bf16), struct((8, 64, LANES...  31.8 us
    all_gather x1, waiting for transfers between devices, local(): down = lax.all_gather(w_down, ('context', 'dp'), axis=1, tiled=True)  27.2 us
    pallas_call x1, Pallas kernels, attend_forward(): call(forward_kernel, (struct((2, CHUNK, LANES), f32), struct((8, 64, LANE...  26.8 us
    ppermute x5, waiting for transfers between devices, mirror(): return lax.ppermute(x, 'context', [(0, 3), (1, 2), (2, 1), (3, 0)])  22.9 us
  transfers between devices with their start and end apart: 36, of which 18 were waited for; matrix products, arithmetic and copies ran while one was open for 6% of the time, Pallas kernels for 21%

profile of v6, /device:TPU:1, one launch (start us, length us, event | category | flops | bytes accessed | tf_op | source)
XLA Modules:
  0.0 583.0 jit_solution(15675124195814548402)
XLA Ops:
  11.3 27.2 %all-gather.5.cloned.1.call-done.down_ref = bf16[2,512,1024]{2,1,0:T(8,128)(2,1)} async-done(((bf16[2,64,1024]{2,1,0:T(8,128)(2,1)}), bf16[2,512,1024]{2,1,0:T(8,128)(2,1)}) %all-gather.5.cloned.1.call-update) | async-done | bytes 2097168 | tf_op jit(solution)/shard_map/all_gather | solution.py:772
  44.0 6.7 %all-to-all-start = ((bf16[16,128,128]{2,1,0:T(8,128)(2,1)}), bf16[16,128,128]{2,1,0:T(8,128)(2,1)S(1)}, u32[]{:S(2)}, u32[]{:S(2)}) async-start(bf16[16,128,128]{2,1,0:T(8,128)(2,1)} %get-tuple-element.75), calls=%async_computation | async-start | bytes 1048576 | tf_op jit(solution)/shard_map/all_to_all | solution.py:707
  50.7 47.2 %all-gather.7.cloned.1.call-done = bf16[2048,1152]{1,0:T(8,128)(2,1)} async-done(((bf16[128,1152]{1,0:T(8,128)(2,1)}), bf16[2048,1152]{1,0:T(8,128)(2,1)}) %all-gather.7.cloned.1.call-update) | async-done | bytes 4718608 | tf_op jit(solution)/shard_map/all_gather | solution.py:774
  105.6 6.3 %collective-permute-done.1.left_ref = bf16[2048,128]{1,0:T(8,128)(2,1)S(1)} collective-permute-done((bf16[2048,128]{1,0:T(8,128)(2,1)S(1)}, bf16[2048,128]{1,0:T(8,128)(2,1)S(1)}, u32[]{:S(2)}, u32[]{:S(2)}) %collective-permute-start.1) | collective-permute-done | bytes 524320 | tf_op jit(solution)/shard_map/ppermute | solution.py:719
  115.5 16.6 %collective-permute-done.q_far_ref = bf16[8,64,128]{2,1,0:T(8,128)(2,1)S(1)} collective-permute-done((bf16[8,64,128]{2,1,0:T(8,128)(2,1)S(1)}, bf16[8,64,128]{2,1,0:T(8,128)(2,1)S(1)}, u32[]{:S(2)}, u32[]{:S(2)}) %collective-permute-start) | collective-permute-done | bytes 131104 | tf_op jit(solution)/shard_map/ppermute | solution.py:711
  138.5 26.8 %attend.1 = (f32[2,512,128]{2,1,0:T(8,128)}, bf16[8,64,128]{2,1,0:T(8,128)(2,1)}, bf16[8,64,128]{2,1,0:T(8,128)(2,1)}, f32[4,8,512]{2,1,0:T(8,128)}, bf16[8192,128]{1,0:T(8,128)(2,1)}) custom-call(s32[3]{0:T(128)} %pad_add_fusion.place_ref, bf16[16,64,128]{2,1,0:T(8,128)(2,1)} %copy-done.8, bf16[8,64,128]{2,1,0:T(8,128)(2,1)} %copy-done.25, ...), custom_call_target="tpu_custom_call" | custom-call | flops 20000000000 | bytes 4000000 | tf_op jit(solution)/shard_map/attend/pallas_call | solution.py:182
  171.7 6.6 %all-to-all-start.3 = ((bf16[16,64,128]{2,1,0:T(8,128)(2,1)}), bf16[16,64,128]{2,1,0:T(8,128)(2,1)S(1)}, u32[]{:S(2)}, u32[]{:S(2)}) async-start(bf16[16,64,128]{2,1,0:T(8,128)(2,1)} %constant_dynamic-update-slice_fusion), calls=%async_computation.3 | async-start | bytes 524288 | tf_op jit(solution)/shard_map/all_to_all | solution.py:707
  180.1 11.0 %raw.1 = (bf16[2,768,1024]{2,1,0:T(8,128)(2,1)}, f32[2,768,512]{2,1,0:T(8,128)}) custom-call(s32[1]{0:T(128)} %bitcast.7.first_ref, bf16[16,128,1152]{2,1,0:T(8,128)(2,1)} %bitcast.51, bf16[2,512,1024]{2,1,0:T(8,128)(2,1)} %all-gather.5.cloned.1.call-done.down_ref), custom_call_target="tpu_custom_call" | custom-call | flops 1610612736 | bytes 12000000 | tf_op jit(solution)/shard_map/raw/pallas_call | solution.py:319
  196.8 6.8 %all-to-all-start.4 = ((bf16[16,2,48,1024]{3,2,1,0:T(8,128)(2,1)}), bf16[16,2,48,1024]{3,2,1,0:T(8,128)(2,1)S(1)}, u32[]{:S(2)}, u32[]{:S(2)}) async-start(bf16[16,2,48,1024]{3,2,1,0:T(8,128)(2,1)} %bitcast.54), calls=%async_computation.4 | async-start | bytes 6291456 | tf_op jit(solution)/shard_map/all_to_all | solution.py:707
  204.5 34.1 %all-to-all-done.4.x_ref = bf16[16,2,48,1024]{3,2,1,0:T(8,128)(2,1)S(1)} async-done(((bf16[16,2,48,1024]{3,2,1,0:T(8,128)(2,1)}), bf16[16,2,48,1024]{3,2,1,0:T(8,128)(2,1)S(1)}, u32[]{:S(2)}, u32[]{:S(2)}) %all-to-all-start.4) | async-done | bytes 3145760 | tf_op jit(solution)/shard_map/all_to_all | solution.py:707
  240.2 16.0 %experts.1 = (bf16[16,2,48,1024]{3,2,1,0:T(8,128)(2,1)}, bf16[2,768,512]{2,1,0:T(8,128)(2,1)}, bf16[2,768,1024]{2,1,0:T(8,128)(2,1)}, f32[2,768,1]{2,1,0:T(8,128...) custom-call(s32[1]{0:T(128)} %bitcast.7.first_ref, bf16[16,2,48,1024]{3,2,1,0:T(8,128)(2,1)} %copy-done.3, ...), custom_call_target="tpu_custom_call" | custom-call | flops 8053063680 | bytes 20000000 | tf_op jit(solution)/shard_map/experts/pallas_call | solution.py:383
  256.2 7.4 %all-to-all-start.5 = ((bf16[16,2,48,1024]{3,2,1,0:T(8,128)(2,1)}), bf16[16,2,48,1024]{3,2,1,0:T(8,128)(2,1)S(1)}, u32[]{:S(2)}, u32[]{:S(2)}) async-start(bf16[16,2,48,1024]{3,2,1,0:T(8,128)(2,1)} %get-tuple-element.86), calls=%async_computation.5 | async-start | bytes 6291456 | tf_op jit(solution)/shard_map/all_to_all | solution.py:707
  263.7 13.5 %expert_grads.1 = (bf16[16,2,48,1024]{3,2,1,0:T(8,128)(2,1)}, bf16[2,1024,1024]{2,1,0:T(8,128)(2,1)}, bf16[2,512,1024]{2,1,0:T(8,128)(2,1)}, f32[2,32,1024]{2,1,0:T(8,128)}) custom-call(bf16[16,2,48,1024]{3,2,1,0:T(8,128)(2,1)} %copy-done.3, bf16[2,768,1024]{2,1,0:T(8,128)(2,1)} %get-tuple-element.87.top_ref, f32[2,768,1]{2,1,0:T(8,128)} %get-tuple-element.88.gate_ref, ...), custom_call_target="tpu_custom_call" | custom-call | flops 6442450944 | bytes 24000000 | tf_op jit(solution)/shard_map/expert_grads/pallas_call | solution.py:424
  277.1 19.8 %all-to-all-done.5 = bf16[16,2,48,1024]{3,2,1,0:T(8,128)(2,1)S(1)} async-done(((bf16[16,2,48,1024]{3,2,1,0:T(8,128)(2,1)}), bf16[16,2,48,1024]{3,2,1,0:T(8,128)(2,1)S(1)}, u32[]{:S(2)}, u32[]{:S(2)}) %all-to-all-start.5) | async-done | bytes 3145760 | tf_op jit(solution)/shard_map/all_to_all | solution.py:707
  305.6 10.4 %all-to-all-start.6 = ((bf16[16,64,128]{2,1,0:T(8,128)(2,1)}), bf16[16,64,128]{2,1,0:T(8,128)(2,1)S(1)}, u32[]{:S(2)}, u32[]{:S(2)}) async-start(bf16[16,64,128]{2,1,0:T(8,128)(2,1)} %get-tuple-element.96), calls=%async_computation.6 | async-start | bytes 524288 | tf_op jit(solution)/shard_map/all_to_all | solution.py:707
  316.2 7.1 %all-to-all-done.6.do_ref = bf16[16,64,128]{2,1,0:T(8,128)(2,1)S(1)} async-done(((bf16[16,64,128]{2,1,0:T(8,128)(2,1)}), bf16[16,64,128]{2,1,0:T(8,128)(2,1)S(1)}, u32[]{:S(2)}, u32[]{:S(2)}) %all-to-all-start.6) | async-done | bytes 262176 | tf_op jit(solution)/shard_map/all_to_all | solution.py:707
  335.1 63.5 %all-gather.11.cloned.1.call-done = bf16[2048,1024]{1,0:T(8,128)(2,1)} async-done(((bf16[128,1024]{1,0:T(8,128)(2,1)}), bf16[2048,1024]{1,0:T(8,128)(2,1)}) %all-gather.11.cloned.1.call-update) | async-done | bytes 4194320 | tf_op jit(solution)/shard_map/all_gather | solution.py:801
  399.3 31.8 %attend_back.1 = (bf16[8,64,128]{2,1,0:T(8,128)(2,1)}, bf16[8,64,128]{2,1,0:T(8,128)(2,1)}, f32[2048,128]{1,0:T(8,128)}, bf16[1024,128]{1,0:T(8,128)(2,1)}, bf16...) custom-call(s32[3]{0:T(128)} %pad_add_fusion.place_ref, ...), custom_call_target="tpu_custom_call" | custom-call | flops 49999998976 | bytes 8000000 | tf_op jit(solution)/shard_map/attend_back/pallas_call | solution.py:266
  481.7 6.3 %collective-permute-done.16 = bf16[384,256]{1,0:T(8,128)(2,1)S(1)} collective-permute-done((bf16[384,256]{1,0:T(8,128)(2,1)}, bf16[384,256]{1,0:T(8,128)(2,1)S(1)}, u32[]{:S(2)}, u32[]{:S(2)}) %collective-permute-start.16) | collective-permute-done | bytes 196640 | tf_op jit(solution)/shard_map/ppermute | solution.py:727
  489.2 6.2 %all-to-all-start.8 = ((bf16[16,64,256]{2,1,0:T(8,128)(2,1)}), bf16[16,64,256]{2,1,0:T(8,128)(2,1)S(1)}, u32[]{:S(2)}, u32[]{:S(2)}) async-start(bf16[16,64,256]{2,1,0:T(8,128)(2,1)} %bitcast.21), calls=%async_computation.8 | async-start | bytes 1048576 | tf_op jit(solution)/shard_map/all_to_all | solution.py:707
  506.3 6.6 %all-to-all-start.9 = ((bf16[16,400,256]{2,1,0:T(8,128)(2,1)}), bf16[16,400,256]{2,1,0:T(8,128)(2,1)S(1)}, u32[]{:S(2)}, u32[]{:S(2)}) async-start(bf16[16,400,256]{2,1,0:T(8,128)(2,1)} %spread.1), calls=%async_computation.9 | async-start | bytes 6553600 | tf_op jit(solution)/shard_map/all_to_all | solution.py:707
  523.8 25.8 %all-to-all-done.9 = bf16[16,400,256]{2,1,0:T(8,128)(2,1)S(1)} async-done(((bf16[16,400,256]{2,1,0:T(8,128)(2,1)}), bf16[16,400,256]{2,1,0:T(8,128)(2,1)S(1)}, u32[]{:S(2)}, u32[]{:S(2)}) %all-to-all-start.9) | async-done | bytes 3276832 | tf_op jit(solution)/shard_map/all_to_all | solution.py:707
  549.7 7.6 %collective-permute-start.19 = (bf16[16,400,256]{2,1,0:T(8,128)(2,1)S(1)}, bf16[16,400,256]{2,1,0:T(8,128)(2,1)}, u32[]{:S(2)}, u32[]{:S(2)}) collective-permute-start(bf16[16,400,256]{2,1,0:T(8,128)(2,1)S(1)} %all-to-all-done.9), channel_id=1, source_target_pairs={{0,1},{1,0},{2,3},{3,2},{4,5},{5,4},{6,7},{7,6},{8,9},{9,8},{10,11... | collective-permute-start | bytes 9830408 | tf_op jit(solution)/shard_map/ppermute | solution.py:715
  562.9 10.9 %assemble.1 = (f32[1024,1024]{1,0:T(8,128)}, f32[1024,512]{1,0:T(8,128)}, f32[1024,512]{1,0:T(8,128)}, f32[1024,1024]{1,0:T(8,128)}, f32[1,1024]{1,0:T(1,128)}) custom-call(s32[3]{0:T(128)} %pad_add_fusion.place_ref, bf16[8,2,400,256]{3,2,1,0:T(8,128)(2,1)} %bitcast.47, bf16[8,2,400,256]{3,2,1,0:T(8,128)(2,1)} %bitcast.26.other_ref, ...), custom_call_target="tpu_custom_call" | custom-call | flops 1000000 | bytes 22000000 | tf_op jit(solution)/shard_map/assemble/pallas_call | solution.py:664
  (172 shorter events, 145.6 us)
Async XLA Ops:
  7.2 31.4 %all-gather.5.cloned.1.call-start = ((), (), s32[]{:S(2)}) async-start(), calls=%async_computation.12 | async-start | bytes 2359296 | tf_op jit(solution)/shard_map/all_gather | solution.py:772
  7.9 90.0 %all-gather.7.cloned.1.call-start = ((), (), s32[]{:S(2)}) async-start(), calls=%async_computation.13 | async-start | bytes 5013504 | tf_op jit(solution)/shard_map/all_gather | solution.py:774
  44.0 53.9 %all-to-all-start = ((bf16[16,128,128]{2,1,0:T(8,128)(2,1)}), bf16[16,128,128]{2,1,0:T(8,128)(2,1)S(1)}, u32[]{:S(2)}, u32[]{:S(2)}) async-start(bf16[16,128,128]{2,1,0:T(8,128)(2,1)} %get-tuple-element.75), calls=%async_computation | async-start | bytes 1048576 | tf_op jit(solution)/shard_map/all_to_all | solution.py:707
  50.6 187.9 %all-gather.9.cloned.1.call-start = ((), (), s32[]{:S(2)}) async-start(), calls=%async_computation.14 | async-start | bytes 4718592 | tf_op jit(solution)/shard_map/all_gather | solution.py:775
  97.9 14.1 %collective-permute-start.1 = (bf16[2048,128]{1,0:T(8,128)(2,1)S(1)}, bf16[2048,128]{1,0:T(8,128)(2,1)S(1)}, u32[]{:S(2)}, u32[]{:S(2)}) collective-permute-start(bf16[2048,128]{1,0:T(8,128)(2,1)S(1)} %bitcast.64), channel_id=1, source_target_pairs={{0,2},{2,4},{4,6},{6,0},{1,3},{3,5},{5,7},{7,1},{8,10},{10,12},{12... | collective-permute-start | bytes 1572872 | tf_op jit(solution)/shard_map/ppermute | solution.py:719
  100.7 14.8 %all-to-all-start.1 = ((bf16[16,64,128]{2,1,0:T(8,128)(2,1)}), bf16[16,64,128]{2,1,0:T(8,128)(2,1)S(1)}, u32[]{:S(2)}, u32[]{:S(2)}) async-start(bf16[16,64,128]{2,1,0:T(8,128)(2,1)} %get-tuple-element.76), calls=%async_computation.1 | async-start | bytes 524288 | tf_op jit(solution)/shard_map/all_to_all | solution.py:707
  112.0 20.2 %collective-permute-start.2 = (bf16[1024,128]{1,0:T(8,128)(2,1)S(1)}, bf16[1024,128]{1,0:T(8,128)(2,1)S(1)}, u32[]{:S(2)}, u32[]{:S(2)}) collective-permute-start(bf16[1024,128]{1,0:T(8,128)(2,1)S(1)} %slice.53), channel_id=1, source_target_pairs={{0,2},{2,4},{4,6},{6,0},{1,3},{3,5},{5,7},{7,1},{8,10},{10,12},{12... | collective-permute-start | bytes 786440 | tf_op jit(solution)/shard_map/ppermute | solution.py:719
  112.1 20.0 %collective-permute-start.4 = (bf16[1024,128]{1,0:T(8,128)(2,1)S(1)}, bf16[1024,128]{1,0:T(8,128)(2,1)S(1)}, u32[]{:S(2)}, u32[]{:S(2)}) collective-permute-start(bf16[1024,128]{1,0:T(8,128)(2,1)S(1)} %slice.54), channel_id=1, source_target_pairs={{0,6},{2,0},{4,2},{6,4},{1,7},{3,1},{5,3},{7,5},{8,14},{10,8},{12,... | collective-permute-start | bytes 786440 | tf_op jit(solution)/shard_map/ppermute | solution.py:719
  115.4 16.7 %collective-permute-start = (bf16[8,64,128]{2,1,0:T(8,128)(2,1)S(1)}, bf16[8,64,128]{2,1,0:T(8,128)(2,1)S(1)}, u32[]{:S(2)}, u32[]{:S(2)}) collective-permute-start(bf16[8,64,128]{2,1,0:T(8,128)(2,1)S(1)} %slice.52), channel_id=1, source_target_pairs={{0,6},{2,4},{4,2},{6,0},{1,7},{3,5},{5,3},{7,1},{8,14},{10,12},{12... | collective-permute-start | bytes 393224 | tf_op jit(solution)/shard_map/ppermute | solution.py:711
  133.0 32.3 %all-to-all-start.2 = ((bf16[16,64,1024]{2,1,0:T(8,128)(2,1)}), bf16[16,64,1024]{2,1,0:T(8,128)(2,1)S(1)}, u32[]{:S(2)}, u32[]{:S(2)}) async-start(bf16[16,64,1024]{2,1,0:T(8,128)(2,1)} %get-tuple-element.77), calls=%async_computation.2 | async-start | bytes 4194304 | tf_op jit(solution)/shard_map/all_to_all | solution.py:707
  171.7 19.5 %all-to-all-start.3 = ((bf16[16,64,128]{2,1,0:T(8,128)(2,1)}), bf16[16,64,128]{2,1,0:T(8,128)(2,1)S(1)}, u32[]{:S(2)}, u32[]{:S(2)}) async-start(bf16[16,64,128]{2,1,0:T(8,128)(2,1)} %constant_dynamic-update-slice_fusion), calls=%async_computation.3 | async-start | bytes 524288 | tf_op jit(solution)/shard_map/all_to_all | solution.py:707
  196.8 41.8 %all-to-all-start.4 = ((bf16[16,2,48,1024]{3,2,1,0:T(8,128)(2,1)}), bf16[16,2,48,1024]{3,2,1,0:T(8,128)(2,1)S(1)}, u32[]{:S(2)}, u32[]{:S(2)}) async-start(bf16[16,2,48,1024]{3,2,1,0:T(8,128)(2,1)} %bitcast.54), calls=%async_computation.4 | async-start | bytes 6291456 | tf_op jit(solution)/shard_map/all_to_all | solution.py:707
  256.2 40.7 %all-to-all-start.5 = ((bf16[16,2,48,1024]{3,2,1,0:T(8,128)(2,1)}), bf16[16,2,48,1024]{3,2,1,0:T(8,128)(2,1)S(1)}, u32[]{:S(2)}, u32[]{:S(2)}) async-start(bf16[16,2,48,1024]{3,2,1,0:T(8,128)(2,1)} %get-tuple-element.86), calls=%async_computation.5 | async-start | bytes 6291456 | tf_op jit(solution)/shard_map/all_to_all | solution.py:707
  263.6 135.0 %all-gather.11.cloned.1.call-start = ((), (), s32[]{:S(2)}) async-start(), calls=%async_computation.15 | async-start | bytes 4456448 | tf_op jit(solution)/shard_map/all_gather | solution.py:801
  305.6 17.8 %all-to-all-start.6 = ((bf16[16,64,128]{2,1,0:T(8,128)(2,1)}), bf16[16,64,128]{2,1,0:T(8,128)(2,1)S(1)}, u32[]{:S(2)}, u32[]{:S(2)}) async-start(bf16[16,64,128]{2,1,0:T(8,128)(2,1)} %get-tuple-element.96), calls=%async_computation.6 | async-start | bytes 524288 | tf_op jit(solution)/shard_map/all_to_all | solution.py:707
  323.3 75.3 %collective-permute-start.6 = (bf16[8,64,128]{2,1,0:T(8,128)(2,1)S(1)}, bf16[8,64,128]{2,1,0:T(8,128)(2,1)S(1)}, u32[]{:S(2)}, u32[]{:S(2)}) collective-permute-start(bf16[8,64,128]{2,1,0:T(8,128)(2,1)S(1)} %slice.55), channel_id=1, source_target_pairs={{0,6},{2,4},{4,2},{6,0},{1,7},{3,5},{5,3},{7,1},{8,14},{10,12},{12... | collective-permute-start | bytes 393224 | tf_op jit(solution)/shard_map/ppermute | solution.py:711
  330.5 114.8 %all-to-all-start.7 = ((bf16[16,112,1024]{2,1,0:T(8,128)(2,1)}), bf16[16,112,1024]{2,1,0:T(8,128)(2,1)}, u32[]{:S(2)}, u32[]{:S(2)}) async-start(bf16[16,112,1024]{2,1,0:T(8,128)(2,1)} %fusion.1), calls=%async_computation.7 | async-start | bytes 7340032 | tf_op jit(solution)/shard_map/all_to_all | solution.py:707
  335.0 177.9 %reduce-scatter.3.cloned.1.call-start = ((), (), s32[]{:S(2)}) async-start(), calls=%async_computation.16 | async-start | bytes 4718592 | tf_op jit(solution)/shard_map/reduce_scatter | solution.py:807
  432.6 15.1 %collective-permute-start.11 = (bf16[1024,128]{1,0:T(8,128)(2,1)}, bf16[1024,128]{1,0:T(8,128)(2,1)S(1)}, u32[]{:S(2)}, u32[]{:S(2)}) collective-permute-start(bf16[1024,128]{1,0:T(8,128)(2,1)} %get-tuple-element.112), channel_id=1, source_target_pairs={{0,2},{2,4},{4,6},{6,0},{1,3},{3,5},{5,7},{7,1},{8,10},{10,12},{12... | collective-permute-start | bytes 786440 | tf_op jit(solution)/shard_map/ppermute | solution.py:719
  432.6 15.1 %collective-permute-start.12 = (bf16[1024,128]{1,0:T(8,128)(2,1)}, bf16[1024,128]{1,0:T(8,128)(2,1)S(1)}, u32[]{:S(2)}, u32[]{:S(2)}) collective-permute-start(bf16[1024,128]{1,0:T(8,128)(2,1)} %get-tuple-element.113), channel_id=1, source_target_pairs={{0,6},{2,0},{4,2},{6,4},{1,7},{3,1},{5,3},{7,5},{8,14},{10,8},{12,... | collective-permute-start | bytes 786440 | tf_op jit(solution)/shard_map/ppermute | solution.py:719
  489.2 16.3 %all-to-all-start.8 = ((bf16[16,64,256]{2,1,0:T(8,128)(2,1)}), bf16[16,64,256]{2,1,0:T(8,128)(2,1)S(1)}, u32[]{:S(2)}, u32[]{:S(2)}) async-start(bf16[16,64,256]{2,1,0:T(8,128)(2,1)} %bitcast.21), calls=%async_computation.8 | async-start | bytes 1048576 | tf_op jit(solution)/shard_map/all_to_all | solution.py:707
  506.3 43.4 %all-to-all-start.9 = ((bf16[16,400,256]{2,1,0:T(8,128)(2,1)}), bf16[16,400,256]{2,1,0:T(8,128)(2,1)S(1)}, u32[]{:S(2)}, u32[]{:S(2)}) async-start(bf16[16,400,256]{2,1,0:T(8,128)(2,1)} %spread.1), calls=%async_computation.9 | async-start | bytes 6553600 | tf_op jit(solution)/shard_map/all_to_all | solution.py:707
  512.8 61.1 %reduce-scatter.5.cloned.1.call-start = ((), (), s32[]{:S(2)}) async-start(), calls=%async_computation.17 | async-start | bytes 2359296 | tf_op jit(solution)/shard_map/reduce_scatter | solution.py:839
  549.7 13.3 %collective-permute-start.19 = (bf16[16,400,256]{2,1,0:T(8,128)(2,1)S(1)}, bf16[16,400,256]{2,1,0:T(8,128)(2,1)}, u32[]{:S(2)}, u32[]{:S(2)}) collective-permute-start(bf16[16,400,256]{2,1,0:T(8,128)(2,1)S(1)} %all-to-all-done.9), channel_id=1, source_target_pairs={{0,1},{1,0},{2,3},{3,2},{4,5},{5,4},{6,7},{7,6},{8,9},{9,8},{10,11... | collective-permute-start | bytes 9830408 | tf_op jit(solution)/shard_map/ppermute | solution.py:715
  (40 other events, 334.5 us)
Sparse Core Ops, SparseCore 0:
  9.7 28.8 all-gather.4
  41.3 56.5 all-gather.6
  99.6 40.6 all-gather.8
  303.8 94.7 all-gather.10
  401.4 33.5 reduce-scatter.2
  515.8 33.5 reduce-scatter.4
